TPU v7x, 32 devices: a whole 2x2x4 slice. The times are simulated.
32 devices in a mesh: section: 4 (over y, x), seqtp: 8 (over z, core).
Axes of the slice: x: 2, y: 2, z: 4, core: 2. Of those that a mesh axis runs over, the one named last changes fastest.
Arguments:
- saved_in: bfloat16 [4, 4, 16, 4096], P('section', None, 'seqtp'), may hold values from -40 to 40
- grad_in: bfloat16 [4, 16, 4096], P('section', 'seqtp'), may hold values from -6 to 6
- slot_table: int32 [4], P('section'), may hold values from 0 to 3
- gain: bfloat16 [4, 4096], P('section'), may hold values from 0.099609375 to 1.8984375
- w_gate: bfloat16 [4096, 3072], P(None, 'seqtp'), may hold values from -0.09375 to 0.09375
- w_up: bfloat16 [4096, 3072], P(None, 'seqtp'), may hold values from -0.09375 to 0.09375
- w_down: bfloat16 [3072, 4096], P('seqtp'), may hold values from -0.109375 to 0.109375
Outputs:
- grad_prev: bfloat16 [4, 16, 4096], P('section', 'seqtp')
All inputs are finite; a program needn't handle non-finite values.
Results may differ from a plain program's by a relative error of at most 0.0052.
Values may be sent and summed in bfloat16 or wider, within the bound.
No kernel may reach another device: no remote copies, remote signals or barrier semaphores. Data moves between devices by JAX's collectives and lax.ppermute only.
A program may use at most 64 MiB of HBM per device.

v0:
```python
import jax
import jax.numpy as jnp
from jax import lax
from jax.sharding import PartitionSpec as P

EPS = 1e-05


def passed_along(x, axis, by):
    length = lax.axis_size(axis)
    return lax.ppermute(x, axis, [(i, (i + by) % length) for i in range(length)])


def rms_norm(values, gain_vec):
    wide = values.astype(jnp.float32)
    recip = lax.rsqrt(jnp.mean(wide * wide, axis=-1, keepdims=True) + EPS)
    return ((wide * recip * gain_vec).astype(jnp.bfloat16), recip)


def transposed(left, weight):
    return lax.dot_general(
        left, weight, (((1,), (1,)), ((), ())), preferred_element_type=jnp.float32
    )


def on_device(saved_in, grad_in, slot_table, gain, w_gate, w_up, w_down):
    cotangent = grad_in[0]
    gain_vec = gain[0].astype(jnp.float32)
    behind = lax.dynamic_index_in_dim(saved_in[0], slot_table[0], 0, keepdims=False)
    normed_b, recip_b = rms_norm(behind, gain_vec)
    width = w_gate.shape[1]
    paired = jnp.stack([normed_b, cotangent])
    piece = lax.all_gather(paired, "seqtp", axis=1, tiled=True)
    gate_b = jnp.dot(piece[0], w_gate, preferred_element_type=jnp.float32)
    up_b = jnp.dot(piece[0], w_up, preferred_element_type=jnp.float32)
    d_hidden = transposed(piece[1], w_down)
    probe = jax.nn.sigmoid(gate_b)
    d_gate = (d_hidden * up_b * probe * (1.0 + gate_b * (1.0 - probe))).astype(jnp.bfloat16)
    d_up = (d_hidden * gate_b * probe).astype(jnp.bfloat16)
    d_both = jnp.concatenate([d_gate, d_up], axis=1)
    grad_sum = lax.psum_scatter(
        transposed(d_both[:, :width], w_gate) + transposed(d_both[:, width:], w_up),
        "seqtp",
        scatter_dimension=0,
        tiled=True,
    )
    scaled = gain_vec * grad_sum
    unit = behind.astype(jnp.float32) * recip_b
    grad_x = cotangent.astype(jnp.float32) + recip_b * (
        scaled - unit * jnp.mean(scaled * unit, axis=-1, keepdims=True)
    )
    grad_x = grad_x.astype(jnp.bfloat16)
    grad_prev = passed_along(grad_x, "section", -1)
    return grad_prev[None]


def solution(mesh):
    return jax.shard_map(
        on_device,
        mesh=mesh,
        in_specs=(
            P("section", None, "seqtp", None),
            P("section", "seqtp", None),
            P("section"),
            P("section", None),
            P(None, "seqtp"),
            P(None, "seqtp"),
            P("seqtp", None),
        ),
        out_specs=P("section", "seqtp", None),
        check_vma=False,
    )
```

profile of v0, /device:TPU:0, one launch (start us, length us, event | category | flops | bytes accessed | tf_op | source)
XLA Modules:
  0.0 105.4 jit_solution(14713561289250649122)
XLA Ops:
  6.5 0.0 copy-start
  6.5 0.0 all-reduce.3.cloned.1.call-start
  7.3 0.0 copy-start.1
  7.4 0.9 constant_dynamic-slice_fusion
  8.3 0.1 fusion.6
  8.4 0.7 mul.110
  9.2 0.7 copy.11
  9.9 0.1 fusion.9
  10.1 0.1 pad_maximum_fusion
  10.1 15.9 %all_gather.3 = bf16[2,16,4096]{2,0,1:T(2,128)(2,1)S(1)} all-gather(bf16[2,2,4096]{2,0,1:T(2,128)(2,1)S(1)} %pad_maximum_fusion), channel_id=1, replica_groups=mesh['section'=4,'seqtp'=8] {'seqtp'}, dimensions={1}, use_global_device_ids=true | all-gather | bytes 294912 | tf_op jit(solution)/shard_map/all_gather | solution.py:33
  26.0 0.4 fusion.17
  26.4 0.0 copy-start.2
  26.4 0.7 copy-done.2
  27.1 2.4 %fusion.5 = f32[16,384]{1,0:T(8,128)S(1)} fusion(bf16[4096,384]{1,0:T(8,128)(2,1)} %param.11, bf16[1,16,4096]{2,0,1:T(2,128)(2,1)S(1)} %get-tuple-element.5), kind=kOutput, calls=%fused_computation.9 | convolution fusion | flops 50331648 | bytes 3301376 | tf_op jit(solution)/shard_map/dot_general | solution.py:34
  29.5 0.0 copy-done.1
  29.5 0.9 fusion.4
  30.5 0.0 copy-done
  30.5 3.6 %fusion.3 = f32[16,4096]{1,0:T(8,128)S(1)} fusion(bf16[4096,384]{1,0:T(8,128)(2,1)} %param.11, f32[16,384]{1,0:T(8,128)S(1)} %fusion.4, bf16[4096,384]{1,0:T(8,128)(2,1)S(1)} %copy-done, bf16[1,16,4096]{2,0,1:T(2,128)(2,1)} %copy-done.2, f32[16,384]{1,0:T(8,128)S(1)} %fusion.5), kind=kOutput, calls=%fused_computation.5 | convolution fusion | flops 100724736 | bytes 6733824 | tf_op jit(solution)/shard_map/dot_general | solution.py:21
  34.1 0.0 copy-start.4
  34.1 0.0 copy-start.3
  34.1 1.7 %convolution_add_fusion = f32[16,4096]{1,0:T(8,128)} fusion(f32[16,4096]{1,0:T(8,128)S(1)} %fusion.3, bf16[4096,384]{1,0:T(8,128)(2,1)S(1)} %copy-done, f32[16,384]{1,0:T(8,128)S(1)} %fusion.4, f32[16,384]{1,0:T(8,128)S(1)} %fusion.5), kind=kOutput, calls=%fused_computation | convolution fusion | flops 50434048 | bytes 3719168 | tf_op jit(solution)/shard_map/dot_general | solution.py:21
  35.7 0.0 all-reduce.3.cloned.1.call-update
  35.7 0.0 copy-done.4
  35.7 0.6 dynamic-slice.1
  37.0 54.9 %all-reduce.3.cloned.1.call-done = f32[16,4096]{1,0:T(8,128)} async-done(((f32[16,4096]{1,0:T(8,128)}), f32[16,4096]{1,0:T(8,128)}) %all-reduce.3.cloned.1.call-update) | async-done | bytes 262160
  91.9 1.1 %multiply_reduce_fusion = f32[2]{0:T(128)S(1)} fusion(f32[1,1,2,4096]{3,0,2,1:T(1,128)S(1)} %copy_convert_fusion, f32[16,4096]{1,0:T(8,128)} %all-reduce.3.cloned.1.call-done, u32[]{:T(128)S(6)} %multiply.13, f32[2]{0:T(128)S(1)} %add_rsqrt_fusion, f32[4096]{0:T(1024)S(1)} %bitcast.39), kind=kLoop, calls=%fused_computation.21 | loop fusion | flops 32766 | bytes 81940 | tf_op jit(solution)/shard_map/reduce_sum | solution.py:50
  93.0 0.0 copy-done.3
  93.0 1.0 fusion.7
  94.0 2.4 %collective-permute-start = (bf16[2,4096]{1,0:T(2,128)(2,1)S(1)}, bf16[2,4096]{1,0:T(2,128)(2,1)S(1)}, u32[]{:S(2)}, u32[]{:S(2)}) collective-permute-start(bf16[2,4096]{1,0:T(2,128)(2,1)S(1)} %fusion.7), channel_id=1, source_target_pairs={{0,24},{8,0},{16,8},{24,16},{1,25},{9,1},{17,9},{25,17},{2,26},{10... | collective-permute-start | bytes 49160 | tf_op jit(solution)/shard_map/ppermute | solution.py:11
  96.5 1.4 %collective-permute-done = bf16[2,4096]{1,0:T(2,128)(2,1)S(1)} collective-permute-done((bf16[2,4096]{1,0:T(2,128)(2,1)S(1)}, bf16[2,4096]{1,0:T(2,128)(2,1)S(1)}, u32[]{:S(2)}, u32[]{:S(2)}) %collective-permute-start) | collective-permute-done | bytes 16416 | tf_op jit(solution)/shard_map/ppermute | solution.py:11
  97.9 0.6 copy.33
  (3 shorter events, 0.0 us)
Async XLA Ops:
  6.5 23.9 %copy-start = (bf16[4096,384]{1,0:T(8,128)(2,1)S(1)}, bf16[4096,384]{1,0:T(8,128)(2,1)}, u32[]{:S(2)}) copy-start(bf16[4096,384]{1,0:T(8,128)(2,1)} %param.12) | copy-start | bytes 9437188
  6.5 85.4 %all-reduce.3.cloned.1.call-start = ((), (), s32[]{:S(2)}) async-start(), calls=%async_computation | async-start | bytes 524288
  7.3 22.2 %copy-start.1 = (bf16[384,4096]{1,0:T(8,128)(2,1)S(1)}, bf16[384,4096]{1,0:T(8,128)(2,1)}, u32[]{:S(2)}) copy-start(bf16[384,4096]{1,0:T(8,128)(2,1)} %param.13) | copy-start | bytes 9437188
  26.4 0.7 copy-start.2
  34.1 1.7 %copy-start.4 = (u32[32]{0:T(128)S(1)}, u32[32]{0:T(128)}, u32[]{:S(2)}) copy-start(u32[32]{0:T(128)} %constant.23) | copy-start | bytes 388
  34.1 59.0 %copy-start.3 = (bf16[1,2,4096]{2,1,0:T(2,128)(2,1)S(1)}, bf16[1,2,4096]{2,1,0:T(2,128)(2,1)}, u32[]{:S(2)}) copy-start(bf16[1,2,4096]{2,1,0:T(2,128)(2,1)} %param.8) | copy-start | bytes 49156
  94.0 3.9 %collective-permute-start = (bf16[2,4096]{1,0:T(2,128)(2,1)S(1)}, bf16[2,4096]{1,0:T(2,128)(2,1)S(1)}, u32[]{:S(2)}, u32[]{:S(2)}) collective-permute-start(bf16[2,4096]{1,0:T(2,128)(2,1)S(1)} %fusion.7), channel_id=1, source_target_pairs={{0,24},{8,0},{16,8},{24,16},{1,25},{9,1},{17,9},{25,17},{2,26},{10... | collective-permute-start | bytes 49160 | tf_op jit(solution)/shard_map/ppermute | solution.py:11
Sparse Core Ops, SparseCore 0:
  35.9 55.9 all-reduce.2
where the time goes:
time: 106 us; the launch traced here: 105 us
  waiting for transfers between devices  56.4 us (53%)
  blocking collectives  15.9 us (15%)
  between operations  14.9 us (14%)
  matrix products  8.61 us (8%)
  local copies, waits for them, and re-layouts  3.89 us (4%)
  other arithmetic  3.25 us (3%)
  starting transfers between devices  2.43 us (2%)
    unnamed x2, waiting for transfers between devices  54.9 us
    all_gather x1, blocking collectives, on_device(): piece = lax.all_gather(paired, 'seqtp', axis=1, tiled=True)  15.9 us
    dot_general x3, matrix products, transposed(): lax.dot_general(left, weight, (((1,), (1,)), ((), ())), preferred_element...  6.16 us
    unnamed x13, local copies, waits for them, and re-layouts  2.63 us
    dot_general x1, matrix products, on_device(): gate_b = jnp.dot(piece[0], w_gate, preferred_element_type=jnp.float32)  2.45 us
    ppermute x1, starting transfers between devices, passed_along(): lax.ppermute(x, axis, [(i, (i + by) % length) for i in range(length)])  2.43 us
  transfers between devices with their start and end apart: 2, of which 2 were waited for; matrix products, arithmetic and copies ran while one was open for 1% of the time, Pallas kernels for 0%

commit v1 on v0

v1 whole, which is shorter than its diff:
```python
import functools

import jax
import jax.numpy as jnp
from jax import lax
from jax.experimental import pallas as pl
from jax.experimental.pallas import tpu as pltpu
from jax.sharding import PartitionSpec as P

EPS = 1e-05
CORES = 2


def whole(n):
    return [pl.BlockSpec(memory_space=pltpu.VMEM)] * n


def params(mib):
    return pltpu.CompilerParams(vmem_limit_bytes=mib * 2**20)


def prepare(slot_ref, saved_ref, grad_ref, gain_ref, sent_ref, own_ref):
    d = grad_ref.shape[-1]
    behind = saved_ref[0, slot_ref[0]]
    wide = behind.astype(jnp.float32)
    gain = gain_ref[...].astype(jnp.float32)
    recip = lax.rsqrt(jnp.mean(wide * wide, axis=-1, keepdims=True) + EPS)
    grad = grad_ref[0]
    sent_ref[:, :d] = (wide * recip * gain).astype(jnp.bfloat16)
    sent_ref[:, d:] = grad
    own_ref[:, :d] = behind
    own_ref[:, d : 2 * d] = grad
    half = d // 2
    own_ref[0:1, 2 * d :] = gain_ref[:, :half]
    own_ref[1:2, 2 * d :] = gain_ref[:, half:]


def nt(left, weight):
    return lax.dot_general(
        left, weight, (((1,), (1,)), ((), ())), preferred_element_type=jnp.float32
    )


def expert(n_near, *refs):
    near, (far_ref, gate_ref, up_ref, down_ref, mine_ref, other_ref, rows_ref) = (
        refs[:n_near],
        refs[n_near:],
    )
    d = gate_ref.shape[0]
    r = near[0].shape[0]
    for k, ref in enumerate(near):
        rows_ref[k * r : (k + 1) * r] = ref[...].astype(jnp.float32)
        rows_ref[(n_near + k) * r : (n_near + k + 1) * r] = far_ref[k].astype(jnp.float32)
    normed = rows_ref[:, :d].astype(jnp.bfloat16)
    grad = rows_ref[:, d:].astype(jnp.bfloat16)
    gate = jnp.dot(normed, gate_ref[...], preferred_element_type=jnp.float32)
    up = jnp.dot(normed, up_ref[...], preferred_element_type=jnp.float32)
    d_hidden = nt(grad, down_ref[...])
    p = jax.nn.sigmoid(gate)
    d_gate = (d_hidden * up * p * (1.0 + gate * (1.0 - p))).astype(jnp.bfloat16)
    d_up = (d_hidden * gate * p).astype(jnp.bfloat16)
    total = nt(d_gate, gate_ref[...]) + nt(d_up, up_ref[...])
    half = n_near * r
    mine_ref[...] = total[:half]
    other_ref[...] = total[half:]


def add_cores(n_near, mine_ref, got_ref, *out_refs):
    r = out_refs[0].shape[0]
    total = mine_ref[...] + got_ref[...]
    for k, ref in enumerate(out_refs):
        ref[...] = total[k * r : (k + 1) * r].astype(ref.dtype)


def finish(n_near, own_ref, *refs):
    parts, out_ref, gain_ref = refs[:n_near], refs[n_near], refs[n_near + 1]
    d = parts[0].shape[-1]
    half = d // 2
    gain_ref[:, :half] = own_ref[0:1, 2 * d :].astype(jnp.float32)
    gain_ref[:, half:] = own_ref[1:2, 2 * d :].astype(jnp.float32)
    total = sum(ref[...].astype(jnp.float32) for ref in parts)
    wide = own_ref[:, :d].astype(jnp.float32)
    grad = own_ref[:, d : 2 * d].astype(jnp.float32)
    recip = lax.rsqrt(jnp.mean(wide * wide, axis=-1, keepdims=True) + EPS)
    scaled = gain_ref[...] * total
    unit = wide * recip
    mean = jnp.mean(scaled * unit, axis=-1, keepdims=True)
    out_ref[0] = (grad + recip * (scaled - unit * mean)).astype(out_ref.dtype)


def on_device(sections, members, saved_in, grad_in, slot_table, gain, w_gate, w_up, w_down):
    chips = members // CORES
    r, d = grad_in.shape[1:]
    f32, bf16 = jnp.float32, jnp.bfloat16
    shape = jax.ShapeDtypeStruct
    far_first = [k for k in range(chips - 1, 0, -1)]

    def near(i, k):
        chip, core = divmod(i, CORES)
        return (chip ^ k if chips & (chips - 1) == 0 else (chip + k) % chips) * CORES + core

    def to_chip(x, k):
        return lax.ppermute(x, "seqtp", [(i, near(i, k)) for i in range(members)])

    def to_core(x):
        return lax.ppermute(x, "seqtp", [(i, i ^ 1) for i in range(members)])

    def home(x, k):
        pairs = [
            (s * members + near(i, k), (s - 1) % sections * members + i)
            for s in range(sections)
            for i in range(members)
        ]
        return lax.ppermute(x, ("section", "seqtp"), pairs)

    sent, own = pl.pallas_call(
        prepare,
        out_shape=[shape((r, 2 * d), bf16), shape((r, 2 * d + d // 2), bf16)],
        in_specs=[pl.BlockSpec(memory_space=pltpu.SMEM)] + whole(3),
        out_specs=whole(2),
        name="prepare",
    )(slot_table, saved_in, grad_in, gain)
    blocks = {0: sent}
    for k in far_first:
        blocks[k] = to_chip(sent, k)
    blocks = [blocks[k] for k in range(chips)]
    far = to_core(jnp.stack(blocks))
    mine, other = pl.pallas_call(
        functools.partial(expert, chips),
        out_shape=[shape((chips * r, d), f32)] * 2,
        in_specs=whole(chips + 4),
        out_specs=whole(2),
        scratch_shapes=[pltpu.VMEM((members * r, 2 * d), f32)],
        compiler_params=params(24),
        name="expert",
    )(*blocks, far, w_gate, w_up, w_down)
    got = to_core(other)
    sums = pl.pallas_call(
        functools.partial(add_cores, chips),
        out_shape=[shape((r, d), bf16)] * chips,
        in_specs=whole(2),
        out_specs=whole(chips),
        name="add_cores",
    )(mine, got)
    landed = {}
    for k in far_first + [0]:
        landed[k] = home(sums[k], k)
    own = home(own, 0)
    return pl.pallas_call(
        functools.partial(finish, chips),
        out_shape=shape((1, r, d), bf16),
        in_specs=whole(chips + 1),
        out_specs=pl.BlockSpec(memory_space=pltpu.VMEM),
        scratch_shapes=[pltpu.VMEM((1, d), f32)],
        name="finish",
    )(own, *[landed[k] for k in range(chips)])


def solution(mesh):
    return jax.shard_map(
        functools.partial(on_device, mesh.shape["section"], mesh.shape["seqtp"]),
        mesh=mesh,
        in_specs=(
            P("section", None, "seqtp", None),
            P("section", "seqtp", None),
            P("section"),
            P("section", None),
            P(None, "seqtp"),
            P(None, "seqtp"),
            P("seqtp", None),
        ),
        out_specs=P("section", "seqtp", None),
        check_vma=False,
    )
```

time: 106 us -> 44 us (0.42)
  waiting for transfers between devices: 56.4 us -> 8.82 us
  blocking collectives: 15.9 us -> 0 us
  between operations: 14.9 us -> 0.74 us
  starting transfers between devices: 2.43 us -> 15.9 us
  Pallas kernels: 0 us -> 8.69 us
  matrix products: 8.61 us -> 0 us
  local copies, waits for them, and re-layouts: 3.89 us -> 8.36 us
  other arithmetic: 3.25 us -> 1 us
    unnamed x2 -> x0, waiting for transfers between devices: 54.9 us -> none
    all_gather x1 -> x0, blocking collectives: 15.9 us -> none  [on_device(): piece = lax.all_gather(paired, 'seqtp', axis=1, tiled=True)]
    ppermute x1 -> x10, starting transfers between devices: 2.43 us -> 15.9 us  [the longest x5 10.1 us: home(): return lax.ppermute(x, ('section', 'seqtp'), pairs)]
    pallas_call x0 -> x4, Pallas kernels: none -> 8.69 us  [the longest x1 3.76 us: on_device(): pl.pallas_call(functools.partial(expert, chips), out_shape=[shape((chips...]
    dot_general x4 -> x0, matrix products: 8.61 us -> none  [the longest x3 6.16 us: transposed(): lax.dot_general(left, weight, (((1,), (1,)), ((), ())), preferred_element...]
    ppermute x1 -> x10, waiting for transfers between devices: 1.44 us -> 8.82 us  [the longest x3 4.46 us: to_chip(): return lax.ppermute(x, 'seqtp', [(i, near(i, k)) for i in range(members)])]
    unnamed x13 -> x24, local copies, waits for them, and re-layouts: 2.63 us -> 8.36 us
    reduce_sum x2 -> x0, other arithmetic: 1.27 us -> none  [the longest x1 1.12 us: on_device(): jnp.mean(scaled * unit, axis=-1, keepdims=True)]
  transfers between devices with their start and end apart: 2 -> 10, of which waited for: 2 -> 4; matrix products, arithmetic and copies ran while one was open for 1% -> 0% of each run, Pallas kernels for 0% -> 4%
where the time goes in v1:
time: 44 us; the launch traced here: 43.6 us
  starting transfers between devices  15.9 us (36%)
  waiting for transfers between devices  8.82 us (20%)
  Pallas kernels  8.69 us (20%)
  local copies, waits for them, and re-layouts  8.36 us (19%)
  other arithmetic  1 us (2%)
  between operations  0.74 us (2%)
    ppermute x5, starting transfers between devices, home(): return lax.ppermute(x, ('section', 'seqtp'), pairs)  10.1 us
    unnamed x24, local copies, waits for them, and re-layouts  8.36 us
    ppermute x3, starting transfers between devices, to_chip(): return lax.ppermute(x, 'seqtp', [(i, near(i, k)) for i in range(members)])  5.62 us
    ppermute x3, waiting for transfers between devices, to_chip(): return lax.ppermute(x, 'seqtp', [(i, near(i, k)) for i in range(members)])  4.46 us
    pallas_call x1, Pallas kernels, on_device(): pl.pallas_call(functools.partial(expert, chips), out_shape=[shape((chips...  3.76 us
    ppermute x5, waiting for transfers between devices, home(): return lax.ppermute(x, ('section', 'seqtp'), pairs)  3.03 us
    pallas_call x1, Pallas kernels, on_device(): pl.pallas_call(functools.partial(finish, chips), out_shape=shape((1, r, d...  1.7 us
    pallas_call x1, Pallas kernels, on_device(): pl.pallas_call(prepare, out_shape=[shape((r, 2 * d), bf16), shape((r, 2 *...  1.62 us
  transfers between devices with their start and end apart: 10, of which 4 were waited for; matrix products, arithmetic and copies ran while one was open for 0% of the time, Pallas kernels for 4%

profile of v1, /device:TPU:0, one launch (start us, length us, event | category | flops | bytes accessed | tf_op | source)
XLA Modules:
  0.0 43.6 jit_solution(17061593361042950319)
XLA Ops:
  0.7 1.6 %prepare.1 = (bf16[2,8192]{1,0:T(2,128)(2,1)}, bf16[2,10240]{1,0:T(2,128)(2,1)}) custom-call(s32[1]{0:T(128)S(6)} %copy.8.slot_ref, bf16[1,4,2,4096]{3,2,1,0:T(2,128)(2,1)} %saved_ref.1, bf16[1,2,4096]{2,1,0:T(2,128)(2,1)} %grad_ref.1, bf16[1,4096]{1,0:T(2,128)(2,1)} %gain_ref.1), custom_call_target="tpu_custom_call" | custom-call | tf_op jit(solution)/shard_map/prepare/pallas_call | solution.py:116
  2.3 5.0 %collective-permute-start.3 = (bf16[2,8192]{1,0:T(2,128)(2,1)}, bf16[2,8192]{1,0:T(2,128)(2,1)S(1)}, u32[]{:S(2)}, u32[]{:S(2)}) collective-permute-start(bf16[2,8192]{1,0:T(2,128)(2,1)} %get-tuple-element.14.refs_0_), channel_id=1, source_target_pairs={{0,6},{1,7},{2,4},{3,5},{4,2},{5,3},{6,0},{7,1},{8,14},{9,15},{10,... | collective-permute-start | bytes 98312 | tf_op jit(solution)/shard_map/ppermute | solution.py:103
  7.3 0.0 collective-permute-start.2
  7.3 0.6 %collective-permute-start.1 = (bf16[2,8192]{1,0:T(2,128)(2,1)}, bf16[2,8192]{1,0:T(2,128)(2,1)S(1)}, u32[]{:S(2)}, u32[]{:S(2)}) collective-permute-start(bf16[2,8192]{1,0:T(2,128)(2,1)} %get-tuple-element.14.refs_0_), channel_id=1, source_target_pairs={{0,2},{1,3},{2,0},{3,1},{4,6},{5,7},{6,4},{7,5},{8,10},{9,11},{10,... | collective-permute-start | bytes 98312 | tf_op jit(solution)/shard_map/ppermute | solution.py:103
  7.9 1.5 %collective-permute-done.3.refs_3_ = bf16[2,8192]{1,0:T(2,128)(2,1)S(1)} collective-permute-done((bf16[2,8192]{1,0:T(2,128)(2,1)}, bf16[2,8192]{1,0:T(2,128)(2,1)S(1)}, u32[]{:S(2)}, u32[]{:S(2)}) %collective-permute-start.3) | collective-permute-done | bytes 32800 | tf_op jit(solution)/shard_map/ppermute | solution.py:103
  9.4 2.9 %collective-permute-done.2.refs_2_ = bf16[2,8192]{1,0:T(2,128)(2,1)S(1)} collective-permute-done((bf16[2,8192]{1,0:T(2,128)(2,1)}, bf16[2,8192]{1,0:T(2,128)(2,1)S(1)}, u32[]{:S(2)}, u32[]{:S(2)}) %collective-permute-start.2) | collective-permute-done | bytes 32800 | tf_op jit(solution)/shard_map/ppermute | solution.py:103
  12.4 0.0 collective-permute-done.1.refs_1_
  12.4 0.0 copy-start.11
  12.4 1.0 %pad_maximum_fusion = bf16[4,2,8192]{2,1,0:T(2,128)(2,1)S(1)} fusion(bf16[1,2,8192]{2,1,0:T(2,128)(2,1)S(1)} %bitcast.5, bf16[1,2,8192]{2,1,0:T(2,128)(2,1)S(1)} %bitcast.6, bf16[1,2,8192]{2,1,0:T(2,128)(2,1)S(1)} %bitcast.7, bf16[1,2,8192]{2,1,0:T(2,128)(2,1)} %bitcast.4), kind=kLoop, calls=%fused_computation | loop fusion | flops 196608 | bytes 262144 | tf_op jit(solution)/shard_map/stack | solution.py:127
  13.4 0.1 collective-permute-start.4
  13.4 1.3 %collective-permute-done.4.refs_4_ = bf16[4,2,8192]{2,1,0:T(2,128)(2,1)S(1)} collective-permute-done((bf16[4,2,8192]{2,1,0:T(2,128)(2,1)S(1)}, bf16[4,2,8192]{2,1,0:T(2,128)(2,1)S(1)}, u32[]{:S(2)}, u32[]{:S(2)}) %collective-permute-start.4) | collective-permute-done | bytes 131104 | tf_op jit(solution)/shard_map/ppermute | solution.py:106
  14.8 0.0 copy-start
  14.8 1.9 %copy-done = bf16[4096,384]{1,0:T(8,128)(2,1)S(1)} copy-done((bf16[4096,384]{1,0:T(8,128)(2,1)S(1)}, bf16[4096,384]{1,0:T(8,128)(2,1)}, u32[]{:S(2)}) %copy-start) | copy-done | bytes 3145752
  16.7 0.0 copy-start.1
  16.7 1.9 %copy-done.1 = bf16[4096,384]{1,0:T(8,128)(2,1)S(1)} copy-done((bf16[4096,384]{1,0:T(8,128)(2,1)S(1)}, bf16[4096,384]{1,0:T(8,128)(2,1)}, u32[]{:S(2)}) %copy-start.1) | copy-done | bytes 3145752
  18.6 0.0 copy-start.2
  18.6 1.9 %copy-done.2 = bf16[384,4096]{1,0:T(8,128)(2,1)S(1)} copy-done((bf16[384,4096]{1,0:T(8,128)(2,1)S(1)}, bf16[384,4096]{1,0:T(8,128)(2,1)}, u32[]{:S(2)}) %copy-start.2) | copy-done | bytes 3145752
  20.4 0.0 copy-start.3
  20.4 0.8 %copy-done.3 = bf16[2,8192]{1,0:T(2,128)(2,1)S(1)} copy-done((bf16[2,8192]{1,0:T(2,128)(2,1)S(1)}, bf16[2,8192]{1,0:T(2,128)(2,1)}, u32[]{:S(2)}) %copy-start.3) | copy-done | bytes 32792
  21.2 3.8 %expert.1 = (f32[8,4096]{1,0:T(8,128)S(1)}, f32[8,4096]{1,0:T(8,128)S(1)}) custom-call(bf16[2,8192]{1,0:T(2,128)(2,1)S(1)} %copy-done.3, bf16[2,8192]{1,0:T(2,128)(2,1)S(1)} %collective-permute-done.1.refs_1_, bf16[2,8192]{1,0:T(2,128)(2,1)S(1)} %collective-permute-done.2.refs_2_, bf16[2,8192]{1,0:T(2,128)(2,1)S(1)} %collective-permute-done.3.refs_3_, ...), custom_call_target="tpu_custom_call" | custom-call | tf_op jit(solution)/shard_map/expert/pallas_call | solution.py:128
  25.0 0.0 copy-start.4
  25.0 0.7 %copy-done.4 = f32[8,4096]{1,0:T(8,128)} copy-done((f32[8,4096]{1,0:T(8,128)}, f32[8,4096]{1,0:T(8,128)S(1)}, u32[]{:S(2)}) %copy-start.4) | copy-done | bytes 131096
  25.6 0.1 collective-permute-start.5
  25.8 0.0 copy-done.11
  25.8 2.5 %collective-permute-start = (bf16[2,10240]{1,0:T(2,128)(2,1)S(1)}, bf16[2,10240]{1,0:T(2,128)(2,1)S(1)}, u32[]{:S(2)}, u32[]{:S(2)}) collective-permute-start(bf16[2,10240]{1,0:T(2,128)(2,1)S(1)} %copy-done.11), channel_id=1, source_target_pairs={{0,24},{1,25},{2,26},{3,27},{4,28},{5,29},{6,30},{7,31},{8,0},{9,1... | collective-permute-start | bytes 122888 | tf_op jit(solution)/shard_map/ppermute | solution.py:114
  28.2 0.0 collective-permute-done.5.got_ref
  28.3 0.0 copy-start.5
  28.3 0.7 %copy-done.5 = f32[8,4096]{1,0:T(8,128)} copy-done((f32[8,4096]{1,0:T(8,128)}, f32[8,4096]{1,0:T(8,128)S(1)}, u32[]{:S(2)}) %copy-start.5) | copy-done | bytes 131096
  28.9 1.6 %add_cores.1 = (bf16[2,4096]{1,0:T(2,128)(2,1)}, bf16[2,4096]{1,0:T(2,128)(2,1)}, bf16[2,4096]{1,0:T(2,128)(2,1)}, bf16[2,4096]{1,0:T(2,128)(2,1)}) custom-call(f32[8,4096]{1,0:T(8,128)} %copy-done.4, f32[8,4096]{1,0:T(8,128)} %copy-done.5), custom_call_target="tpu_custom_call" | custom-call | tf_op jit(solution)/shard_map/add_cores/pallas_call | solution.py:138
  30.5 1.2 %collective-permute-start.6 = (bf16[2,4096]{1,0:T(2,128)(2,1)}, bf16[2,4096]{1,0:T(2,128)(2,1)S(1)}, u32[]{:S(2)}, u32[]{:S(2)}) collective-permute-start(bf16[2,4096]{1,0:T(2,128)(2,1)} %get-tuple-element.17), channel_id=1, source_target_pairs={{0,24},{1,25},{2,26},{3,27},{4,28},{5,29},{6,30},{7,31},{8,0},{9,1... | collective-permute-start | bytes 49160 | tf_op jit(solution)/shard_map/ppermute | solution.py:114
  31.7 0.1 collective-permute-start.7
  31.8 2.8 %collective-permute-start.8 = (bf16[2,4096]{1,0:T(2,128)(2,1)}, bf16[2,4096]{1,0:T(2,128)(2,1)S(1)}, u32[]{:S(2)}, u32[]{:S(2)}) collective-permute-start(bf16[2,4096]{1,0:T(2,128)(2,1)} %get-tuple-element.19), channel_id=1, source_target_pairs={{4,24},{5,25},{6,26},{7,27},{0,28},{1,29},{2,30},{3,31},{12,0},{13... | collective-permute-start | bytes 49160 | tf_op jit(solution)/shard_map/ppermute | solution.py:114
  34.6 3.6 %collective-permute-start.9 = (bf16[2,4096]{1,0:T(2,128)(2,1)}, bf16[2,4096]{1,0:T(2,128)(2,1)S(1)}, u32[]{:S(2)}, u32[]{:S(2)}) collective-permute-start(bf16[2,4096]{1,0:T(2,128)(2,1)} %get-tuple-element.20), channel_id=1, source_target_pairs={{6,24},{7,25},{4,26},{5,27},{2,28},{3,29},{0,30},{1,31},{14,0},{15... | collective-permute-start | bytes 49160 | tf_op jit(solution)/shard_map/ppermute | solution.py:114
  38.2 0.0 collective-permute-done.own_ref
  38.2 0.0 copy-start.6
  38.2 0.0 collective-permute-done.6.refs_0_
  38.2 0.0 copy-start.7
  38.2 0.0 collective-permute-done.7.refs_1_
  38.2 0.0 copy-start.8
  38.2 0.0 collective-permute-done.8.refs_2_
  38.2 0.0 copy-start.9
  38.2 3.0 %collective-permute-done.9.refs_3_ = bf16[2,4096]{1,0:T(2,128)(2,1)S(1)} collective-permute-done((bf16[2,4096]{1,0:T(2,128)(2,1)}, bf16[2,4096]{1,0:T(2,128)(2,1)S(1)}, u32[]{:S(2)}, u32[]{:S(2)}) %collective-permute-start.9) | collective-permute-done | bytes 16416 | tf_op jit(solution)/shard_map/ppermute | solution.py:114
  41.2 0.0 copy-done.6
  41.2 0.0 copy-done.7
  41.2 0.0 copy-done.8
  41.2 0.0 copy-done.9
  41.3 0.0 copy-start.10
  41.3 0.6 %copy-done.10 = bf16[2,4096]{1,0:T(2,128)(2,1)} copy-done((bf16[2,4096]{1,0:T(2,128)(2,1)}, bf16[2,4096]{1,0:T(2,128)(2,1)S(1)}, u32[]{:S(2)}) %copy-start.10) | copy-done | bytes 16408
  41.9 1.7 %finish.1 = bf16[1,2,4096]{2,1,0:T(2,128)(2,1)} custom-call(bf16[2,10240]{1,0:T(2,128)(2,1)} %copy-done.6, bf16[2,4096]{1,0:T(2,128)(2,1)} %copy-done.7, bf16[2,4096]{1,0:T(2,128)(2,1)} %copy-done.8, bf16[2,4096]{1,0:T(2,128)(2,1)} %copy-done.9, bf16[2,4096]{1,0:T(2,128)(2,1)} %copy-done.10), custom_call_target="tpu_custom_call" | custom-call | tf_op jit(solution)/shard_map/finish/pallas_call | solution.py:149
Async XLA Ops:
  2.3 7.2 %collective-permute-start.3 = (bf16[2,8192]{1,0:T(2,128)(2,1)}, bf16[2,8192]{1,0:T(2,128)(2,1)S(1)}, u32[]{:S(2)}, u32[]{:S(2)}) collective-permute-start(bf16[2,8192]{1,0:T(2,128)(2,1)} %get-tuple-element.14.refs_0_), channel_id=1, source_target_pairs={{0,6},{1,7},{2,4},{3,5},{4,2},{5,3},{6,0},{7,1},{8,14},{9,15},{10,... | collective-permute-start | bytes 98312 | tf_op jit(solution)/shard_map/ppermute | solution.py:103
  7.3 5.0 %collective-permute-start.2 = (bf16[2,8192]{1,0:T(2,128)(2,1)}, bf16[2,8192]{1,0:T(2,128)(2,1)S(1)}, u32[]{:S(2)}, u32[]{:S(2)}) collective-permute-start(bf16[2,8192]{1,0:T(2,128)(2,1)} %get-tuple-element.14.refs_0_), channel_id=1, source_target_pairs={{0,4},{1,5},{2,6},{3,7},{4,0},{5,1},{6,2},{7,3},{8,12},{9,13},{10,... | collective-permute-start | bytes 98312 | tf_op jit(solution)/shard_map/ppermute | solution.py:103
  7.3 5.0 %collective-permute-start.1 = (bf16[2,8192]{1,0:T(2,128)(2,1)}, bf16[2,8192]{1,0:T(2,128)(2,1)S(1)}, u32[]{:S(2)}, u32[]{:S(2)}) collective-permute-start(bf16[2,8192]{1,0:T(2,128)(2,1)} %get-tuple-element.14.refs_0_), channel_id=1, source_target_pairs={{0,2},{1,3},{2,0},{3,1},{4,6},{5,7},{6,4},{7,5},{8,10},{9,11},{10,... | collective-permute-start | bytes 98312 | tf_op jit(solution)/shard_map/ppermute | solution.py:103
  12.4 13.4 %copy-start.11 = (bf16[2,10240]{1,0:T(2,128)(2,1)S(1)}, bf16[2,10240]{1,0:T(2,128)(2,1)}, u32[]{:S(2)}) copy-start(bf16[2,10240]{1,0:T(2,128)(2,1)} %get-tuple-element.13) | copy-start | bytes 122884
  13.4 1.4 %collective-permute-start.4 = (bf16[4,2,8192]{2,1,0:T(2,128)(2,1)S(1)}, bf16[4,2,8192]{2,1,0:T(2,128)(2,1)S(1)}, u32[]{:S(2)}, u32[]{:S(2)}) collective-permute-start(bf16[4,2,8192]{2,1,0:T(2,128)(2,1)S(1)} %pad_maximum_fusion), channel_id=1, source_target_pairs={{0,1},{1,0},{2,3},{3,2},{4,5},{5,4},{6,7},{7,6},{8,9},{9,8},{10,11... | collective-permute-start | bytes 393224 | tf_op jit(solution)/shard_map/ppermute | solution.py:106
  14.8 1.9 %copy-start = (bf16[4096,384]{1,0:T(8,128)(2,1)S(1)}, bf16[4096,384]{1,0:T(8,128)(2,1)}, u32[]{:S(2)}) copy-start(bf16[4096,384]{1,0:T(8,128)(2,1)} %refs_5_.1) | copy-start | bytes 9437188
  16.7 1.9 %copy-start.1 = (bf16[4096,384]{1,0:T(8,128)(2,1)S(1)}, bf16[4096,384]{1,0:T(8,128)(2,1)}, u32[]{:S(2)}) copy-start(bf16[4096,384]{1,0:T(8,128)(2,1)} %refs_6_.1) | copy-start | bytes 9437188
  18.6 1.9 %copy-start.2 = (bf16[384,4096]{1,0:T(8,128)(2,1)S(1)}, bf16[384,4096]{1,0:T(8,128)(2,1)}, u32[]{:S(2)}) copy-start(bf16[384,4096]{1,0:T(8,128)(2,1)} %refs_7_.1) | copy-start | bytes 9437188
  20.4 0.8 %copy-start.3 = (bf16[2,8192]{1,0:T(2,128)(2,1)S(1)}, bf16[2,8192]{1,0:T(2,128)(2,1)}, u32[]{:S(2)}) copy-start(bf16[2,8192]{1,0:T(2,128)(2,1)} %get-tuple-element.14.refs_0_) | copy-start | bytes 98308
  25.0 0.7 %copy-start.4 = (f32[8,4096]{1,0:T(8,128)}, f32[8,4096]{1,0:T(8,128)S(1)}, u32[]{:S(2)}) copy-start(f32[8,4096]{1,0:T(8,128)S(1)} %get-tuple-element.15.mine_ref) | copy-start | bytes 393220
  25.6 2.6 %collective-permute-start.5 = (f32[8,4096]{1,0:T(8,128)S(1)}, f32[8,4096]{1,0:T(8,128)S(1)}, u32[]{:S(2)}, u32[]{:S(2)}) collective-permute-start(f32[8,4096]{1,0:T(8,128)S(1)} %get-tuple-element.16), channel_id=1, source_target_pairs={{0,1},{1,0},{2,3},{3,2},{4,5},{5,4},{6,7},{7,6},{8,9},{9,8},{10,11... | collective-permute-start | bytes 393224 | tf_op jit(solution)/shard_map/ppermute | solution.py:106
  25.8 12.4 %collective-permute-start = (bf16[2,10240]{1,0:T(2,128)(2,1)S(1)}, bf16[2,10240]{1,0:T(2,128)(2,1)S(1)}, u32[]{:S(2)}, u32[]{:S(2)}) collective-permute-start(bf16[2,10240]{1,0:T(2,128)(2,1)S(1)} %copy-done.11), channel_id=1, source_target_pairs={{0,24},{1,25},{2,26},{3,27},{4,28},{5,29},{6,30},{7,31},{8,0},{9,1... | collective-permute-start | bytes 122888 | tf_op jit(solution)/shard_map/ppermute | solution.py:114
  28.3 0.7 %copy-start.5 = (f32[8,4096]{1,0:T(8,128)}, f32[8,4096]{1,0:T(8,128)S(1)}, u32[]{:S(2)}) copy-start(f32[8,4096]{1,0:T(8,128)S(1)} %collective-permute-done.5.got_ref) | copy-start | bytes 393220
  30.5 7.7 %collective-permute-start.6 = (bf16[2,4096]{1,0:T(2,128)(2,1)}, bf16[2,4096]{1,0:T(2,128)(2,1)S(1)}, u32[]{:S(2)}, u32[]{:S(2)}) collective-permute-start(bf16[2,4096]{1,0:T(2,128)(2,1)} %get-tuple-element.17), channel_id=1, source_target_pairs={{0,24},{1,25},{2,26},{3,27},{4,28},{5,29},{6,30},{7,31},{8,0},{9,1... | collective-permute-start | bytes 49160 | tf_op jit(solution)/shard_map/ppermute | solution.py:114
  31.7 6.5 %collective-permute-start.7 = (bf16[2,4096]{1,0:T(2,128)(2,1)}, bf16[2,4096]{1,0:T(2,128)(2,1)S(1)}, u32[]{:S(2)}, u32[]{:S(2)}) collective-permute-start(bf16[2,4096]{1,0:T(2,128)(2,1)} %get-tuple-element.18), channel_id=1, source_target_pairs={{2,24},{3,25},{0,26},{1,27},{6,28},{7,29},{4,30},{5,31},{10,0},{11... | collective-permute-start | bytes 49160 | tf_op jit(solution)/shard_map/ppermute | solution.py:114
  31.8 6.4 %collective-permute-start.8 = (bf16[2,4096]{1,0:T(2,128)(2,1)}, bf16[2,4096]{1,0:T(2,128)(2,1)S(1)}, u32[]{:S(2)}, u32[]{:S(2)}) collective-permute-start(bf16[2,4096]{1,0:T(2,128)(2,1)} %get-tuple-element.19), channel_id=1, source_target_pairs={{4,24},{5,25},{6,26},{7,27},{0,28},{1,29},{2,30},{3,31},{12,0},{13... | collective-permute-start | bytes 49160 | tf_op jit(solution)/shard_map/ppermute | solution.py:114
  34.6 6.6 %collective-permute-start.9 = (bf16[2,4096]{1,0:T(2,128)(2,1)}, bf16[2,4096]{1,0:T(2,128)(2,1)S(1)}, u32[]{:S(2)}, u32[]{:S(2)}) collective-permute-start(bf16[2,4096]{1,0:T(2,128)(2,1)} %get-tuple-element.20), channel_id=1, source_target_pairs={{6,24},{7,25},{4,26},{5,27},{2,28},{3,29},{0,30},{1,31},{14,0},{15... | collective-permute-start | bytes 49160 | tf_op jit(solution)/shard_map/ppermute | solution.py:114
  38.2 3.1 %copy-start.6 = (bf16[2,10240]{1,0:T(2,128)(2,1)}, bf16[2,10240]{1,0:T(2,128)(2,1)S(1)}, u32[]{:S(2)}) copy-start(bf16[2,10240]{1,0:T(2,128)(2,1)S(1)} %collective-permute-done.own_ref) | copy-start | bytes 122884
  38.2 3.1 %copy-start.7 = (bf16[2,4096]{1,0:T(2,128)(2,1)}, bf16[2,4096]{1,0:T(2,128)(2,1)S(1)}, u32[]{:S(2)}) copy-start(bf16[2,4096]{1,0:T(2,128)(2,1)S(1)} %collective-permute-done.6.refs_0_) | copy-start | bytes 49156
  38.2 3.1 %copy-start.8 = (bf16[2,4096]{1,0:T(2,128)(2,1)}, bf16[2,4096]{1,0:T(2,128)(2,1)S(1)}, u32[]{:S(2)}) copy-start(bf16[2,4096]{1,0:T(2,128)(2,1)S(1)} %collective-permute-done.7.refs_1_) | copy-start | bytes 49156
  38.2 3.0 %copy-start.9 = (bf16[2,4096]{1,0:T(2,128)(2,1)}, bf16[2,4096]{1,0:T(2,128)(2,1)S(1)}, u32[]{:S(2)}) copy-start(bf16[2,4096]{1,0:T(2,128)(2,1)S(1)} %collective-permute-done.8.refs_2_) | copy-start | bytes 49156
  41.3 0.6 %copy-start.10 = (bf16[2,4096]{1,0:T(2,128)(2,1)}, bf16[2,4096]{1,0:T(2,128)(2,1)S(1)}, u32[]{:S(2)}) copy-start(bf16[2,4096]{1,0:T(2,128)(2,1)S(1)} %collective-permute-done.9.refs_3_) | copy-start | bytes 49156

commit v2 on v1

v2 whole, which is shorter than its diff:
```python
import functools

import jax
import jax.numpy as jnp
from jax import lax
from jax.experimental import pallas as pl
from jax.experimental.pallas import tpu as pltpu
from jax.sharding import PartitionSpec as P

EPS = 1e-05
CORES = 2


VMEM = pltpu.VMEM


def whole(n):
    return [pl.BlockSpec(memory_space=VMEM)] * n


def near_core(*arrays):
    return [pltpu.with_memory_space_constraint(x, VMEM) for x in arrays]


def params(mib):
    return pltpu.CompilerParams(vmem_limit_bytes=mib * 2**20)


def prepare(slot_hbm, saved_hbm, grad_hbm, gain_hbm, sent_ref, own_ref, *scratch):
    slot_ref, saved_ref, grad_ref, gain_ref, sems = scratch
    copies = [
        pltpu.make_async_copy(src, dst, sems.at[i])
        for i, (src, dst) in enumerate(
            zip((slot_hbm, saved_hbm, grad_hbm, gain_hbm), scratch)
        )
    ]
    for copy in copies:
        copy.start()
    for copy in copies:
        copy.wait()
    d = grad_ref.shape[-1]
    behind = saved_ref[0, slot_ref[0]]
    wide = behind.astype(jnp.float32)
    gain = gain_ref[...].astype(jnp.float32)
    recip = lax.rsqrt(jnp.mean(wide * wide, axis=-1, keepdims=True) + EPS)
    grad = grad_ref[0]
    sent_ref[:, :d] = (wide * recip * gain).astype(jnp.bfloat16)
    sent_ref[:, d:] = grad
    own_ref[:, :d] = behind
    own_ref[:, d : 2 * d] = grad
    half = d // 2
    own_ref[0:1, 2 * d :] = gain_ref[:, :half]
    own_ref[1:2, 2 * d :] = gain_ref[:, half:]


def stack(n, *refs):
    out_ref = refs[-1]
    r = refs[0].shape[0]
    for k, ref in enumerate(refs[:n]):
        out_ref[k * r : (k + 1) * r] = ref[...]


def nt(left, weight):
    return lax.dot_general(
        left, weight, (((1,), (1,)), ((), ())), preferred_element_type=jnp.float32
    )


def fetch(gate_hbm, up_hbm, down_hbm, both_ref, down_ref, sems):
    d, h = gate_hbm.shape
    parts = sems.shape[1]
    copies = []
    for n in range(parts):
        rows, cols = pl.ds(n * d // parts, d // parts), pl.ds(n * h // parts, h // parts)
        copies += [
            pltpu.make_async_copy(gate_hbm.at[rows], both_ref.at[rows, :h], sems.at[0, n]),
            pltpu.make_async_copy(up_hbm.at[rows], both_ref.at[rows, h:], sems.at[1, n]),
            pltpu.make_async_copy(down_hbm.at[cols], down_ref.at[cols], sems.at[2, n]),
        ]
    for copy in copies:
        copy.start()
    for copy in copies:
        copy.wait()


def expert(*refs):
    *blocks, both_ref, down_ref, mine_ref, other_ref, rows_ref = refs
    d, h2 = both_ref.shape
    h = h2 // 2
    r = blocks[0].shape[0]
    for k, ref in enumerate(blocks):
        rows_ref[k * r : (k + 1) * r] = ref[...].astype(jnp.float32)
    normed = rows_ref[:, :d].astype(jnp.bfloat16)
    grad = rows_ref[:, d:].astype(jnp.bfloat16)
    both = jnp.dot(normed, both_ref[...], preferred_element_type=jnp.float32)
    gate, up = both[:, :h], both[:, h:]
    d_hidden = nt(grad, down_ref[...])
    p = jax.nn.sigmoid(gate)
    d_gate = d_hidden * up * p * (1.0 + gate * (1.0 - p))
    d_up = d_hidden * gate * p
    d_both = jnp.concatenate([d_gate, d_up], axis=1).astype(jnp.bfloat16)
    total = nt(d_both, both_ref[...])
    half = total.shape[0] // 2
    mine_ref[...] = total[:half]
    other_ref[...] = total[half:]


def add_cores(mine_ref, got_ref, *out_refs):
    total = mine_ref[...] + got_ref[...]
    r = out_refs[0].shape[0]
    for k, ref in enumerate(out_refs):
        ref[...] = total[k * r : (k + 1) * r].astype(ref.dtype)


def add_chips(*refs):
    *parts, keep_ref, send_ref = refs
    total = sum(ref[...].astype(jnp.float32) for ref in parts)
    r = keep_ref.shape[0]
    keep_ref[...] = total[:r]
    send_ref[...] = total[r:]


def finish(own_ref, keep_ref, got_ref, out_ref, gain_ref):
    d = out_ref.shape[-1]
    half = d // 2
    gain_ref[:, :half] = own_ref[0:1, 2 * d :].astype(jnp.float32)
    gain_ref[:, half:] = own_ref[1:2, 2 * d :].astype(jnp.float32)
    wide = own_ref[:, :d].astype(jnp.float32)
    grad = own_ref[:, d : 2 * d].astype(jnp.float32)
    recip = lax.rsqrt(jnp.mean(wide * wide, axis=-1, keepdims=True) + EPS)
    scaled = gain_ref[...] * (keep_ref[...] + got_ref[...])
    unit = wide * recip
    mean = jnp.mean(scaled * unit, axis=-1, keepdims=True)
    out_ref[0] = (grad + recip * (scaled - unit * mean)).astype(out_ref.dtype)


def on_device(sections, members, saved_in, grad_in, slot_table, gain, w_gate, w_up, w_down):
    chips = members // CORES
    r, d = grad_in.shape[1:]
    f32, bf16 = jnp.float32, jnp.bfloat16
    shape = jax.ShapeDtypeStruct
    served = [list(range(chips - 1 - c, -1, -CORES)) for c in range(CORES)]
    steps = [list(ks) for ks in zip(*served)][::-1]

    def near(i, ks):
        chip, core = divmod(i, CORES)
        k = ks[core]
        return (chip ^ k if chips & (chips - 1) == 0 else (chip + k) % chips) * CORES + core

    def to_chip(x, ks):
        return lax.ppermute(x, "seqtp", [(i, near(i, ks)) for i in range(members)])

    def to_core(x):
        return lax.ppermute(x, "seqtp", [(i, i ^ 1) for i in range(members)])

    def home(x, ks):
        pairs = [
            (s * members + near(i, ks), (s - 1) % sections * members + i)
            for s in range(sections)
            for i in range(members)
        ]
        return lax.ppermute(x, ("section", "seqtp"), pairs)

    sent, own = pl.pallas_call(
        prepare,
        out_shape=[VMEM((r, 2 * d), bf16), VMEM((r, 2 * d + d // 2), bf16)],
        in_specs=[pl.BlockSpec(memory_space=pl.ANY)] * 4,
        out_specs=whole(2),
        scratch_shapes=[
            pltpu.SMEM(slot_table.shape, slot_table.dtype),
            VMEM(saved_in.shape, bf16),
            VMEM(grad_in.shape, bf16),
            VMEM(gain.shape, bf16),
            pltpu.SemaphoreType.DMA((4,)),
        ],
        compiler_params=params(4),
        name="prepare",
    )(*[slot_table] + [pltpu.with_memory_space_constraint(x, pltpu.HBM) for x in (saved_in, grad_in, gain)])
    def stacked(parts, after=()):
        rows = sum(part.shape[0] for part in parts)
        return pl.pallas_call(
            functools.partial(stack, len(parts)),
            out_shape=VMEM((rows,) + parts[0].shape[1:], bf16),
            in_specs=whole(len(parts)) + [pl.BlockSpec(memory_space=pl.ANY)] * len(after),
            out_specs=pl.BlockSpec(memory_space=VMEM),
            compiler_params=params(4),
            name="stack",
        )(*near_core(*parts, *after))

    chip_rows = stacked([sent, to_core(sent)])
    hidden = w_down.shape[0]
    weights = pl.pallas_call(
        fetch,
        out_shape=[VMEM((d, 2 * hidden), bf16), VMEM((hidden, d), bf16)],
        in_specs=[pl.BlockSpec(memory_space=pl.ANY)] * 3,
        out_specs=whole(2),
        scratch_shapes=[pltpu.SemaphoreType.DMA((3, 1))],
        compiler_params=params(4),
        cost_estimate=pl.CostEstimate(flops=0, bytes_accessed=12 * d * hidden, transcendentals=0),
        name="fetch",
    )(*[pltpu.with_memory_space_constraint(x, pltpu.HBM) for x in (w_gate, w_up, w_down)])
    blocks = [to_chip(chip_rows, ks) for ks in steps[::-1]][::-1]
    block = stacked(blocks, weights)
    blocks = [block, to_core(block)]
    rows = block.shape[0]
    mine, other = pl.pallas_call(
        expert,
        out_shape=[VMEM((rows, d), f32)] * 2,
        in_specs=whole(len(blocks) + 2),
        out_specs=whole(2),
        scratch_shapes=[VMEM((2 * rows, 2 * d), f32)],
        compiler_params=params(16),
        name="expert",
    )(*near_core(*blocks, *weights))
    sums = pl.pallas_call(
        add_cores,
        out_shape=[VMEM((CORES * r, d), bf16)] * len(steps),
        in_specs=whole(2),
        out_specs=whole(len(steps)),
        compiler_params=params(4),
        name="add_cores",
    )(*near_core(mine, to_core(other)))
    landed = [home(block, ks) for block, ks in zip(sums[::-1], steps[::-1])]
    own = home(own, [0] * CORES)
    keep, send = pl.pallas_call(
        add_chips,
        out_shape=[VMEM((r, d), f32)] * 2,
        in_specs=whole(len(steps)),
        out_specs=whole(2),
        compiler_params=params(4),
        name="add_chips",
    )(*near_core(*landed))
    return pl.pallas_call(
        finish,
        out_shape=shape((1, r, d), bf16),
        in_specs=whole(3),
        out_specs=pl.BlockSpec(memory_space=VMEM),
        scratch_shapes=[VMEM((1, d), f32)],
        compiler_params=params(4),
        name="finish",
    )(*near_core(own, keep, to_core(send)))


def solution(mesh):
    return jax.shard_map(
        functools.partial(on_device, mesh.shape["section"], mesh.shape["seqtp"]),
        mesh=mesh,
        in_specs=(
            P("section", None, "seqtp", None),
            P("section", "seqtp", None),
            P("section"),
            P("section", None),
            P(None, "seqtp"),
            P(None, "seqtp"),
            P("seqtp", None),
        ),
        out_specs=P("section", "seqtp", None),
        check_vma=False,
    )
```

time: 44 us -> 30.5 us (0.69)
  local copies, waits for them, and re-layouts: 8.36 us -> 0 us
  starting transfers between devices: 15.9 us -> 12 us
  other arithmetic: 1 us -> 0 us
  Pallas kernels: 8.69 us -> 9.17 us
    unnamed x24 -> x0, local copies, waits for them, and re-layouts: 8.36 us -> none
    ppermute x5 -> x3, starting transfers between devices: 10.1 us -> 4.27 us  [home(): return lax.ppermute(x, ('section', 'seqtp'), pairs)]
    ppermute x3 -> x2, waiting for transfers between devices: 4.46 us -> 0.43 us  [to_chip(): return lax.ppermute(x, 'seqtp', [(i, near(i, ks)) for i in range(members)])]
    ppermute x2 -> x4, waiting for transfers between devices: 1.34 us -> 4.4 us  [to_core(): return lax.ppermute(x, 'seqtp', [(i, i ^ 1) for i in range(members)])]
    ppermute x3 -> x2, starting transfers between devices: 5.62 us -> 6.92 us  [to_chip(): return lax.ppermute(x, 'seqtp', [(i, near(i, ks)) for i in range(members)])]
    another operation x1 -> x0, other arithmetic: 1 us -> none  [on_device(): far = to_core(jnp.stack(blocks))]
    ppermute x2 -> x4, starting transfers between devices: 0.22 us -> 0.83 us  [to_core(): return lax.ppermute(x, 'seqtp', [(i, i ^ 1) for i in range(members)])]
    ppermute x5 -> x3, waiting for transfers between devices: 3.03 us -> 3.59 us  [home(): return lax.ppermute(x, ('section', 'seqtp'), pairs)]
  transfers between devices with their start and end apart: 10 -> 9, of which waited for: 4 -> 8; matrix products, arithmetic and copies ran while one was open for 0% -> 0% of each run, Pallas kernels for 4% -> 13%
where the time goes in v2:
time: 30.5 us; the launch traced here: 30.3 us
  starting transfers between devices  12 us (39%)
  Pallas kernels  9.17 us (30%)
  waiting for transfers between devices  8.42 us (28%)
  between operations  0.72 us (2%)
    ppermute x2, starting transfers between devices, to_chip(): return lax.ppermute(x, 'seqtp', [(i, near(i, ks)) for i in range(members)])  6.92 us
    ppermute x4, waiting for transfers between devices, to_core(): return lax.ppermute(x, 'seqtp', [(i, i ^ 1) for i in range(members)])  4.4 us
    ppermute x3, starting transfers between devices, home(): return lax.ppermute(x, ('section', 'seqtp'), pairs)  4.27 us
    pallas_call x1, Pallas kernels, on_device(): pl.pallas_call(fetch, out_shape=[VMEM((d, 2 * hidden), bf16), VMEM((hidde...  3.79 us
    ppermute x3, waiting for transfers between devices, home(): return lax.ppermute(x, ('section', 'seqtp'), pairs)  3.59 us
    pallas_call x1, Pallas kernels, on_device(): pl.pallas_call(expert, out_shape=[VMEM((rows, d), f32)] * 2, in_specs=who...  3.4 us
    pallas_call x1, Pallas kernels, on_device(): pl.pallas_call(prepare, out_shape=[VMEM((r, 2 * d), bf16), VMEM((r, 2 * d...  1.02 us
    pallas_call x1, Pallas kernels, on_device(): pl.pallas_call(finish, out_shape=shape((1, r, d), bf16), in_specs=whole(3...  0.88 us
  transfers between devices with their start and end apart: 9, of which 8 were waited for; matrix products, arithmetic and copies ran while one was open for 0% of the time, Pallas kernels for 13%

profile of v2, /device:TPU:0, one launch (start us, length us, event | category | flops | bytes accessed | tf_op | source)
XLA Modules:
  0.0 30.3 jit_solution(6031929286512485907)
XLA Ops:
  0.7 1.0 %prepare.1 = (bf16[2,8192]{1,0:T(2,128)(2,1)S(1)}, bf16[2,10240]{1,0:T(2,128)(2,1)S(1)}) custom-call(s32[1]{0:T(128)S(6)} %copy.8.slot_hbm, bf16[1,4,2,4096]{3,2,1,0:T(2,128)(2,1)} %saved_hbm.1, bf16[1,2,4096]{2,1,0:T(2,128)(2,1)} %grad_hbm.1, bf16[1,4096]{1,0:T(2,128)(2,1)} %gain_hbm.1), custom_call_target="tpu_custom_call" | custom-call | tf_op jit(solution)/shard_map/prepare/pallas_call | solution.py:164
  1.7 0.5 %collective-permute-start.1 = (bf16[2,8192]{1,0:T(2,128)(2,1)S(1)}, bf16[2,8192]{1,0:T(2,128)(2,1)S(1)}, u32[]{:S(2)}, u32[]{:S(2)}) collective-permute-start(bf16[2,8192]{1,0:T(2,128)(2,1)S(1)} %get-tuple-element.16.refs_0_), channel_id=1, source_target_pairs={{0,1},{1,0},{2,3},{3,2},{4,5},{5,4},{6,7},{7,6},{8,9},{9,8},{10,11... | collective-permute-start | bytes 98312 | tf_op jit(solution)/shard_map/ppermute | solution.py:154
  2.2 0.9 %collective-permute-done.1.refs_1_ = bf16[2,8192]{1,0:T(2,128)(2,1)S(1)} collective-permute-done((bf16[2,8192]{1,0:T(2,128)(2,1)S(1)}, bf16[2,8192]{1,0:T(2,128)(2,1)S(1)}, u32[]{:S(2)}, u32[]{:S(2)}) %collective-permute-start.1) | collective-permute-done | bytes 32800 | tf_op jit(solution)/shard_map/ppermute | solution.py:154
  3.1 5.0 %collective-permute-start.3 = (bf16[4,8192]{1,0:T(4,128)(2,1)S(1)}, bf16[4,8192]{1,0:T(4,128)(2,1)S(1)}, u32[]{:S(2)}, u32[]{:S(2)}) collective-permute-start(bf16[4,8192]{1,0:T(4,128)(2,1)S(1)} %stack.2), channel_id=1, source_target_pairs={{0,6},{1,5},{2,4},{3,7},{4,2},{5,1},{6,0},{7,3},{8,14},{9,13},{10,... | collective-permute-start | bytes 196616 | tf_op jit(solution)/shard_map/ppermute | solution.py:151
  8.1 1.9 %collective-permute-start.2 = (bf16[4,8192]{1,0:T(4,128)(2,1)S(1)}, bf16[4,8192]{1,0:T(4,128)(2,1)S(1)}, u32[]{:S(2)}, u32[]{:S(2)}) collective-permute-start(bf16[4,8192]{1,0:T(4,128)(2,1)S(1)} %stack.2), channel_id=1, source_target_pairs={{0,2},{1,1},{2,0},{3,3},{4,6},{5,5},{6,4},{7,7},{8,10},{9,9},{10,8... | collective-permute-start | bytes 196616 | tf_op jit(solution)/shard_map/ppermute | solution.py:151
  10.0 3.8 %fetch.1 = (bf16[4096,768]{1,0:T(8,128)(2,1)S(1)}, bf16[384,4096]{1,0:T(8,128)(2,1)S(1)}) custom-call(bf16[4096,384]{1,0:T(8,128)(2,1)} %gate_hbm.1, bf16[4096,384]{1,0:T(8,128)(2,1)} %up_hbm.1, bf16[384,4096]{1,0:T(8,128)(2,1)} %down_hbm.1), custom_call_target="tpu_custom_call" | custom-call | bytes 18874368 | tf_op jit(solution)/shard_map/fetch/pallas_call | solution.py:192
  13.8 0.0 collective-permute-done.3.refs_1_
  13.8 0.4 %collective-permute-done.2.refs_0_ = bf16[4,8192]{1,0:T(4,128)(2,1)S(1)} collective-permute-done((bf16[4,8192]{1,0:T(4,128)(2,1)S(1)}, bf16[4,8192]{1,0:T(4,128)(2,1)S(1)}, u32[]{:S(2)}, u32[]{:S(2)}) %collective-permute-start.2) | collective-permute-done | bytes 65568 | tf_op jit(solution)/shard_map/ppermute | solution.py:151
  14.3 0.1 collective-permute-start.4
  14.4 1.3 %collective-permute-done.4.refs_1_ = bf16[8,8192]{1,0:T(8,128)(2,1)S(1)} collective-permute-done((bf16[8,8192]{1,0:T(8,128)(2,1)S(1)}, bf16[8,8192]{1,0:T(8,128)(2,1)S(1)}, u32[]{:S(2)}, u32[]{:S(2)}) %collective-permute-start.4) | collective-permute-done | bytes 131104 | tf_op jit(solution)/shard_map/ppermute | solution.py:154
  15.7 3.4 %expert.1 = (f32[8,4096]{1,0:T(8,128)S(1)}, f32[8,4096]{1,0:T(8,128)S(1)}) custom-call(bf16[8,8192]{1,0:T(8,128)(2,1)S(1)} %stack.3.refs_0_, bf16[8,8192]{1,0:T(8,128)(2,1)S(1)} %collective-permute-done.4.refs_1_, bf16[4096,768]{1,0:T(8,128)(2,1)S(1)} %get-tuple-element.17.refs_2_, bf16[384,4096]{1,0:T(8,128)(2,1)S(1)} %get-tuple-element.18.refs_3_), custom_call_target="tpu_custom_call" | custom-call | tf_op jit(solution)/shard_map/expert/pallas_call | solution.py:206
  19.1 0.2 collective-permute-start.5
  19.3 1.2 %collective-permute-done.5.got_ref = f32[8,4096]{1,0:T(8,128)S(1)} collective-permute-done((f32[8,4096]{1,0:T(8,128)S(1)}, f32[8,4096]{1,0:T(8,128)S(1)}, u32[]{:S(2)}, u32[]{:S(2)}) %collective-permute-start.5) | collective-permute-done | bytes 131104 | tf_op jit(solution)/shard_map/ppermute | solution.py:154
  20.5 2.7 %collective-permute-start.6 = (bf16[4,4096]{1,0:T(4,128)(2,1)S(1)}, bf16[4,4096]{1,0:T(4,128)(2,1)S(1)}, u32[]{:S(2)}, u32[]{:S(2)}) collective-permute-start(bf16[4,4096]{1,0:T(4,128)(2,1)S(1)} %get-tuple-element.21), channel_id=1, source_target_pairs={{6,24},{5,25},{4,26},{7,27},{2,28},{1,29},{0,30},{3,31},{14,0},{13... | collective-permute-start | bytes 98312 | tf_op jit(solution)/shard_map/ppermute | solution.py:162
  23.2 0.9 %collective-permute-start.7 = (bf16[4,4096]{1,0:T(4,128)(2,1)S(1)}, bf16[4,4096]{1,0:T(4,128)(2,1)S(1)}, u32[]{:S(2)}, u32[]{:S(2)}) collective-permute-start(bf16[4,4096]{1,0:T(4,128)(2,1)S(1)} %get-tuple-element.22), channel_id=1, source_target_pairs={{2,24},{1,25},{0,26},{3,27},{6,28},{5,29},{4,30},{7,31},{10,0},{9,... | collective-permute-start | bytes 98312 | tf_op jit(solution)/shard_map/ppermute | solution.py:162
  24.1 0.7 %collective-permute-start = (bf16[2,10240]{1,0:T(2,128)(2,1)S(1)}, bf16[2,10240]{1,0:T(2,128)(2,1)S(1)}, u32[]{:S(2)}, u32[]{:S(2)}) collective-permute-start(bf16[2,10240]{1,0:T(2,128)(2,1)S(1)} %get-tuple-element.15), channel_id=1, source_target_pairs={{0,24},{1,25},{2,26},{3,27},{4,28},{5,29},{6,30},{7,31},{8,0},{9,1... | collective-permute-start | bytes 122888 | tf_op jit(solution)/shard_map/ppermute | solution.py:162
  24.8 2.4 %collective-permute-done.6.refs_0_ = bf16[4,4096]{1,0:T(4,128)(2,1)S(1)} collective-permute-done((bf16[4,4096]{1,0:T(4,128)(2,1)S(1)}, bf16[4,4096]{1,0:T(4,128)(2,1)S(1)}, u32[]{:S(2)}, u32[]{:S(2)}) %collective-permute-start.6) | collective-permute-done | bytes 32800 | tf_op jit(solution)/shard_map/ppermute | solution.py:162
  27.1 1.0 %collective-permute-done.7.refs_1_ = bf16[4,4096]{1,0:T(4,128)(2,1)S(1)} collective-permute-done((bf16[4,4096]{1,0:T(4,128)(2,1)S(1)}, bf16[4,4096]{1,0:T(4,128)(2,1)S(1)}, u32[]{:S(2)}, u32[]{:S(2)}) %collective-permute-start.7) | collective-permute-done | bytes 32800 | tf_op jit(solution)/shard_map/ppermute | solution.py:162
  28.2 0.1 collective-permute-start.8
  28.2 0.2 collective-permute-done.own_ref
  28.4 1.0 %collective-permute-done.8.got_ref = f32[2,4096]{1,0:T(2,128)S(1)} collective-permute-done((f32[2,4096]{1,0:T(2,128)S(1)}, f32[2,4096]{1,0:T(2,128)S(1)}, u32[]{:S(2)}, u32[]{:S(2)}) %collective-permute-start.8) | collective-permute-done | bytes 32800 | tf_op jit(solution)/shard_map/ppermute | solution.py:154
  29.4 0.9 %finish.1 = bf16[1,2,4096]{2,1,0:T(2,128)(2,1)} custom-call(bf16[2,10240]{1,0:T(2,128)(2,1)S(1)} %collective-permute-done.own_ref, f32[2,4096]{1,0:T(2,128)S(1)} %get-tuple-element.23.keep_ref, f32[2,4096]{1,0:T(2,128)S(1)} %collective-permute-done.8.got_ref), custom_call_target="tpu_custom_call" | custom-call | tf_op jit(solution)/shard_map/finish/pallas_call | solution.py:233
  (4 shorter events, 0.1 us)
Async XLA Ops:
  1.7 1.4 %collective-permute-start.1 = (bf16[2,8192]{1,0:T(2,128)(2,1)S(1)}, bf16[2,8192]{1,0:T(2,128)(2,1)S(1)}, u32[]{:S(2)}, u32[]{:S(2)}) collective-permute-start(bf16[2,8192]{1,0:T(2,128)(2,1)S(1)} %get-tuple-element.16.refs_0_), channel_id=1, source_target_pairs={{0,1},{1,0},{2,3},{3,2},{4,5},{5,4},{6,7},{7,6},{8,9},{9,8},{10,11... | collective-permute-start | bytes 98312 | tf_op jit(solution)/shard_map/ppermute | solution.py:154
  3.1 10.7 %collective-permute-start.3 = (bf16[4,8192]{1,0:T(4,128)(2,1)S(1)}, bf16[4,8192]{1,0:T(4,128)(2,1)S(1)}, u32[]{:S(2)}, u32[]{:S(2)}) collective-permute-start(bf16[4,8192]{1,0:T(4,128)(2,1)S(1)} %stack.2), channel_id=1, source_target_pairs={{0,6},{1,5},{2,4},{3,7},{4,2},{5,1},{6,0},{7,3},{8,14},{9,13},{10,... | collective-permute-start | bytes 196616 | tf_op jit(solution)/shard_map/ppermute | solution.py:151
  8.1 6.1 %collective-permute-start.2 = (bf16[4,8192]{1,0:T(4,128)(2,1)S(1)}, bf16[4,8192]{1,0:T(4,128)(2,1)S(1)}, u32[]{:S(2)}, u32[]{:S(2)}) collective-permute-start(bf16[4,8192]{1,0:T(4,128)(2,1)S(1)} %stack.2), channel_id=1, source_target_pairs={{0,2},{1,1},{2,0},{3,3},{4,6},{5,5},{6,4},{7,7},{8,10},{9,9},{10,8... | collective-permute-start | bytes 196616 | tf_op jit(solution)/shard_map/ppermute | solution.py:151
  14.3 1.4 %collective-permute-start.4 = (bf16[8,8192]{1,0:T(8,128)(2,1)S(1)}, bf16[8,8192]{1,0:T(8,128)(2,1)S(1)}, u32[]{:S(2)}, u32[]{:S(2)}) collective-permute-start(bf16[8,8192]{1,0:T(8,128)(2,1)S(1)} %stack.3.refs_0_), channel_id=1, source_target_pairs={{0,1},{1,0},{2,3},{3,2},{4,5},{5,4},{6,7},{7,6},{8,9},{9,8},{10,11... | collective-permute-start | bytes 393224 | tf_op jit(solution)/shard_map/ppermute | solution.py:154
  19.1 1.4 %collective-permute-start.5 = (f32[8,4096]{1,0:T(8,128)S(1)}, f32[8,4096]{1,0:T(8,128)S(1)}, u32[]{:S(2)}, u32[]{:S(2)}) collective-permute-start(f32[8,4096]{1,0:T(8,128)S(1)} %get-tuple-element.20), channel_id=1, source_target_pairs={{0,1},{1,0},{2,3},{3,2},{4,5},{5,4},{6,7},{7,6},{8,9},{9,8},{10,11... | collective-permute-start | bytes 393224 | tf_op jit(solution)/shard_map/ppermute | solution.py:154
  20.5 6.7 %collective-permute-start.6 = (bf16[4,4096]{1,0:T(4,128)(2,1)S(1)}, bf16[4,4096]{1,0:T(4,128)(2,1)S(1)}, u32[]{:S(2)}, u32[]{:S(2)}) collective-permute-start(bf16[4,4096]{1,0:T(4,128)(2,1)S(1)} %get-tuple-element.21), channel_id=1, source_target_pairs={{6,24},{5,25},{4,26},{7,27},{2,28},{1,29},{0,30},{3,31},{14,0},{13... | collective-permute-start | bytes 98312 | tf_op jit(solution)/shard_map/ppermute | solution.py:162
  23.2 4.9 %collective-permute-start.7 = (bf16[4,4096]{1,0:T(4,128)(2,1)S(1)}, bf16[4,4096]{1,0:T(4,128)(2,1)S(1)}, u32[]{:S(2)}, u32[]{:S(2)}) collective-permute-start(bf16[4,4096]{1,0:T(4,128)(2,1)S(1)} %get-tuple-element.22), channel_id=1, source_target_pairs={{2,24},{1,25},{0,26},{3,27},{6,28},{5,29},{4,30},{7,31},{10,0},{9,... | collective-permute-start | bytes 98312 | tf_op jit(solution)/shard_map/ppermute | solution.py:162
  24.1 4.4 %collective-permute-start = (bf16[2,10240]{1,0:T(2,128)(2,1)S(1)}, bf16[2,10240]{1,0:T(2,128)(2,1)S(1)}, u32[]{:S(2)}, u32[]{:S(2)}) collective-permute-start(bf16[2,10240]{1,0:T(2,128)(2,1)S(1)} %get-tuple-element.15), channel_id=1, source_target_pairs={{0,24},{1,25},{2,26},{3,27},{4,28},{5,29},{6,30},{7,31},{8,0},{9,1... | collective-permute-start | bytes 122888 | tf_op jit(solution)/shard_map/ppermute | solution.py:162
  28.2 1.3 %collective-permute-start.8 = (f32[2,4096]{1,0:T(2,128)S(1)}, f32[2,4096]{1,0:T(2,128)S(1)}, u32[]{:S(2)}, u32[]{:S(2)}) collective-permute-start(f32[2,4096]{1,0:T(2,128)S(1)} %get-tuple-element.24), channel_id=1, source_target_pairs={{0,1},{1,0},{2,3},{3,2},{4,5},{5,4},{6,7},{7,6},{8,9},{9,8},{10,11... | collective-permute-start | bytes 98312 | tf_op jit(solution)/shard_map/ppermute | solution.py:154

commit v3 on v2

--- a/solution.py
+++ b/solution.py
@@ -60,46 +60,62 @@
         out_ref[k * r : (k + 1) * r] = ref[...]
 
 
+def nn(left, weight):
+    return jnp.dot(left, weight, preferred_element_type=jnp.float32)
+
+
 def nt(left, weight):
     return lax.dot_general(
         left, weight, (((1,), (1,)), ((), ())), preferred_element_type=jnp.float32
     )
 
 
-def fetch(gate_hbm, up_hbm, down_hbm, both_ref, down_ref, sems):
+def fetch(gate_hbm, up_hbm, both_ref, turned_ref, sems, up_sem):
     d, h = gate_hbm.shape
-    parts = sems.shape[1]
-    copies = []
-    for n in range(parts):
-        rows, cols = pl.ds(n * d // parts, d // parts), pl.ds(n * h // parts, h // parts)
-        copies += [
-            pltpu.make_async_copy(gate_hbm.at[rows], both_ref.at[rows, :h], sems.at[0, n]),
-            pltpu.make_async_copy(up_hbm.at[rows], both_ref.at[rows, h:], sems.at[1, n]),
-            pltpu.make_async_copy(down_hbm.at[cols], down_ref.at[cols], sems.at[2, n]),
-        ]
-    for copy in copies:
+    parts = sems.shape[0]
+    rows = d // parts
+    copies = [
+        pltpu.make_async_copy(
+            gate_hbm.at[pl.ds(n * rows, rows)], both_ref.at[pl.ds(n * rows, rows), pl.ds(0, h)], sems.at[n]
+        )
+        for n in range(parts)
+    ]
+    up = pltpu.make_async_copy(up_hbm, both_ref.at[:, pl.ds(h, h)], up_sem)
+    for copy in copies + [up]:
         copy.start()
-    for copy in copies:
+    for n, copy in enumerate(copies):
         copy.wait()
-
-
-def expert(*refs):
-    *blocks, both_ref, down_ref, mine_ref, other_ref, rows_ref = refs
-    d, h2 = both_ref.shape
-    h = h2 // 2
+        turned_ref[:, n * rows : (n + 1) * rows] = both_ref[n * rows : (n + 1) * rows, :h].T
+    up.wait()
+
+
+def turn(both_ref, after, turned_ref):
+    h, d = turned_ref.shape
+    step = d // 8
+    for n in range(0, d, step):
+        turned_ref[:, n : n + step] = both_ref[n : n + step, h:].T
+
+
+def arrange(*refs):
+    *blocks, normed_ref, grad_ref, rows_ref = refs
+    d = normed_ref.shape[1]
     r = blocks[0].shape[0]
     for k, ref in enumerate(blocks):
         rows_ref[k * r : (k + 1) * r] = ref[...].astype(jnp.float32)
-    normed = rows_ref[:, :d].astype(jnp.bfloat16)
-    grad = rows_ref[:, d:].astype(jnp.bfloat16)
-    both = jnp.dot(normed, both_ref[...], preferred_element_type=jnp.float32)
-    gate, up = both[:, :h], both[:, h:]
-    d_hidden = nt(grad, down_ref[...])
+    normed_ref[...] = rows_ref[:, :d].astype(jnp.bfloat16)
+    grad_ref[...] = rows_ref[:, d:].astype(jnp.bfloat16)
+
+
+def expert(normed_ref, hidden_ref, both_ref, gate_ref, up_ref, mine_ref, other_ref):
+    h = hidden_ref.shape[1]
+    gate = nn(normed_ref[...], both_ref[:, :h])
+    up = nn(normed_ref[...], both_ref[:, h:])
+    d_hidden = hidden_ref[...]
     p = jax.nn.sigmoid(gate)
     d_gate = d_hidden * up * p * (1.0 + gate * (1.0 - p))
     d_up = d_hidden * gate * p
     d_both = jnp.concatenate([d_gate, d_up], axis=1).astype(jnp.bfloat16)
-    total = nt(d_both, both_ref[...])
+    total = nn(d_both[:, :h], gate_ref[...]) + nn(d_both[:, h:], up_ref[...])
     half = total.shape[0] // 2
     mine_ref[...] = total[:half]
     other_ref[...] = total[half:]
@@ -139,7 +155,7 @@
     r, d = grad_in.shape[1:]
     f32, bf16 = jnp.float32, jnp.bfloat16
     shape = jax.ShapeDtypeStruct
-    served = [list(range(chips - 1 - c, -1, -CORES)) for c in range(CORES)]
+    served = [list(range(chips - CORES + c, -1, -CORES)) for c in range(CORES)]
     steps = [list(ks) for ks in zip(*served)][::-1]
 
     def near(i, ks):
@@ -189,29 +205,46 @@
 
     chip_rows = stacked([sent, to_core(sent)])
     hidden = w_down.shape[0]
-    weights = pl.pallas_call(
+    both, gate_turned = pl.pallas_call(
         fetch,
         out_shape=[VMEM((d, 2 * hidden), bf16), VMEM((hidden, d), bf16)],
-        in_specs=[pl.BlockSpec(memory_space=pl.ANY)] * 3,
-        out_specs=whole(2),
-        scratch_shapes=[pltpu.SemaphoreType.DMA((3, 1))],
-        compiler_params=params(4),
-        cost_estimate=pl.CostEstimate(flops=0, bytes_accessed=12 * d * hidden, transcendentals=0),
+        in_specs=[pl.BlockSpec(memory_space=pl.ANY)] * 2,
+        out_specs=whole(2),
+        scratch_shapes=[pltpu.SemaphoreType.DMA((4,)), pltpu.SemaphoreType.DMA],
+        compiler_params=params(4),
+        cost_estimate=pl.CostEstimate(flops=0, bytes_accessed=8 * d * hidden, transcendentals=0),
         name="fetch",
-    )(*[pltpu.with_memory_space_constraint(x, pltpu.HBM) for x in (w_gate, w_up, w_down)])
+    )(*[pltpu.with_memory_space_constraint(x, pltpu.HBM) for x in (w_gate, w_up)])
     blocks = [to_chip(chip_rows, ks) for ks in steps[::-1]][::-1]
-    block = stacked(blocks, weights)
+    block = stacked(blocks, [both])
     blocks = [block, to_core(block)]
     rows = block.shape[0]
+    up_turned = pl.pallas_call(
+        turn,
+        out_shape=VMEM((hidden, d), bf16),
+        in_specs=whole(1) + [pl.BlockSpec(memory_space=pl.ANY)],
+        out_specs=pl.BlockSpec(memory_space=VMEM),
+        compiler_params=params(4),
+        cost_estimate=pl.CostEstimate(flops=0, bytes_accessed=4 * d * hidden, transcendentals=0),
+        name="turn",
+    )(*near_core(both, block))
+    normed, grad = pl.pallas_call(
+        arrange,
+        out_shape=[VMEM((2 * rows, d), bf16)] * 2,
+        in_specs=whole(len(blocks)),
+        out_specs=whole(2),
+        scratch_shapes=[VMEM((2 * rows, 2 * d), f32)],
+        compiler_params=params(4),
+        name="arrange",
+    )(*near_core(*blocks))
     mine, other = pl.pallas_call(
         expert,
         out_shape=[VMEM((rows, d), f32)] * 2,
-        in_specs=whole(len(blocks) + 2),
-        out_specs=whole(2),
-        scratch_shapes=[VMEM((2 * rows, 2 * d), f32)],
+        in_specs=whole(5),
+        out_specs=whole(2),
         compiler_params=params(16),
         name="expert",
-    )(*near_core(*blocks, *weights))
+    )(*near_core(normed, nt(grad, w_down), both, gate_turned, up_turned))
     sums = pl.pallas_call(
         add_cores,
         out_shape=[VMEM((CORES * r, d), bf16)] * len(steps),

time: 30.5 us -> 28 us (0.918)
  waiting for transfers between devices: 8.42 us -> 5.38 us
  Pallas kernels: 9.17 us -> 7.73 us
  matrix products: 0 us -> 0.91 us
  starting transfers between devices: 12 us -> 12.9 us
    ppermute x4, starting transfers between devices: 0.83 us -> 3.91 us  [to_core(): return lax.ppermute(x, 'seqtp', [(i, i ^ 1) for i in range(members)])]
    ppermute x2, starting transfers between devices: 6.92 us -> 4.65 us  [to_chip(): return lax.ppermute(x, 'seqtp', [(i, near(i, ks)) for i in range(members)])]
    pallas_call x1, Pallas kernels: 3.4 us -> 1.76 us  [on_device(): pl.pallas_call(expert, out_shape=[VMEM((rows, d), f32)] * 2, in_specs=who...]
    ppermute x4, waiting for transfers between devices: 4.4 us -> 2.78 us  [to_core(): return lax.ppermute(x, 'seqtp', [(i, i ^ 1) for i in range(members)])]
    ppermute x3, waiting for transfers between devices: 3.59 us -> 2.19 us  [home(): return lax.ppermute(x, ('section', 'seqtp'), pairs)]
    pallas_call x0 -> x2, Pallas kernels: none -> 0.92 us  [the longest x1 0.9 us: on_device(): pl.pallas_call(turn, out_shape=VMEM((hidden, d), bf16), in_specs=whole(1)...]
    dot_general x0 -> x1, matrix products: none -> 0.91 us  [nt(): lax.dot_general(left, weight, (((1,), (1,)), ((), ())), preferred_element...]
    pallas_call x1, Pallas kernels: 3.79 us -> 2.91 us  [on_device(): pl.pallas_call(fetch, out_shape=[VMEM((d, 2 * hidden), bf16), VMEM((hidde...]
  transfers between devices with their start and end apart: 9 -> 9, of which waited for: 8 -> 7; matrix products, arithmetic and copies ran while one was open for 0% -> 0% of each run, Pallas kernels for 13% -> 14%
where the time goes in v3:
time: 28 us; the launch traced here: 27.8 us
  starting transfers between devices  12.9 us (46%)
  Pallas kernels  7.73 us (28%)
  waiting for transfers between devices  5.38 us (19%)
  matrix products  0.91 us (3%)
  between operations  0.87 us (3%)
    ppermute x2, starting transfers between devices, to_chip(): return lax.ppermute(x, 'seqtp', [(i, near(i, ks)) for i in range(members)])  4.65 us
    ppermute x3, starting transfers between devices, home(): return lax.ppermute(x, ('section', 'seqtp'), pairs)  4.34 us
    ppermute x4, starting transfers between devices, to_core(): return lax.ppermute(x, 'seqtp', [(i, i ^ 1) for i in range(members)])  3.91 us
    pallas_call x1, Pallas kernels, on_device(): pl.pallas_call(fetch, out_shape=[VMEM((d, 2 * hidden), bf16), VMEM((hidde...  2.91 us
    ppermute x4, waiting for transfers between devices, to_core(): return lax.ppermute(x, 'seqtp', [(i, i ^ 1) for i in range(members)])  2.78 us
    ppermute x3, waiting for transfers between devices, home(): return lax.ppermute(x, ('section', 'seqtp'), pairs)  2.19 us
    pallas_call x1, Pallas kernels, on_device(): pl.pallas_call(expert, out_shape=[VMEM((rows, d), f32)] * 2, in_specs=who...  1.76 us
    pallas_call x1, Pallas kernels, on_device(): pl.pallas_call(prepare, out_shape=[VMEM((r, 2 * d), bf16), VMEM((r, 2 * d...  1.18 us
  transfers between devices with their start and end apart: 9, of which 7 were waited for; matrix products, arithmetic and copies ran while one was open for 0% of the time, Pallas kernels for 14%

profile of v3, /device:TPU:0, one launch (start us, length us, event | category | flops | bytes accessed | tf_op | source)
XLA Modules:
  0.0 27.8 jit_solution(12337588562309809590)
XLA Ops:
  0.0 0.0 copy-start
  0.8 1.2 %prepare.1 = (bf16[2,8192]{1,0:T(2,128)(2,1)S(1)}, bf16[2,10240]{1,0:T(2,128)(2,1)S(1)}) custom-call(s32[1]{0:T(128)S(6)} %copy.8.slot_hbm, bf16[1,4,2,4096]{3,2,1,0:T(2,128)(2,1)} %saved_hbm.1, bf16[1,2,4096]{2,1,0:T(2,128)(2,1)} %grad_hbm.1, bf16[1,4096]{1,0:T(2,128)(2,1)} %gain_hbm.1), custom_call_target="tpu_custom_call" | custom-call | tf_op jit(solution)/shard_map/prepare/pallas_call | solution.py:180
  2.0 0.5 %collective-permute-start.1 = (bf16[2,8192]{1,0:T(2,128)(2,1)S(1)}, bf16[2,8192]{1,0:T(2,128)(2,1)S(1)}, u32[]{:S(2)}, u32[]{:S(2)}) collective-permute-start(bf16[2,8192]{1,0:T(2,128)(2,1)S(1)} %get-tuple-element.18.refs_0_), channel_id=1, source_target_pairs={{0,1},{1,0},{2,3},{3,2},{4,5},{5,4},{6,7},{7,6},{8,9},{9,8},{10,11... | collective-permute-start | bytes 98312 | tf_op jit(solution)/shard_map/ppermute | solution.py:170
  2.5 0.9 %collective-permute-done.1.refs_1_ = bf16[2,8192]{1,0:T(2,128)(2,1)S(1)} collective-permute-done((bf16[2,8192]{1,0:T(2,128)(2,1)S(1)}, bf16[2,8192]{1,0:T(2,128)(2,1)S(1)}, u32[]{:S(2)}, u32[]{:S(2)}) %collective-permute-start.1) | collective-permute-done | bytes 32800 | tf_op jit(solution)/shard_map/ppermute | solution.py:170
  3.4 4.0 %collective-permute-start.3 = (bf16[4,8192]{1,0:T(4,128)(2,1)S(1)}, bf16[4,8192]{1,0:T(4,128)(2,1)S(1)}, u32[]{:S(2)}, u32[]{:S(2)}) collective-permute-start(bf16[4,8192]{1,0:T(4,128)(2,1)S(1)} %stack.2), channel_id=1, source_target_pairs={{0,4},{1,7},{2,6},{3,5},{4,0},{5,3},{6,2},{7,1},{8,12},{9,15},{10,... | collective-permute-start | bytes 196616 | tf_op jit(solution)/shard_map/ppermute | solution.py:167
  7.4 0.7 %collective-permute-start.2 = (bf16[4,8192]{1,0:T(4,128)(2,1)S(1)}, bf16[4,8192]{1,0:T(4,128)(2,1)S(1)}, u32[]{:S(2)}, u32[]{:S(2)}) collective-permute-start(bf16[4,8192]{1,0:T(4,128)(2,1)S(1)} %stack.2), channel_id=1, source_target_pairs={{0,0},{1,3},{2,2},{3,1},{4,4},{5,7},{6,6},{7,5},{8,8},{9,11},{10,1... | collective-permute-start | bytes 196616 | tf_op jit(solution)/shard_map/ppermute | solution.py:167
  8.0 2.9 %fetch.1 = (bf16[4096,768]{1,0:T(8,128)(2,1)S(1)}, bf16[384,4096]{1,0:T(8,128)(2,1)S(1)}) custom-call(bf16[4096,384]{1,0:T(8,128)(2,1)} %gate_hbm.1, bf16[4096,384]{1,0:T(8,128)(2,1)} %up_hbm.1), custom_call_target="tpu_custom_call" | custom-call | bytes 12582912 | tf_op jit(solution)/shard_map/fetch/pallas_call | solution.py:208
  11.0 0.4 %collective-permute-done.3.refs_1_ = bf16[4,8192]{1,0:T(4,128)(2,1)S(1)} collective-permute-done((bf16[4,8192]{1,0:T(4,128)(2,1)S(1)}, bf16[4,8192]{1,0:T(4,128)(2,1)S(1)}, u32[]{:S(2)}, u32[]{:S(2)}) %collective-permute-start.3) | collective-permute-done | bytes 65568 | tf_op jit(solution)/shard_map/ppermute | solution.py:167
  11.4 0.0 collective-permute-done.2.refs_0_
  11.4 2.0 %collective-permute-start.4 = (bf16[8,8192]{1,0:T(8,128)(2,1)S(1)}, bf16[8,8192]{1,0:T(8,128)(2,1)S(1)}, u32[]{:S(2)}, u32[]{:S(2)}) collective-permute-start(bf16[8,8192]{1,0:T(8,128)(2,1)S(1)} %stack.3.refs_0_.after), channel_id=1, source_target_pairs={{0,1},{1,0},{2,3},{3,2},{4,5},{5,4},{6,7},{7,6},{8,9},{9,8},{10,11... | collective-permute-start | bytes 393224 | tf_op jit(solution)/shard_map/ppermute | solution.py:170
  13.4 0.9 %turn.1.up_ref = bf16[384,4096]{1,0:T(8,128)(2,1)S(1)} custom-call(bf16[4096,768]{1,0:T(8,128)(2,1)S(1)} %get-tuple-element.19.refs_2_.both_ref, bf16[8,8192]{1,0:T(8,128)(2,1)S(1)} %stack.3.refs_0_.after), custom_call_target="tpu_custom_call" | custom-call | bytes 6291456 | tf_op jit(solution)/shard_map/turn/pallas_call | solution.py:222
  14.3 0.1 collective-permute-done.4.refs_1_
  14.4 0.0 copy-done
  14.4 0.9 %fusion.hidden_ref = f32[16,384]{1,0:T(8,128)S(1)} fusion(bf16[16,4096]{1,0:T(8,128)(2,1)S(1)} %get-tuple-element.21, bf16[384,4096]{1,0:T(8,128)(2,1)S(1)} %copy-done), kind=kOutput, calls=%fused_computation | convolution fusion | flops 50331648 | bytes 3301376 | tf_op jit(solution)/shard_map/dot_general | solution.py:68
  15.3 1.8 %expert.1 = (f32[8,4096]{1,0:T(8,128)S(1)}, f32[8,4096]{1,0:T(8,128)S(1)}) custom-call(bf16[16,4096]{1,0:T(8,128)(2,1)S(1)} %get-tuple-element.20.normed_ref, f32[16,384]{1,0:T(8,128)S(1)} %fusion.hidden_ref, bf16[4096,768]{1,0:T(8,128)(2,1)S(1)} %get-tuple-element.19.refs_2_.both_ref, bf16[384,4096]{1,0:T(8,128)(2,1)S(1)} %get-tuple-element.22.gate_ref, ...), custom_call_target="tpu_custom_call" | custom-call | tf_op jit(solution)/shard_map/expert/pallas_call | solution.py:240
  17.1 0.4 %collective-permute-start.5 = (f32[8,4096]{1,0:T(8,128)S(1)}, f32[8,4096]{1,0:T(8,128)S(1)}, u32[]{:S(2)}, u32[]{:S(2)}) collective-permute-start(f32[8,4096]{1,0:T(8,128)S(1)} %get-tuple-element.24), channel_id=1, source_target_pairs={{0,1},{1,0},{2,3},{3,2},{4,5},{5,4},{6,7},{7,6},{8,9},{9,8},{10,11... | collective-permute-start | bytes 393224 | tf_op jit(solution)/shard_map/ppermute | solution.py:170
  17.4 1.0 %collective-permute-done.5.got_ref = f32[8,4096]{1,0:T(8,128)S(1)} collective-permute-done((f32[8,4096]{1,0:T(8,128)S(1)}, f32[8,4096]{1,0:T(8,128)S(1)}, u32[]{:S(2)}, u32[]{:S(2)}) %collective-permute-start.5) | collective-permute-done | bytes 131104 | tf_op jit(solution)/shard_map/ppermute | solution.py:170
  18.5 2.4 %collective-permute-start.6 = (bf16[4,4096]{1,0:T(4,128)(2,1)S(1)}, bf16[4,4096]{1,0:T(4,128)(2,1)S(1)}, u32[]{:S(2)}, u32[]{:S(2)}) collective-permute-start(bf16[4,4096]{1,0:T(4,128)(2,1)S(1)} %get-tuple-element.25), channel_id=1, source_target_pairs={{4,24},{7,25},{6,26},{5,27},{0,28},{3,29},{2,30},{1,31},{12,0},{15... | collective-permute-start | bytes 98312 | tf_op jit(solution)/shard_map/ppermute | solution.py:178
  20.8 0.5 %collective-permute-start.7 = (bf16[4,4096]{1,0:T(4,128)(2,1)S(1)}, bf16[4,4096]{1,0:T(4,128)(2,1)S(1)}, u32[]{:S(2)}, u32[]{:S(2)}) collective-permute-start(bf16[4,4096]{1,0:T(4,128)(2,1)S(1)} %get-tuple-element.26), channel_id=1, source_target_pairs={{0,24},{3,25},{2,26},{1,27},{4,28},{7,29},{6,30},{5,31},{8,0},{11,... | collective-permute-start | bytes 98312 | tf_op jit(solution)/shard_map/ppermute | solution.py:178
  21.4 1.4 %collective-permute-start = (bf16[2,10240]{1,0:T(2,128)(2,1)S(1)}, bf16[2,10240]{1,0:T(2,128)(2,1)S(1)}, u32[]{:S(2)}, u32[]{:S(2)}) collective-permute-start(bf16[2,10240]{1,0:T(2,128)(2,1)S(1)} %get-tuple-element.17), channel_id=1, source_target_pairs={{0,24},{1,25},{2,26},{3,27},{4,28},{5,29},{6,30},{7,31},{8,0},{9,1... | collective-permute-start | bytes 122888 | tf_op jit(solution)/shard_map/ppermute | solution.py:178
  22.8 1.4 %collective-permute-done.6.refs_0_ = bf16[4,4096]{1,0:T(4,128)(2,1)S(1)} collective-permute-done((bf16[4,4096]{1,0:T(4,128)(2,1)S(1)}, bf16[4,4096]{1,0:T(4,128)(2,1)S(1)}, u32[]{:S(2)}, u32[]{:S(2)}) %collective-permute-start.6) | collective-permute-done | bytes 32800 | tf_op jit(solution)/shard_map/ppermute | solution.py:178
  24.2 0.8 %collective-permute-done.7.refs_1_ = bf16[4,4096]{1,0:T(4,128)(2,1)S(1)} collective-permute-done((bf16[4,4096]{1,0:T(4,128)(2,1)S(1)}, bf16[4,4096]{1,0:T(4,128)(2,1)S(1)}, u32[]{:S(2)}, u32[]{:S(2)}) %collective-permute-start.7) | collective-permute-done | bytes 32800 | tf_op jit(solution)/shard_map/ppermute | solution.py:178
  25.0 1.1 %collective-permute-start.8 = (f32[2,4096]{1,0:T(2,128)S(1)}, f32[2,4096]{1,0:T(2,128)S(1)}, u32[]{:S(2)}, u32[]{:S(2)}) collective-permute-start(f32[2,4096]{1,0:T(2,128)S(1)} %get-tuple-element.28), channel_id=1, source_target_pairs={{0,1},{1,0},{2,3},{3,2},{4,5},{5,4},{6,7},{7,6},{8,9},{9,8},{10,11... | collective-permute-start | bytes 98312 | tf_op jit(solution)/shard_map/ppermute | solution.py:170
  26.1 0.0 collective-permute-done.own_ref
  26.1 0.9 %collective-permute-done.8.got_ref = f32[2,4096]{1,0:T(2,128)S(1)} collective-permute-done((f32[2,4096]{1,0:T(2,128)S(1)}, f32[2,4096]{1,0:T(2,128)S(1)}, u32[]{:S(2)}, u32[]{:S(2)}) %collective-permute-start.8) | collective-permute-done | bytes 32800 | tf_op jit(solution)/shard_map/ppermute | solution.py:170
  26.9 0.9 %finish.1 = bf16[1,2,4096]{2,1,0:T(2,128)(2,1)} custom-call(bf16[2,10240]{1,0:T(2,128)(2,1)S(1)} %collective-permute-done.own_ref, f32[2,4096]{1,0:T(2,128)S(1)} %get-tuple-element.27.keep_ref, f32[2,4096]{1,0:T(2,128)S(1)} %collective-permute-done.8.got_ref), custom_call_target="tpu_custom_call" | custom-call | tf_op jit(solution)/shard_map/finish/pallas_call | solution.py:266
  (5 shorter events, 0.1 us)
Async XLA Ops:
  0.0 14.4 %copy-start = (bf16[384,4096]{1,0:T(8,128)(2,1)S(1)}, bf16[384,4096]{1,0:T(8,128)(2,1)}, u32[]{:S(2)}) copy-start(bf16[384,4096]{1,0:T(8,128)(2,1)} %param.13) | copy-start | bytes 9437188
  2.0 1.4 %collective-permute-start.1 = (bf16[2,8192]{1,0:T(2,128)(2,1)S(1)}, bf16[2,8192]{1,0:T(2,128)(2,1)S(1)}, u32[]{:S(2)}, u32[]{:S(2)}) collective-permute-start(bf16[2,8192]{1,0:T(2,128)(2,1)S(1)} %get-tuple-element.18.refs_0_), channel_id=1, source_target_pairs={{0,1},{1,0},{2,3},{3,2},{4,5},{5,4},{6,7},{7,6},{8,9},{9,8},{10,11... | collective-permute-start | bytes 98312 | tf_op jit(solution)/shard_map/ppermute | solution.py:170
  3.4 8.0 %collective-permute-start.3 = (bf16[4,8192]{1,0:T(4,128)(2,1)S(1)}, bf16[4,8192]{1,0:T(4,128)(2,1)S(1)}, u32[]{:S(2)}, u32[]{:S(2)}) collective-permute-start(bf16[4,8192]{1,0:T(4,128)(2,1)S(1)} %stack.2), channel_id=1, source_target_pairs={{0,4},{1,7},{2,6},{3,5},{4,0},{5,3},{6,2},{7,1},{8,12},{9,15},{10,... | collective-permute-start | bytes 196616 | tf_op jit(solution)/shard_map/ppermute | solution.py:167
  7.4 4.0 %collective-permute-start.2 = (bf16[4,8192]{1,0:T(4,128)(2,1)S(1)}, bf16[4,8192]{1,0:T(4,128)(2,1)S(1)}, u32[]{:S(2)}, u32[]{:S(2)}) collective-permute-start(bf16[4,8192]{1,0:T(4,128)(2,1)S(1)} %stack.2), channel_id=1, source_target_pairs={{0,0},{1,3},{2,2},{3,1},{4,4},{5,7},{6,6},{7,5},{8,8},{9,11},{10,1... | collective-permute-start | bytes 196616 | tf_op jit(solution)/shard_map/ppermute | solution.py:167
  11.4 3.0 %collective-permute-start.4 = (bf16[8,8192]{1,0:T(8,128)(2,1)S(1)}, bf16[8,8192]{1,0:T(8,128)(2,1)S(1)}, u32[]{:S(2)}, u32[]{:S(2)}) collective-permute-start(bf16[8,8192]{1,0:T(8,128)(2,1)S(1)} %stack.3.refs_0_.after), channel_id=1, source_target_pairs={{0,1},{1,0},{2,3},{3,2},{4,5},{5,4},{6,7},{7,6},{8,9},{9,8},{10,11... | collective-permute-start | bytes 393224 | tf_op jit(solution)/shard_map/ppermute | solution.py:170
  17.1 1.4 %collective-permute-start.5 = (f32[8,4096]{1,0:T(8,128)S(1)}, f32[8,4096]{1,0:T(8,128)S(1)}, u32[]{:S(2)}, u32[]{:S(2)}) collective-permute-start(f32[8,4096]{1,0:T(8,128)S(1)} %get-tuple-element.24), channel_id=1, source_target_pairs={{0,1},{1,0},{2,3},{3,2},{4,5},{5,4},{6,7},{7,6},{8,9},{9,8},{10,11... | collective-permute-start | bytes 393224 | tf_op jit(solution)/shard_map/ppermute | solution.py:170
  18.5 5.8 %collective-permute-start.6 = (bf16[4,4096]{1,0:T(4,128)(2,1)S(1)}, bf16[4,4096]{1,0:T(4,128)(2,1)S(1)}, u32[]{:S(2)}, u32[]{:S(2)}) collective-permute-start(bf16[4,4096]{1,0:T(4,128)(2,1)S(1)} %get-tuple-element.25), channel_id=1, source_target_pairs={{4,24},{7,25},{6,26},{5,27},{0,28},{3,29},{2,30},{1,31},{12,0},{15... | collective-permute-start | bytes 98312 | tf_op jit(solution)/shard_map/ppermute | solution.py:178
  20.8 4.2 %collective-permute-start.7 = (bf16[4,4096]{1,0:T(4,128)(2,1)S(1)}, bf16[4,4096]{1,0:T(4,128)(2,1)S(1)}, u32[]{:S(2)}, u32[]{:S(2)}) collective-permute-start(bf16[4,4096]{1,0:T(4,128)(2,1)S(1)} %get-tuple-element.26), channel_id=1, source_target_pairs={{0,24},{3,25},{2,26},{1,27},{4,28},{7,29},{6,30},{5,31},{8,0},{11,... | collective-permute-start | bytes 98312 | tf_op jit(solution)/shard_map/ppermute | solution.py:178
  21.4 4.7 %collective-permute-start = (bf16[2,10240]{1,0:T(2,128)(2,1)S(1)}, bf16[2,10240]{1,0:T(2,128)(2,1)S(1)}, u32[]{:S(2)}, u32[]{:S(2)}) collective-permute-start(bf16[2,10240]{1,0:T(2,128)(2,1)S(1)} %get-tuple-element.17), channel_id=1, source_target_pairs={{0,24},{1,25},{2,26},{3,27},{4,28},{5,29},{6,30},{7,31},{8,0},{9,1... | collective-permute-start | bytes 122888 | tf_op jit(solution)/shard_map/ppermute | solution.py:178
  25.0 1.9 %collective-permute-start.8 = (f32[2,4096]{1,0:T(2,128)S(1)}, f32[2,4096]{1,0:T(2,128)S(1)}, u32[]{:S(2)}, u32[]{:S(2)}) collective-permute-start(f32[2,4096]{1,0:T(2,128)S(1)} %get-tuple-element.28), channel_id=1, source_target_pairs={{0,1},{1,0},{2,3},{3,2},{4,5},{5,4},{6,7},{7,6},{8,9},{9,8},{10,11... | collective-permute-start | bytes 98312 | tf_op jit(solution)/shard_map/ppermute | solution.py:170

commit v4 on v3

v4 whole, which is shorter than its diff:
```python
import functools

import jax
import jax.numpy as jnp
from jax import lax
from jax.experimental import pallas as pl
from jax.experimental.pallas import tpu as pltpu
from jax.sharding import PartitionSpec as P

EPS = 1e-05
CORES = 2
VMEM = pltpu.VMEM


def whole(n):
    return [pl.BlockSpec(memory_space=VMEM)] * n


def anywhere(n):
    return [pl.BlockSpec(memory_space=pl.ANY)] * n


def near_core(*arrays):
    return [pltpu.with_memory_space_constraint(x, VMEM) for x in arrays]


def far_off(*arrays):
    return [pltpu.with_memory_space_constraint(x, pltpu.HBM) for x in arrays]


def params(mib):
    return pltpu.CompilerParams(vmem_limit_bytes=mib * 2**20)


def cost(bytes_accessed):
    return pl.CostEstimate(flops=0, bytes_accessed=bytes_accessed, transcendentals=0)


def on_chip_with(bit):
    return lax.rem(lax.div(lax.axis_index("seqtp"), CORES * max(bit, 1)), 2) == 1


def crossed(blocks, swap):
    out = list(blocks)
    for n in range(0, len(blocks) - 1, 2):
        a, b = blocks[n : n + 2]
        out[n], out[n + 1] = jnp.where(swap, a, b), jnp.where(swap, b, a)
    return out


def on_first_core():
    return lax.rem(lax.axis_index("seqtp"), CORES) == 0


def nn(left, weight):
    return jnp.dot(left, weight, preferred_element_type=jnp.float32)


def nt(left, weight):
    return lax.dot_general(
        left, weight, (((1,), (1,)), ((), ())), preferred_element_type=jnp.float32
    )


def prepare(slot_ref, saved_hbm, grad_hbm, gain_hbm, sent_ref, own_ref, behind_ref, gain_ref, sems):
    r, d = grad_hbm.shape[1:]
    copies = [
        pltpu.make_async_copy(src, dst, sems.at[i])
        for i, (src, dst) in enumerate(
            (
                (saved_hbm.at[0, slot_ref[0]], behind_ref),
                (grad_hbm.at[0], sent_ref.at[:, pl.ds(d, d)]),
                (gain_hbm, gain_ref),
            )
        )
    ]
    for copy in copies:
        copy.start()
    for copy in copies:
        copy.wait()
    behind = behind_ref[...]
    wide = behind.astype(jnp.float32)
    recip = lax.rsqrt(jnp.mean(wide * wide, axis=-1, keepdims=True) + EPS)
    sent_ref[:, :d] = (wide * recip * gain_ref[...].astype(jnp.float32)).astype(jnp.bfloat16)
    own_ref[:, :d] = behind
    own_ref[:, d : 2 * d] = sent_ref[:, d:]
    piece = d // r
    for n in range(r):
        own_ref[n : n + 1, 2 * d :] = gain_ref[:, n * piece : (n + 1) * piece]


def join(mine_ref, other_ref, rows_ref):
    r = mine_ref.shape[0]
    mine, other = mine_ref[...], other_ref[...]
    first = on_first_core()
    rows_ref[:r] = jnp.where(first, mine, other)
    rows_ref[r:] = jnp.where(first, other, mine)


def fetch(gate_hbm, up_hbm, both_ref, turned_ref, sems, up_sem):
    d, h = gate_hbm.shape
    parts = sems.shape[0]
    rows = d // parts
    copies = [
        pltpu.make_async_copy(
            gate_hbm.at[pl.ds(n * rows, rows)], both_ref.at[pl.ds(n * rows, rows), pl.ds(0, h)], sems.at[n]
        )
        for n in range(parts)
    ]
    up = pltpu.make_async_copy(up_hbm, both_ref.at[:, pl.ds(h, h)], up_sem)
    for copy in copies + [up]:
        copy.start()
    for n, copy in enumerate(copies):
        copy.wait()
        turned_ref[:, n * rows : (n + 1) * rows] = both_ref[n * rows : (n + 1) * rows, :h].T
    up.wait()


def turn(both_ref, after, turned_ref):
    h, d = turned_ref.shape
    step = d // 8
    for n in range(0, d, step):
        turned_ref[:, n : n + step] = both_ref[n : n + step, h:].T


def collect(turns, own_ref, *refs):
    *blocks, after, out_ref = refs
    r = own_ref.shape[0]
    first, turned = on_first_core(), on_chip_with(turns)
    came = [ref[...] for ref in blocks[::-1]]
    nearer = [own_ref[...]] + came[:-1]
    farther = crossed(came, turned) if turns else came
    for n, (a, b) in enumerate(zip(nearer, farther)):
        out_ref[n * r : (n + 1) * r] = jnp.where(first, a, b)


def arrange(near_ref, far_ref, normed_ref, grad_ref, rows_ref):
    d = normed_ref.shape[1]
    half = near_ref.shape[0]
    first = on_first_core()
    near, far = near_ref[...].astype(jnp.float32), far_ref[...].astype(jnp.float32)
    rows_ref[:half] = jnp.where(first, near, far)
    rows_ref[half:] = jnp.where(first, far, near)
    normed_ref[...] = rows_ref[:, :d].astype(jnp.bfloat16)
    grad_ref[...] = rows_ref[:, d:].astype(jnp.bfloat16)


def expert(rows, normed_ref, hidden_ref, both_ref, gate_ref, up_ref, mine_ref, other_ref):
    h = hidden_ref.shape[1]
    gate = nn(normed_ref[...], both_ref[:, :h])
    up = nn(normed_ref[...], both_ref[:, h:])
    d_hidden = hidden_ref[...]
    p = jax.nn.sigmoid(gate)
    d_gate = d_hidden * up * p * (1.0 + gate * (1.0 - p))
    d_up = d_hidden * gate * p
    d_both = jnp.concatenate([d_gate, d_up], axis=1).astype(jnp.bfloat16)
    total = nn(d_both[:, :h], gate_ref[...]) + nn(d_both[:, h:], up_ref[...])
    first = on_first_core()
    for n in range(mine_ref.shape[0] // rows):
        even = total[2 * n * rows : (2 * n + 1) * rows]
        odd = total[(2 * n + 1) * rows : (2 * n + 2) * rows]
        mine_ref[n * rows : (n + 1) * rows] = jnp.where(first, even, odd)
        other_ref[n * rows : (n + 1) * rows] = jnp.where(first, odd, even)


def add_cores(turns, mine_ref, got_ref, *out_refs):
    total = (mine_ref[...] + got_ref[...]).astype(jnp.bfloat16)
    r = out_refs[0].shape[0]
    parts = [total[k * r : (k + 1) * r] for k in range(len(out_refs))]
    first = on_first_core()
    odd = crossed(parts, jnp.logical_not(on_chip_with(turns))) if turns else parts
    for ref, a, b in zip(out_refs, parts[::-1], odd):
        ref[...] = jnp.where(first, a, b)


def add_chips(*refs):
    *parts, keep_ref, send_ref = refs
    total = sum(ref[...].astype(jnp.float32) for ref in parts)
    r = keep_ref.shape[0]
    first = on_first_core()
    keep_ref[...] = jnp.where(first, total[:r], total[r:])
    send_ref[...] = jnp.where(first, total[r:], total[:r])


def finish(own_ref, keep_ref, got_ref, out_ref, gain_ref):
    r, d = keep_ref.shape
    piece = d // r
    for n in range(r):
        gain_ref[:, n * piece : (n + 1) * piece] = own_ref[n : n + 1, 2 * d :].astype(jnp.float32)
    wide = own_ref[:, :d].astype(jnp.float32)
    grad = own_ref[:, d : 2 * d].astype(jnp.float32)
    recip = lax.rsqrt(jnp.mean(wide * wide, axis=-1, keepdims=True) + EPS)
    scaled = gain_ref[...] * (keep_ref[...] + got_ref[...])
    unit = wide * recip
    mean = jnp.mean(scaled * unit, axis=-1, keepdims=True)
    out_ref[0] = (grad + recip * (scaled - unit * mean)).astype(out_ref.dtype)


def on_device(sections, members, saved_in, grad_in, slot_table, gain, w_gate, w_up, w_down):
    chips = members // CORES
    r, d = grad_in.shape[1:]
    hidden = w_down.shape[0]
    f32, bf16 = jnp.float32, jnp.bfloat16
    half = chips // CORES
    power = chips & (chips - 1) == 0
    out_turns, home_turns = (half, 1) if power else (0, 0)

    def swapped(n, t, bit, chip):
        return t ^ 1 if bit and chip & bit and t | 1 < n else t

    def route(goal):
        pairs = []
        for s in range(sections):
            for i in range(members):
                to, chip = goal(s, *divmod(i, CORES))
                pairs.append((s * members + i, to % sections * members + chip % chips * CORES + i % CORES))
        return pairs

    def ahead(x, t):
        def goal(s, chip, core):
            if core:
                k = half + swapped(half, t, out_turns, chip)
            else:
                k = (t + 1) % half
            return s + (k == 0), chip ^ k if power else chip + k

        return lax.ppermute(x, ("section", "seqtp"), route(goal))

    def home(x, t):
        def goal(s, chip, core):
            k = 2 * swapped(half, t, home_turns, chip) + 1 if core else 2 * (half - 1 - t)
            return s - 1, chip ^ k if power else chip - k

        return lax.ppermute(x, ("section", "seqtp"), route(goal))

    def back(x):
        return lax.ppermute(x, ("section", "seqtp"), route(lambda s, chip, core: (s - 1, chip)))

    def to_core(x):
        return lax.ppermute(x, "seqtp", [(i, i ^ 1) for i in range(members)])

    sent, own = pl.pallas_call(
        prepare,
        out_shape=[VMEM((r, 2 * d), bf16), VMEM((r, 2 * d + d // r), bf16)],
        in_specs=[pl.BlockSpec(memory_space=pltpu.SMEM)] + anywhere(3),
        out_specs=whole(2),
        scratch_shapes=[VMEM((r, d), bf16), VMEM(gain.shape, bf16), pltpu.SemaphoreType.DMA((3,))],
        compiler_params=params(4),
        name="prepare",
    )(slot_table, *far_off(saved_in, grad_in, gain))
    chip_rows = pl.pallas_call(
        join,
        out_shape=VMEM((CORES * r, 2 * d), bf16),
        in_specs=whole(2),
        out_specs=pl.BlockSpec(memory_space=VMEM),
        compiler_params=params(4),
        name="join",
    )(*near_core(sent, to_core(sent)))
    both, gate_turned = pl.pallas_call(
        fetch,
        out_shape=[VMEM((d, 2 * hidden), bf16), VMEM((hidden, d), bf16)],
        in_specs=anywhere(2),
        out_specs=whole(2),
        scratch_shapes=[pltpu.SemaphoreType.DMA((4,)), pltpu.SemaphoreType.DMA],
        compiler_params=params(4),
        cost_estimate=cost(8 * d * hidden),
        name="fetch",
    )(*far_off(w_gate, w_up))
    blocks = [ahead(chip_rows, t) for t in range(half)]
    rows = chips * r
    block = pl.pallas_call(
        functools.partial(collect, out_turns),
        out_shape=VMEM((rows, 2 * d), bf16),
        in_specs=whole(1 + len(blocks)) + anywhere(1),
        out_specs=pl.BlockSpec(memory_space=VMEM),
        compiler_params=params(4),
        name="collect",
    )(*near_core(chip_rows, *blocks[::-1], both))
    far = to_core(block)
    up_turned = pl.pallas_call(
        turn,
        out_shape=VMEM((hidden, d), bf16),
        in_specs=whole(1) + anywhere(1),
        out_specs=pl.BlockSpec(memory_space=VMEM),
        compiler_params=params(4),
        cost_estimate=cost(4 * d * hidden),
        name="turn",
    )(*near_core(both, block))
    normed, grad = pl.pallas_call(
        arrange,
        out_shape=[VMEM((2 * rows, d), bf16)] * 2,
        in_specs=whole(2),
        out_specs=whole(2),
        scratch_shapes=[VMEM((2 * rows, 2 * d), f32)],
        compiler_params=params(4),
        name="arrange",
    )(*near_core(block, far))
    mine, other = pl.pallas_call(
        functools.partial(expert, CORES * r),
        out_shape=[VMEM((rows, d), f32)] * 2,
        in_specs=whole(5),
        out_specs=whole(2),
        compiler_params=params(16),
        name="expert",
    )(*near_core(normed, nt(grad, w_down), both, gate_turned, up_turned))
    sums = pl.pallas_call(
        functools.partial(add_cores, home_turns),
        out_shape=[VMEM((CORES * r, d), bf16)] * half,
        in_specs=whole(2),
        out_specs=whole(half),
        compiler_params=params(4),
        name="add_cores",
    )(*near_core(mine, to_core(other)))
    landed = [home(x, t) for t, x in enumerate(sums)]
    own = back(own)
    keep, send = pl.pallas_call(
        add_chips,
        out_shape=[VMEM((r, d), f32)] * 2,
        in_specs=whole(half),
        out_specs=whole(2),
        compiler_params=params(4),
        name="add_chips",
    )(*near_core(*landed))
    return pl.pallas_call(
        finish,
        out_shape=jax.ShapeDtypeStruct((1, r, d), bf16),
        in_specs=whole(3),
        out_specs=pl.BlockSpec(memory_space=VMEM),
        scratch_shapes=[VMEM((1, d), f32)],
        compiler_params=params(4),
        name="finish",
    )(*near_core(own, keep, to_core(send)))


def solution(mesh):
    return jax.shard_map(
        functools.partial(on_device, mesh.shape["section"], mesh.shape["seqtp"]),
        mesh=mesh,
        in_specs=(
            P("section", None, "seqtp", None),
            P("section", "seqtp", None),
            P("section"),
            P("section", None),
            P(None, "seqtp"),
            P(None, "seqtp"),
            P("seqtp", None),
        ),
        out_specs=P("section", "seqtp", None),
        check_vma=False,
    )
```

time: 28 us -> 27.4 us (0.979)
  starting transfers between devices: 12.9 us -> 11.1 us
  waiting for transfers between devices: 5.38 us -> 6.41 us
    ppermute x4, starting transfers between devices: 3.91 us -> 0.87 us  [to_core(): return lax.ppermute(x, 'seqtp', [(i, i ^ 1) for i in range(members)])]
    ppermute x5, waiting for transfers between devices: 2.6 us -> 3.95 us  [the longest x2 1.92 us: home(): return lax.ppermute(x, ('section', 'seqtp'), route(goal))]
    ppermute x5, starting transfers between devices: 8.99 us -> 10.2 us  [the longest x2 5.06 us: home(): return lax.ppermute(x, ('section', 'seqtp'), route(goal))]
    ppermute x4, waiting for transfers between devices: 2.78 us -> 2.46 us  [to_core(): return lax.ppermute(x, 'seqtp', [(i, i ^ 1) for i in range(members)])]
where the time goes in v4:
time: 27.4 us; the launch traced here: 27 us
  starting transfers between devices  11.1 us (41%)
  Pallas kernels  7.74 us (28%)
  waiting for transfers between devices  6.41 us (23%)
  matrix products  0.91 us (3%)
  between operations  0.88 us (3%)
    ppermute x2, starting transfers between devices, home(): return lax.ppermute(x, ('section', 'seqtp'), route(goal))  5.06 us
    ppermute x2, starting transfers between devices, ahead(): return lax.ppermute(x, ('section', 'seqtp'), route(goal))  4.46 us
    pallas_call x1, Pallas kernels, on_device(): pl.pallas_call(fetch, out_shape=[VMEM((d, 2 * hidden), bf16), VMEM((hidde...  2.9 us
    ppermute x4, waiting for transfers between devices, to_core(): return lax.ppermute(x, 'seqtp', [(i, i ^ 1) for i in range(members)])  2.46 us
    ppermute x2, waiting for transfers between devices, home(): return lax.ppermute(x, ('section', 'seqtp'), route(goal))  1.92 us
    pallas_call x1, Pallas kernels, on_device(): pl.pallas_call(functools.partial(expert, CORES * r), out_shape=[VMEM((row...  1.76 us
    ppermute x1, waiting for transfers between devices, back(): lax.ppermute(x, ('section', 'seqtp'), route(lambda s, chip, core: (s - 1,...  1.28 us
    pallas_call x1, Pallas kernels, on_device(): pl.pallas_call(prepare, out_shape=[VMEM((r, 2 * d), bf16), VMEM((r, 2 * d...  1.07 us
  transfers between devices with their start and end apart: 9, of which 7 were waited for; matrix products, arithmetic and copies ran while one was open for 0% of the time, Pallas kernels for 14%

profile of v4, /device:TPU:0, one launch (start us, length us, event | category | flops | bytes accessed | tf_op | source)
XLA Modules:
  0.0 27.0 jit_solution(13973588004503210026)
XLA Ops:
  0.0 0.0 copy-start
  0.8 1.1 %prepare.1 = (bf16[2,8192]{1,0:T(2,128)(2,1)S(1)}, bf16[2,10240]{1,0:T(2,128)(2,1)S(1)}) custom-call(s32[1]{0:T(128)S(6)} %copy.8.slot_ref, bf16[1,4,2,4096]{3,2,1,0:T(2,128)(2,1)} %saved_hbm.1, bf16[1,2,4096]{2,1,0:T(2,128)(2,1)} %grad_hbm.1, bf16[1,4096]{1,0:T(2,128)(2,1)} %gain_hbm.1), custom_call_target="tpu_custom_call" | custom-call | tf_op jit(solution)/shard_map/prepare/pallas_call | solution.py:242
  1.9 0.5 %collective-permute-start.1 = (bf16[2,8192]{1,0:T(2,128)(2,1)S(1)}, bf16[2,8192]{1,0:T(2,128)(2,1)S(1)}, u32[]{:S(2)}, u32[]{:S(2)}) collective-permute-start(bf16[2,8192]{1,0:T(2,128)(2,1)S(1)} %get-tuple-element.18.mine_ref), channel_id=1, source_target_pairs={{0,1},{1,0},{2,3},{3,2},{4,5},{5,4},{6,7},{7,6},{8,9},{9,8},{10,11... | collective-permute-start | bytes 98312 | tf_op jit(solution)/shard_map/ppermute | solution.py:240
  2.4 0.9 %collective-permute-done.1.other_ref = bf16[2,8192]{1,0:T(2,128)(2,1)S(1)} collective-permute-done((bf16[2,8192]{1,0:T(2,128)(2,1)S(1)}, bf16[2,8192]{1,0:T(2,128)(2,1)S(1)}, u32[]{:S(2)}, u32[]{:S(2)}) %collective-permute-start.1) | collective-permute-done | bytes 32800 | tf_op jit(solution)/shard_map/ppermute | solution.py:240
  3.3 3.0 %collective-permute-start.3 = (bf16[4,8192]{1,0:T(4,128)(2,1)S(1)}, bf16[4,8192]{1,0:T(4,128)(2,1)S(1)}, u32[]{:S(2)}, u32[]{:S(2)}) collective-permute-start(bf16[4,8192]{1,0:T(4,128)(2,1)S(1)} %join.1.own_ref), channel_id=1, source_target_pairs={{0,2},{1,5},{2,0},{3,7},{4,6},{5,3},{6,4},{7,1},{8,10},{9,13},{10,... | collective-permute-start | bytes 196616 | tf_op jit(solution)/shard_map/ppermute | solution.py:227
  6.3 1.5 %collective-permute-start.2 = (bf16[4,8192]{1,0:T(4,128)(2,1)S(1)}, bf16[4,8192]{1,0:T(4,128)(2,1)S(1)}, u32[]{:S(2)}, u32[]{:S(2)}) collective-permute-start(bf16[4,8192]{1,0:T(4,128)(2,1)S(1)} %join.1.own_ref), channel_id=1, source_target_pairs={{0,8},{1,7},{2,10},{3,5},{4,12},{5,1},{6,14},{7,3},{8,16},{9,15},{... | collective-permute-start | bytes 196616 | tf_op jit(solution)/shard_map/ppermute | solution.py:227
  7.8 2.9 %fetch.1 = (bf16[4096,768]{1,0:T(8,128)(2,1)S(1)}, bf16[384,4096]{1,0:T(8,128)(2,1)S(1)}) custom-call(bf16[4096,384]{1,0:T(8,128)(2,1)} %gate_hbm.1, bf16[4096,384]{1,0:T(8,128)(2,1)} %up_hbm.1), custom_call_target="tpu_custom_call" | custom-call | bytes 12582912 | tf_op jit(solution)/shard_map/fetch/pallas_call | solution.py:259
  10.7 0.0 collective-permute-done.3.refs_1_
  10.7 0.8 %collective-permute-done.2.refs_0_ = bf16[4,8192]{1,0:T(4,128)(2,1)S(1)} collective-permute-done((bf16[4,8192]{1,0:T(4,128)(2,1)S(1)}, bf16[4,8192]{1,0:T(4,128)(2,1)S(1)}, u32[]{:S(2)}, u32[]{:S(2)}) %collective-permute-start.2) | collective-permute-done | bytes 65568 | tf_op jit(solution)/shard_map/ppermute | solution.py:227
  11.5 0.1 collective-permute-start.4
  11.6 0.9 %turn.1.up_ref = bf16[384,4096]{1,0:T(8,128)(2,1)S(1)} custom-call(bf16[4096,768]{1,0:T(8,128)(2,1)S(1)} %get-tuple-element.19.refs_2_.both_ref, bf16[8,8192]{1,0:T(8,128)(2,1)S(1)} %collect.1.near_ref.after), custom_call_target="tpu_custom_call" | custom-call | bytes 6291456 | tf_op jit(solution)/shard_map/turn/pallas_call | solution.py:280
  12.5 0.4 %collective-permute-done.4.far_ref = bf16[8,8192]{1,0:T(8,128)(2,1)S(1)} collective-permute-done((bf16[8,8192]{1,0:T(8,128)(2,1)S(1)}, bf16[8,8192]{1,0:T(8,128)(2,1)S(1)}, u32[]{:S(2)}, u32[]{:S(2)}) %collective-permute-start.4) | collective-permute-done | bytes 131104 | tf_op jit(solution)/shard_map/ppermute | solution.py:240
  12.9 0.1 arrange.1
  13.0 0.0 copy-done
  13.0 0.9 %fusion.hidden_ref = f32[16,384]{1,0:T(8,128)S(1)} fusion(bf16[16,4096]{1,0:T(8,128)(2,1)S(1)} %get-tuple-element.21, bf16[384,4096]{1,0:T(8,128)(2,1)S(1)} %copy-done), kind=kOutput, calls=%fused_computation | convolution fusion | flops 50331648 | bytes 3301376 | tf_op jit(solution)/shard_map/dot_general | solution.py:60
  13.9 1.8 %expert.1 = (f32[8,4096]{1,0:T(8,128)S(1)}, f32[8,4096]{1,0:T(8,128)S(1)}) custom-call(bf16[16,4096]{1,0:T(8,128)(2,1)S(1)} %get-tuple-element.20.normed_ref, f32[16,384]{1,0:T(8,128)S(1)} %fusion.hidden_ref, bf16[4096,768]{1,0:T(8,128)(2,1)S(1)} %get-tuple-element.19.refs_2_.both_ref, bf16[384,4096]{1,0:T(8,128)(2,1)S(1)} %get-tuple-element.22.gate_ref, ...), custom_call_target="tpu_custom_call" | custom-call | tf_op jit(solution)/shard_map/expert/pallas_call | solution.py:298
  15.7 0.2 collective-permute-start.5
  15.8 1.2 %collective-permute-done.5.got_ref = f32[8,4096]{1,0:T(8,128)S(1)} collective-permute-done((f32[8,4096]{1,0:T(8,128)S(1)}, f32[8,4096]{1,0:T(8,128)S(1)}, u32[]{:S(2)}, u32[]{:S(2)}) %collective-permute-start.5) | collective-permute-done | bytes 131104 | tf_op jit(solution)/shard_map/ppermute | solution.py:240
  17.0 0.1 add_cores.1
  17.1 3.8 %collective-permute-start.6 = (bf16[4,4096]{1,0:T(4,128)(2,1)S(1)}, bf16[4,4096]{1,0:T(4,128)(2,1)S(1)}, u32[]{:S(2)}, u32[]{:S(2)}) collective-permute-start(bf16[4,4096]{1,0:T(4,128)(2,1)S(1)} %get-tuple-element.25), channel_id=1, source_target_pairs={{0,28},{1,27},{2,30},{3,29},{4,24},{5,31},{6,26},{7,25},{8,4},{9,3... | collective-permute-start | bytes 98312 | tf_op jit(solution)/shard_map/ppermute | solution.py:234
  20.9 1.3 %collective-permute-start.7 = (bf16[4,4096]{1,0:T(4,128)(2,1)S(1)}, bf16[4,4096]{1,0:T(4,128)(2,1)S(1)}, u32[]{:S(2)}, u32[]{:S(2)}) collective-permute-start(bf16[4,4096]{1,0:T(4,128)(2,1)S(1)} %get-tuple-element.26), channel_id=1, source_target_pairs={{0,24},{1,31},{2,26},{3,25},{4,28},{5,27},{6,30},{7,29},{8,0},{9,7... | collective-permute-start | bytes 98312 | tf_op jit(solution)/shard_map/ppermute | solution.py:234
  22.2 0.7 %collective-permute-start = (bf16[2,10240]{1,0:T(2,128)(2,1)S(1)}, bf16[2,10240]{1,0:T(2,128)(2,1)S(1)}, u32[]{:S(2)}, u32[]{:S(2)}) collective-permute-start(bf16[2,10240]{1,0:T(2,128)(2,1)S(1)} %get-tuple-element.17), channel_id=1, source_target_pairs={{0,24},{1,25},{2,26},{3,27},{4,28},{5,29},{6,30},{7,31},{8,0},{9,1... | collective-permute-start | bytes 122888 | tf_op jit(solution)/shard_map/ppermute | solution.py:237
  22.9 0.7 %collective-permute-done.6.refs_0_ = bf16[4,4096]{1,0:T(4,128)(2,1)S(1)} collective-permute-done((bf16[4,4096]{1,0:T(4,128)(2,1)S(1)}, bf16[4,4096]{1,0:T(4,128)(2,1)S(1)}, u32[]{:S(2)}, u32[]{:S(2)}) %collective-permute-start.6) | collective-permute-done | bytes 32800 | tf_op jit(solution)/shard_map/ppermute | solution.py:234
  23.6 1.2 %collective-permute-done.7.refs_1_ = bf16[4,4096]{1,0:T(4,128)(2,1)S(1)} collective-permute-done((bf16[4,4096]{1,0:T(4,128)(2,1)S(1)}, bf16[4,4096]{1,0:T(4,128)(2,1)S(1)}, u32[]{:S(2)}, u32[]{:S(2)}) %collective-permute-start.7) | collective-permute-done | bytes 32800 | tf_op jit(solution)/shard_map/ppermute | solution.py:234
  24.8 0.1 collective-permute-start.8
  24.9 1.3 %collective-permute-done.own_ref = bf16[2,10240]{1,0:T(2,128)(2,1)S(1)} collective-permute-done((bf16[2,10240]{1,0:T(2,128)(2,1)S(1)}, bf16[2,10240]{1,0:T(2,128)(2,1)S(1)}, u32[]{:S(2)}, u32[]{:S(2)}) %collective-permute-start) | collective-permute-done | bytes 40992 | tf_op jit(solution)/shard_map/ppermute | solution.py:237
  26.2 0.0 collective-permute-done.8.got_ref
  26.2 0.9 %finish.1 = bf16[1,2,4096]{2,1,0:T(2,128)(2,1)} custom-call(bf16[2,10240]{1,0:T(2,128)(2,1)S(1)} %collective-permute-done.own_ref, f32[2,4096]{1,0:T(2,128)S(1)} %get-tuple-element.27.keep_ref, f32[2,4096]{1,0:T(2,128)S(1)} %collective-permute-done.8.got_ref), custom_call_target="tpu_custom_call" | custom-call | tf_op jit(solution)/shard_map/finish/pallas_call | solution.py:324
  (3 shorter events, 0.1 us)
Async XLA Ops:
  0.0 13.0 %copy-start = (bf16[384,4096]{1,0:T(8,128)(2,1)S(1)}, bf16[384,4096]{1,0:T(8,128)(2,1)}, u32[]{:S(2)}) copy-start(bf16[384,4096]{1,0:T(8,128)(2,1)} %param.13) | copy-start | bytes 9437188
  1.9 1.4 %collective-permute-start.1 = (bf16[2,8192]{1,0:T(2,128)(2,1)S(1)}, bf16[2,8192]{1,0:T(2,128)(2,1)S(1)}, u32[]{:S(2)}, u32[]{:S(2)}) collective-permute-start(bf16[2,8192]{1,0:T(2,128)(2,1)S(1)} %get-tuple-element.18.mine_ref), channel_id=1, source_target_pairs={{0,1},{1,0},{2,3},{3,2},{4,5},{5,4},{6,7},{7,6},{8,9},{9,8},{10,11... | collective-permute-start | bytes 98312 | tf_op jit(solution)/shard_map/ppermute | solution.py:240
  3.3 7.4 %collective-permute-start.3 = (bf16[4,8192]{1,0:T(4,128)(2,1)S(1)}, bf16[4,8192]{1,0:T(4,128)(2,1)S(1)}, u32[]{:S(2)}, u32[]{:S(2)}) collective-permute-start(bf16[4,8192]{1,0:T(4,128)(2,1)S(1)} %join.1.own_ref), channel_id=1, source_target_pairs={{0,2},{1,5},{2,0},{3,7},{4,6},{5,3},{6,4},{7,1},{8,10},{9,13},{10,... | collective-permute-start | bytes 196616 | tf_op jit(solution)/shard_map/ppermute | solution.py:227
  6.3 5.2 %collective-permute-start.2 = (bf16[4,8192]{1,0:T(4,128)(2,1)S(1)}, bf16[4,8192]{1,0:T(4,128)(2,1)S(1)}, u32[]{:S(2)}, u32[]{:S(2)}) collective-permute-start(bf16[4,8192]{1,0:T(4,128)(2,1)S(1)} %join.1.own_ref), channel_id=1, source_target_pairs={{0,8},{1,7},{2,10},{3,5},{4,12},{5,1},{6,14},{7,3},{8,16},{9,15},{... | collective-permute-start | bytes 196616 | tf_op jit(solution)/shard_map/ppermute | solution.py:227
  11.5 1.4 %collective-permute-start.4 = (bf16[8,8192]{1,0:T(8,128)(2,1)S(1)}, bf16[8,8192]{1,0:T(8,128)(2,1)S(1)}, u32[]{:S(2)}, u32[]{:S(2)}) collective-permute-start(bf16[8,8192]{1,0:T(8,128)(2,1)S(1)} %collect.1.near_ref.after), channel_id=1, source_target_pairs={{0,1},{1,0},{2,3},{3,2},{4,5},{5,4},{6,7},{7,6},{8,9},{9,8},{10,11... | collective-permute-start | bytes 393224 | tf_op jit(solution)/shard_map/ppermute | solution.py:240
  15.7 1.4 %collective-permute-start.5 = (f32[8,4096]{1,0:T(8,128)S(1)}, f32[8,4096]{1,0:T(8,128)S(1)}, u32[]{:S(2)}, u32[]{:S(2)}) collective-permute-start(f32[8,4096]{1,0:T(8,128)S(1)} %get-tuple-element.24), channel_id=1, source_target_pairs={{0,1},{1,0},{2,3},{3,2},{4,5},{5,4},{6,7},{7,6},{8,9},{9,8},{10,11... | collective-permute-start | bytes 393224 | tf_op jit(solution)/shard_map/ppermute | solution.py:240
  17.1 6.5 %collective-permute-start.6 = (bf16[4,4096]{1,0:T(4,128)(2,1)S(1)}, bf16[4,4096]{1,0:T(4,128)(2,1)S(1)}, u32[]{:S(2)}, u32[]{:S(2)}) collective-permute-start(bf16[4,4096]{1,0:T(4,128)(2,1)S(1)} %get-tuple-element.25), channel_id=1, source_target_pairs={{0,28},{1,27},{2,30},{3,29},{4,24},{5,31},{6,26},{7,25},{8,4},{9,3... | collective-permute-start | bytes 98312 | tf_op jit(solution)/shard_map/ppermute | solution.py:234
  20.9 3.9 %collective-permute-start.7 = (bf16[4,4096]{1,0:T(4,128)(2,1)S(1)}, bf16[4,4096]{1,0:T(4,128)(2,1)S(1)}, u32[]{:S(2)}, u32[]{:S(2)}) collective-permute-start(bf16[4,4096]{1,0:T(4,128)(2,1)S(1)} %get-tuple-element.26), channel_id=1, source_target_pairs={{0,24},{1,31},{2,26},{3,25},{4,28},{5,27},{6,30},{7,29},{8,0},{9,7... | collective-permute-start | bytes 98312 | tf_op jit(solution)/shard_map/ppermute | solution.py:234
  22.2 4.0 %collective-permute-start = (bf16[2,10240]{1,0:T(2,128)(2,1)S(1)}, bf16[2,10240]{1,0:T(2,128)(2,1)S(1)}, u32[]{:S(2)}, u32[]{:S(2)}) collective-permute-start(bf16[2,10240]{1,0:T(2,128)(2,1)S(1)} %get-tuple-element.17), channel_id=1, source_target_pairs={{0,24},{1,25},{2,26},{3,27},{4,28},{5,29},{6,30},{7,31},{8,0},{9,1... | collective-permute-start | bytes 122888 | tf_op jit(solution)/shard_map/ppermute | solution.py:237
  24.8 1.4 %collective-permute-start.8 = (f32[2,4096]{1,0:T(2,128)S(1)}, f32[2,4096]{1,0:T(2,128)S(1)}, u32[]{:S(2)}, u32[]{:S(2)}) collective-permute-start(f32[2,4096]{1,0:T(2,128)S(1)} %get-tuple-element.28), channel_id=1, source_target_pairs={{0,1},{1,0},{2,3},{3,2},{4,5},{5,4},{6,7},{7,6},{8,9},{9,8},{10,11... | collective-permute-start | bytes 98312 | tf_op jit(solution)/shard_map/ppermute | solution.py:240

commit v5 on v4

--- a/solution.py
+++ b/solution.py
@@ -62,39 +62,40 @@
     )
 
 
-def prepare(slot_ref, saved_hbm, grad_hbm, gain_hbm, sent_ref, own_ref, behind_ref, gain_ref, sems):
-    r, d = grad_hbm.shape[1:]
+def prepare(saved_hbm, grad_hbm, gain_hbm, sent_ref, raw_ref, gain_ref, sems):
+    slots, r, d = saved_hbm.shape[1:]
     copies = [
-        pltpu.make_async_copy(src, dst, sems.at[i])
-        for i, (src, dst) in enumerate(
-            (
-                (saved_hbm.at[0, slot_ref[0]], behind_ref),
-                (grad_hbm.at[0], sent_ref.at[:, pl.ds(d, d)]),
-                (gain_hbm, gain_ref),
-            )
-        )
+        pltpu.make_async_copy(saved_hbm.at[0, n], raw_ref.at[:, pl.ds(n * d, d)], sems.at[n]) for n in range(slots)
+    ]
+    copies += [
+        pltpu.make_async_copy(grad_hbm.at[0], sent_ref.at[:, pl.ds(slots * d, d)], sems.at[slots]),
+        pltpu.make_async_copy(gain_hbm, gain_ref, sems.at[slots + 1]),
     ]
     for copy in copies:
         copy.start()
     for copy in copies:
         copy.wait()
-    behind = behind_ref[...]
-    wide = behind.astype(jnp.float32)
-    recip = lax.rsqrt(jnp.mean(wide * wide, axis=-1, keepdims=True) + EPS)
-    sent_ref[:, :d] = (wide * recip * gain_ref[...].astype(jnp.float32)).astype(jnp.bfloat16)
-    own_ref[:, :d] = behind
-    own_ref[:, d : 2 * d] = sent_ref[:, d:]
+    gain = gain_ref[...].astype(jnp.float32)
+    for n in range(slots):
+        wide = raw_ref[:, n * d : (n + 1) * d].astype(jnp.float32)
+        recip = lax.rsqrt(jnp.mean(wide * wide, axis=-1, keepdims=True) + EPS)
+        sent_ref[:, n * d : (n + 1) * d] = (wide * recip * gain).astype(jnp.bfloat16)
+
+
+def join(slot_ref, mine_ref, other_ref, raw_ref, gain_ref, rows_ref, own_ref):
+    r, d = mine_ref.shape[0], gain_ref.shape[1]
+    first = on_first_core()
+    slot = pl.ds(pl.multiple_of(slot_ref[0] * d, d), d)
+    grad = pl.ds(mine_ref.shape[1] - d, d)
+    for part, at in ((slot, 0), (grad, d)):
+        mine, other = mine_ref[:, part], other_ref[:, part]
+        rows_ref[:r, at : at + d] = jnp.where(first, mine, other)
+        rows_ref[r:, at : at + d] = jnp.where(first, other, mine)
+    own_ref[:, :d] = raw_ref[:, slot]
+    own_ref[:, d : 2 * d] = mine_ref[:, grad]
     piece = d // r
     for n in range(r):
         own_ref[n : n + 1, 2 * d :] = gain_ref[:, n * piece : (n + 1) * piece]
-
-
-def join(mine_ref, other_ref, rows_ref):
-    r = mine_ref.shape[0]
-    mine, other = mine_ref[...], other_ref[...]
-    first = on_first_core()
-    rows_ref[:r] = jnp.where(first, mine, other)
-    rows_ref[r:] = jnp.where(first, other, mine)
 
 
 def fetch(gate_hbm, up_hbm, both_ref, turned_ref, sems, up_sem):
@@ -222,7 +223,8 @@
                 k = half + swapped(half, t, out_turns, chip)
             else:
                 k = (t + 1) % half
-            return s + (k == 0), chip ^ k if power else chip + k
+            aside = s if k else s ^ 1 if sections % 2 == 0 else s + 1
+            return aside, chip ^ k if power else chip + k
 
         return lax.ppermute(x, ("section", "seqtp"), route(goal))
 
@@ -239,23 +241,24 @@
     def to_core(x):
         return lax.ppermute(x, "seqtp", [(i, i ^ 1) for i in range(members)])
 
-    sent, own = pl.pallas_call(
+    slots = saved_in.shape[1]
+    sent, raw, gain_row = pl.pallas_call(
         prepare,
-        out_shape=[VMEM((r, 2 * d), bf16), VMEM((r, 2 * d + d // r), bf16)],
-        in_specs=[pl.BlockSpec(memory_space=pltpu.SMEM)] + anywhere(3),
-        out_specs=whole(2),
-        scratch_shapes=[VMEM((r, d), bf16), VMEM(gain.shape, bf16), pltpu.SemaphoreType.DMA((3,))],
+        out_shape=[VMEM((r, (slots + 1) * d), bf16), VMEM((r, slots * d), bf16), VMEM(gain.shape, bf16)],
+        in_specs=anywhere(3),
+        out_specs=whole(3),
+        scratch_shapes=[pltpu.SemaphoreType.DMA((slots + 2,))],
         compiler_params=params(4),
         name="prepare",
-    )(slot_table, *far_off(saved_in, grad_in, gain))
-    chip_rows = pl.pallas_call(
+    )(*far_off(saved_in, grad_in, gain))
+    chip_rows, own = pl.pallas_call(
         join,
-        out_shape=VMEM((CORES * r, 2 * d), bf16),
-        in_specs=whole(2),
-        out_specs=pl.BlockSpec(memory_space=VMEM),
+        out_shape=[VMEM((CORES * r, 2 * d), bf16), VMEM((r, 2 * d + d // r), bf16)],
+        in_specs=[pl.BlockSpec(memory_space=pltpu.SMEM)] + whole(4),
+        out_specs=whole(2),
         compiler_params=params(4),
         name="join",
-    )(*near_core(sent, to_core(sent)))
+    )(slot_table, *near_core(sent, to_core(sent), raw, gain_row))
     both, gate_turned = pl.pallas_call(
         fetch,
         out_shape=[VMEM((d, 2 * hidden), bf16), VMEM((hidden, d), bf16)],

time: 27.4 us -> 26.8 us (0.978)
  waiting for transfers between devices: 6.41 us -> 4.63 us
  starting transfers between devices: 11.1 us -> 12.3 us
    ppermute x2, waiting for transfers between devices: 0.76 us -> 0.01 us  [ahead(): return lax.ppermute(x, ('section', 'seqtp'), route(goal))]
    ppermute x1, starting transfers between devices: 0.7 us -> 1.4 us  [back(): lax.ppermute(x, ('section', 'seqtp'), route(lambda s, chip, core: (s - 1,...]
    ppermute x1, waiting for transfers between devices: 1.28 us -> 0.61 us  [back(): lax.ppermute(x, ('section', 'seqtp'), route(lambda s, chip, core: (s - 1,...]
    ppermute x4, starting transfers between devices: 0.87 us -> 1.53 us  [to_core(): return lax.ppermute(x, 'seqtp', [(i, i ^ 1) for i in range(members)])]
    ppermute x4, waiting for transfers between devices: 2.46 us -> 1.92 us  [to_core(): return lax.ppermute(x, 'seqtp', [(i, i ^ 1) for i in range(members)])]
  transfers between devices with their start and end apart: 9 -> 9, of which waited for: 7 -> 6; matrix products, arithmetic and copies ran while one was open for 0% -> 0% of each run, Pallas kernels for 14% -> 14%
where the time goes in v5:
time: 26.8 us; the launch traced here: 26.5 us
  starting transfers between devices  12.3 us (46%)
  Pallas kernels  7.88 us (29%)
  waiting for transfers between devices  4.63 us (17%)
  matrix products  0.91 us (3%)
  between operations  0.74 us (3%)
    ppermute x2, starting transfers between devices, home(): return lax.ppermute(x, ('section', 'seqtp'), route(goal))  4.94 us
    ppermute x2, starting transfers between devices, ahead(): return lax.ppermute(x, ('section', 'seqtp'), route(goal))  4.47 us
    pallas_call x1, Pallas kernels, on_device(): pl.pallas_call(fetch, out_shape=[VMEM((d, 2 * hidden), bf16), VMEM((hidde...  2.9 us
    ppermute x2, waiting for transfers between devices, home(): return lax.ppermute(x, ('section', 'seqtp'), route(goal))  2.1 us
    ppermute x4, waiting for transfers between devices, to_core(): return lax.ppermute(x, 'seqtp', [(i, i ^ 1) for i in range(members)])  1.92 us
    pallas_call x1, Pallas kernels, on_device(): pl.pallas_call(functools.partial(expert, CORES * r), out_shape=[VMEM((row...  1.76 us
    ppermute x4, starting transfers between devices, to_core(): return lax.ppermute(x, 'seqtp', [(i, i ^ 1) for i in range(members)])  1.53 us
    ppermute x1, starting transfers between devices, back(): lax.ppermute(x, ('section', 'seqtp'), route(lambda s, chip, core: (s - 1,...  1.4 us
  transfers between devices with their start and end apart: 9, of which 6 were waited for; matrix products, arithmetic and copies ran while one was open for 0% of the time, Pallas kernels for 14%

profile of v5, /device:TPU:0, one launch (start us, length us, event | category | flops | bytes accessed | tf_op | source)
XLA Modules:
  0.0 26.5 jit_solution(13902617116730779094)
XLA Ops:
  0.0 0.0 copy-start
  0.0 1.2 %prepare.1 = (bf16[2,20480]{1,0:T(2,128)(2,1)S(1)}, bf16[2,16384]{1,0:T(2,128)(2,1)S(1)}, bf16[1,4096]{1,0:T(2,128)(2,1)S(1)}) custom-call(bf16[1,4,2,4096]{3,2,1,0:T(2,128)(2,1)} %saved_hbm.1, bf16[1,2,4096]{2,1,0:T(2,128)(2,1)} %grad_hbm.1, bf16[1,4096]{1,0:T(2,128)(2,1)} %gain_hbm.1), custom_call_target="tpu_custom_call" | custom-call | tf_op jit(solution)/shard_map/prepare/pallas_call | solution.py:245
  1.2 0.5 %collective-permute-start = (bf16[2,20480]{1,0:T(2,128)(2,1)S(1)}, bf16[2,20480]{1,0:T(2,128)(2,1)S(1)}, u32[]{:S(2)}, u32[]{:S(2)}) collective-permute-start(bf16[2,20480]{1,0:T(2,128)(2,1)S(1)} %get-tuple-element.20.mine_ref), channel_id=1, source_target_pairs={{0,1},{1,0},{2,3},{3,2},{4,5},{5,4},{6,7},{7,6},{8,9},{9,8},{10,11... | collective-permute-start | bytes 245768 | tf_op jit(solution)/shard_map/ppermute | solution.py:242
  2.4 0.3 %collective-permute-done.other_ref = bf16[2,20480]{1,0:T(2,128)(2,1)S(1)} collective-permute-done((bf16[2,20480]{1,0:T(2,128)(2,1)S(1)}, bf16[2,20480]{1,0:T(2,128)(2,1)S(1)}, u32[]{:S(2)}, u32[]{:S(2)}) %collective-permute-start) | collective-permute-done | bytes 81952 | tf_op jit(solution)/shard_map/ppermute | solution.py:242
  2.7 3.0 %collective-permute-start.3 = (bf16[4,8192]{1,0:T(4,128)(2,1)S(1)}, bf16[4,8192]{1,0:T(4,128)(2,1)S(1)}, u32[]{:S(2)}, u32[]{:S(2)}) collective-permute-start(bf16[4,8192]{1,0:T(4,128)(2,1)S(1)} %get-tuple-element.24.own_ref), channel_id=1, source_target_pairs={{0,2},{1,5},{2,0},{3,7},{4,6},{5,3},{6,4},{7,1},{8,10},{9,13},{10,... | collective-permute-start | bytes 196616 | tf_op jit(solution)/shard_map/ppermute | solution.py:229
  5.7 1.5 %collective-permute-start.2 = (bf16[4,8192]{1,0:T(4,128)(2,1)S(1)}, bf16[4,8192]{1,0:T(4,128)(2,1)S(1)}, u32[]{:S(2)}, u32[]{:S(2)}) collective-permute-start(bf16[4,8192]{1,0:T(4,128)(2,1)S(1)} %get-tuple-element.24.own_ref), channel_id=1, source_target_pairs={{0,8},{1,7},{2,10},{3,5},{4,12},{5,1},{6,14},{7,3},{8,0},{9,15},{1... | collective-permute-start | bytes 196616 | tf_op jit(solution)/shard_map/ppermute | solution.py:229
  7.1 2.9 %fetch.1 = (bf16[4096,768]{1,0:T(8,128)(2,1)S(1)}, bf16[384,4096]{1,0:T(8,128)(2,1)S(1)}) custom-call(bf16[4096,384]{1,0:T(8,128)(2,1)} %gate_hbm.1, bf16[4096,384]{1,0:T(8,128)(2,1)} %up_hbm.1), custom_call_target="tpu_custom_call" | custom-call | bytes 12582912 | tf_op jit(solution)/shard_map/fetch/pallas_call | solution.py:262
  10.1 0.0 collective-permute-done.3.refs_1_
  10.1 0.0 collective-permute-done.2.refs_0_
  10.1 0.1 collect.1.near_ref.after
  10.1 0.5 %collective-permute-start.4 = (bf16[8,8192]{1,0:T(8,128)(2,1)S(1)}, bf16[8,8192]{1,0:T(8,128)(2,1)S(1)}, u32[]{:S(2)}, u32[]{:S(2)}) collective-permute-start(bf16[8,8192]{1,0:T(8,128)(2,1)S(1)} %collect.1.near_ref.after), channel_id=1, source_target_pairs={{0,1},{1,0},{2,3},{3,2},{4,5},{5,4},{6,7},{7,6},{8,9},{9,8},{10,11... | collective-permute-start | bytes 393224 | tf_op jit(solution)/shard_map/ppermute | solution.py:242
  10.7 0.9 %turn.1.up_ref = bf16[384,4096]{1,0:T(8,128)(2,1)S(1)} custom-call(bf16[4096,768]{1,0:T(8,128)(2,1)S(1)} %get-tuple-element.25.refs_2_.both_ref, bf16[8,8192]{1,0:T(8,128)(2,1)S(1)} %collect.1.near_ref.after), custom_call_target="tpu_custom_call" | custom-call | bytes 6291456 | tf_op jit(solution)/shard_map/turn/pallas_call | solution.py:283
  11.6 0.1 collective-permute-done.4.far_ref
  11.7 0.1 arrange.1
  11.7 0.0 copy-done
  11.8 0.9 %fusion.hidden_ref = f32[16,384]{1,0:T(8,128)S(1)} fusion(bf16[16,4096]{1,0:T(8,128)(2,1)S(1)} %get-tuple-element.27, bf16[384,4096]{1,0:T(8,128)(2,1)S(1)} %copy-done), kind=kOutput, calls=%fused_computation | convolution fusion | flops 50331648 | bytes 3301376 | tf_op jit(solution)/shard_map/dot_general | solution.py:60
  12.7 1.8 %expert.1 = (f32[8,4096]{1,0:T(8,128)S(1)}, f32[8,4096]{1,0:T(8,128)S(1)}) custom-call(bf16[16,4096]{1,0:T(8,128)(2,1)S(1)} %get-tuple-element.26.normed_ref, f32[16,384]{1,0:T(8,128)S(1)} %fusion.hidden_ref, bf16[4096,768]{1,0:T(8,128)(2,1)S(1)} %get-tuple-element.25.refs_2_.both_ref, bf16[384,4096]{1,0:T(8,128)(2,1)S(1)} %get-tuple-element.28.gate_ref, ...), custom_call_target="tpu_custom_call" | custom-call | tf_op jit(solution)/shard_map/expert/pallas_call | solution.py:301
  14.4 0.4 %collective-permute-start.5 = (f32[8,4096]{1,0:T(8,128)S(1)}, f32[8,4096]{1,0:T(8,128)S(1)}, u32[]{:S(2)}, u32[]{:S(2)}) collective-permute-start(f32[8,4096]{1,0:T(8,128)S(1)} %get-tuple-element.30), channel_id=1, source_target_pairs={{0,1},{1,0},{2,3},{3,2},{4,5},{5,4},{6,7},{7,6},{8,9},{9,8},{10,11... | collective-permute-start | bytes 393224 | tf_op jit(solution)/shard_map/ppermute | solution.py:242
  14.8 1.0 %collective-permute-done.5.got_ref = f32[8,4096]{1,0:T(8,128)S(1)} collective-permute-done((f32[8,4096]{1,0:T(8,128)S(1)}, f32[8,4096]{1,0:T(8,128)S(1)}, u32[]{:S(2)}, u32[]{:S(2)}) %collective-permute-start.5) | collective-permute-done | bytes 131104 | tf_op jit(solution)/shard_map/ppermute | solution.py:242
  15.8 0.1 add_cores.1
  15.9 4.4 %collective-permute-start.6 = (bf16[4,4096]{1,0:T(4,128)(2,1)S(1)}, bf16[4,4096]{1,0:T(4,128)(2,1)S(1)}, u32[]{:S(2)}, u32[]{:S(2)}) collective-permute-start(bf16[4,4096]{1,0:T(4,128)(2,1)S(1)} %get-tuple-element.31), channel_id=1, source_target_pairs={{0,28},{1,27},{2,30},{3,29},{4,24},{5,31},{6,26},{7,25},{8,4},{9,3... | collective-permute-start | bytes 98312 | tf_op jit(solution)/shard_map/ppermute | solution.py:236
  20.2 0.6 %collective-permute-start.7 = (bf16[4,4096]{1,0:T(4,128)(2,1)S(1)}, bf16[4,4096]{1,0:T(4,128)(2,1)S(1)}, u32[]{:S(2)}, u32[]{:S(2)}) collective-permute-start(bf16[4,4096]{1,0:T(4,128)(2,1)S(1)} %get-tuple-element.32), channel_id=1, source_target_pairs={{0,24},{1,31},{2,26},{3,25},{4,28},{5,27},{6,30},{7,29},{8,0},{9,7... | collective-permute-start | bytes 98312 | tf_op jit(solution)/shard_map/ppermute | solution.py:236
  20.8 1.4 %collective-permute-start.1 = (bf16[2,10240]{1,0:T(2,128)(2,1)S(1)}, bf16[2,10240]{1,0:T(2,128)(2,1)S(1)}, u32[]{:S(2)}, u32[]{:S(2)}) collective-permute-start(bf16[2,10240]{1,0:T(2,128)(2,1)S(1)} %get-tuple-element.23), channel_id=1, source_target_pairs={{0,24},{1,25},{2,26},{3,27},{4,28},{5,29},{6,30},{7,31},{8,0},{9,1... | collective-permute-start | bytes 122888 | tf_op jit(solution)/shard_map/ppermute | solution.py:239
  22.2 0.0 collective-permute-done.6.refs_0_
  22.2 2.1 %collective-permute-done.7.refs_1_ = bf16[4,4096]{1,0:T(4,128)(2,1)S(1)} collective-permute-done((bf16[4,4096]{1,0:T(4,128)(2,1)S(1)}, bf16[4,4096]{1,0:T(4,128)(2,1)S(1)}, u32[]{:S(2)}, u32[]{:S(2)}) %collective-permute-start.7) | collective-permute-done | bytes 32800 | tf_op jit(solution)/shard_map/ppermute | solution.py:236
  24.4 0.1 collective-permute-start.8
  24.4 0.6 %collective-permute-done.1.own_ref = bf16[2,10240]{1,0:T(2,128)(2,1)S(1)} collective-permute-done((bf16[2,10240]{1,0:T(2,128)(2,1)S(1)}, bf16[2,10240]{1,0:T(2,128)(2,1)S(1)}, u32[]{:S(2)}, u32[]{:S(2)}) %collective-permute-start.1) | collective-permute-done | bytes 40992 | tf_op jit(solution)/shard_map/ppermute | solution.py:239
  25.0 0.6 %collective-permute-done.8.got_ref = f32[2,4096]{1,0:T(2,128)S(1)} collective-permute-done((f32[2,4096]{1,0:T(2,128)S(1)}, f32[2,4096]{1,0:T(2,128)S(1)}, u32[]{:S(2)}, u32[]{:S(2)}) %collective-permute-start.8) | collective-permute-done | bytes 32800 | tf_op jit(solution)/shard_map/ppermute | solution.py:242
  25.6 0.9 %finish.1 = bf16[1,2,4096]{2,1,0:T(2,128)(2,1)} custom-call(bf16[2,10240]{1,0:T(2,128)(2,1)S(1)} %collective-permute-done.1.own_ref, f32[2,4096]{1,0:T(2,128)S(1)} %get-tuple-element.33.keep_ref, f32[2,4096]{1,0:T(2,128)S(1)} %collective-permute-done.8.got_ref), custom_call_target="tpu_custom_call" | custom-call | tf_op jit(solution)/shard_map/finish/pallas_call | solution.py:327
  (2 shorter events, 0.1 us)
Async XLA Ops:
  0.0 11.7 %copy-start = (bf16[384,4096]{1,0:T(8,128)(2,1)S(1)}, bf16[384,4096]{1,0:T(8,128)(2,1)}, u32[]{:S(2)}) copy-start(bf16[384,4096]{1,0:T(8,128)(2,1)} %param.13) | copy-start | bytes 9437188
  1.2 1.4 %collective-permute-start = (bf16[2,20480]{1,0:T(2,128)(2,1)S(1)}, bf16[2,20480]{1,0:T(2,128)(2,1)S(1)}, u32[]{:S(2)}, u32[]{:S(2)}) collective-permute-start(bf16[2,20480]{1,0:T(2,128)(2,1)S(1)} %get-tuple-element.20.mine_ref), channel_id=1, source_target_pairs={{0,1},{1,0},{2,3},{3,2},{4,5},{5,4},{6,7},{7,6},{8,9},{9,8},{10,11... | collective-permute-start | bytes 245768 | tf_op jit(solution)/shard_map/ppermute | solution.py:242
  2.7 7.4 %collective-permute-start.3 = (bf16[4,8192]{1,0:T(4,128)(2,1)S(1)}, bf16[4,8192]{1,0:T(4,128)(2,1)S(1)}, u32[]{:S(2)}, u32[]{:S(2)}) collective-permute-start(bf16[4,8192]{1,0:T(4,128)(2,1)S(1)} %get-tuple-element.24.own_ref), channel_id=1, source_target_pairs={{0,2},{1,5},{2,0},{3,7},{4,6},{5,3},{6,4},{7,1},{8,10},{9,13},{10,... | collective-permute-start | bytes 196616 | tf_op jit(solution)/shard_map/ppermute | solution.py:229
  5.7 4.4 %collective-permute-start.2 = (bf16[4,8192]{1,0:T(4,128)(2,1)S(1)}, bf16[4,8192]{1,0:T(4,128)(2,1)S(1)}, u32[]{:S(2)}, u32[]{:S(2)}) collective-permute-start(bf16[4,8192]{1,0:T(4,128)(2,1)S(1)} %get-tuple-element.24.own_ref), channel_id=1, source_target_pairs={{0,8},{1,7},{2,10},{3,5},{4,12},{5,1},{6,14},{7,3},{8,0},{9,15},{1... | collective-permute-start | bytes 196616 | tf_op jit(solution)/shard_map/ppermute | solution.py:229
  10.1 1.5 %collective-permute-start.4 = (bf16[8,8192]{1,0:T(8,128)(2,1)S(1)}, bf16[8,8192]{1,0:T(8,128)(2,1)S(1)}, u32[]{:S(2)}, u32[]{:S(2)}) collective-permute-start(bf16[8,8192]{1,0:T(8,128)(2,1)S(1)} %collect.1.near_ref.after), channel_id=1, source_target_pairs={{0,1},{1,0},{2,3},{3,2},{4,5},{5,4},{6,7},{7,6},{8,9},{9,8},{10,11... | collective-permute-start | bytes 393224 | tf_op jit(solution)/shard_map/ppermute | solution.py:242
  14.4 1.4 %collective-permute-start.5 = (f32[8,4096]{1,0:T(8,128)S(1)}, f32[8,4096]{1,0:T(8,128)S(1)}, u32[]{:S(2)}, u32[]{:S(2)}) collective-permute-start(f32[8,4096]{1,0:T(8,128)S(1)} %get-tuple-element.30), channel_id=1, source_target_pairs={{0,1},{1,0},{2,3},{3,2},{4,5},{5,4},{6,7},{7,6},{8,9},{9,8},{10,11... | collective-permute-start | bytes 393224 | tf_op jit(solution)/shard_map/ppermute | solution.py:242
  15.9 6.3 %collective-permute-start.6 = (bf16[4,4096]{1,0:T(4,128)(2,1)S(1)}, bf16[4,4096]{1,0:T(4,128)(2,1)S(1)}, u32[]{:S(2)}, u32[]{:S(2)}) collective-permute-start(bf16[4,4096]{1,0:T(4,128)(2,1)S(1)} %get-tuple-element.31), channel_id=1, source_target_pairs={{0,28},{1,27},{2,30},{3,29},{4,24},{5,31},{6,26},{7,25},{8,4},{9,3... | collective-permute-start | bytes 98312 | tf_op jit(solution)/shard_map/ppermute | solution.py:236
  20.2 4.1 %collective-permute-start.7 = (bf16[4,4096]{1,0:T(4,128)(2,1)S(1)}, bf16[4,4096]{1,0:T(4,128)(2,1)S(1)}, u32[]{:S(2)}, u32[]{:S(2)}) collective-permute-start(bf16[4,4096]{1,0:T(4,128)(2,1)S(1)} %get-tuple-element.32), channel_id=1, source_target_pairs={{0,24},{1,31},{2,26},{3,25},{4,28},{5,27},{6,30},{7,29},{8,0},{9,7... | collective-permute-start | bytes 98312 | tf_op jit(solution)/shard_map/ppermute | solution.py:236
  20.8 4.2 %collective-permute-start.1 = (bf16[2,10240]{1,0:T(2,128)(2,1)S(1)}, bf16[2,10240]{1,0:T(2,128)(2,1)S(1)}, u32[]{:S(2)}, u32[]{:S(2)}) collective-permute-start(bf16[2,10240]{1,0:T(2,128)(2,1)S(1)} %get-tuple-element.23), channel_id=1, source_target_pairs={{0,24},{1,25},{2,26},{3,27},{4,28},{5,29},{6,30},{7,31},{8,0},{9,1... | collective-permute-start | bytes 122888 | tf_op jit(solution)/shard_map/ppermute | solution.py:239
  24.4 1.3 %collective-permute-start.8 = (f32[2,4096]{1,0:T(2,128)S(1)}, f32[2,4096]{1,0:T(2,128)S(1)}, u32[]{:S(2)}, u32[]{:S(2)}) collective-permute-start(f32[2,4096]{1,0:T(2,128)S(1)} %get-tuple-element.34), channel_id=1, source_target_pairs={{0,1},{1,0},{2,3},{3,2},{4,5},{5,4},{6,7},{7,6},{8,9},{9,8},{10,11... | collective-permute-start | bytes 98312 | tf_op jit(solution)/shard_map/ppermute | solution.py:242

commit v6 on v5

--- a/solution.py
+++ b/solution.py
@@ -62,10 +62,10 @@
     )
 
 
-def prepare(saved_hbm, grad_hbm, gain_hbm, sent_ref, raw_ref, gain_ref, sems):
+def prepare(saved_hbm, grad_hbm, gain_hbm, sent_ref, gain_ref, sems):
     slots, r, d = saved_hbm.shape[1:]
     copies = [
-        pltpu.make_async_copy(saved_hbm.at[0, n], raw_ref.at[:, pl.ds(n * d, d)], sems.at[n]) for n in range(slots)
+        pltpu.make_async_copy(saved_hbm.at[0, n], sent_ref.at[:, pl.ds(n * d, d)], sems.at[n]) for n in range(slots)
     ]
     copies += [
         pltpu.make_async_copy(grad_hbm.at[0], sent_ref.at[:, pl.ds(slots * d, d)], sems.at[slots]),
@@ -75,14 +75,9 @@
         copy.start()
     for copy in copies:
         copy.wait()
-    gain = gain_ref[...].astype(jnp.float32)
-    for n in range(slots):
-        wide = raw_ref[:, n * d : (n + 1) * d].astype(jnp.float32)
-        recip = lax.rsqrt(jnp.mean(wide * wide, axis=-1, keepdims=True) + EPS)
-        sent_ref[:, n * d : (n + 1) * d] = (wide * recip * gain).astype(jnp.bfloat16)
-
-
-def join(slot_ref, mine_ref, other_ref, raw_ref, gain_ref, rows_ref, own_ref):
+
+
+def join(slot_ref, mine_ref, other_ref, gain_ref, rows_ref):
     r, d = mine_ref.shape[0], gain_ref.shape[1]
     first = on_first_core()
     slot = pl.ds(pl.multiple_of(slot_ref[0] * d, d), d)
@@ -91,11 +86,9 @@
         mine, other = mine_ref[:, part], other_ref[:, part]
         rows_ref[:r, at : at + d] = jnp.where(first, mine, other)
         rows_ref[r:, at : at + d] = jnp.where(first, other, mine)
-    own_ref[:, :d] = raw_ref[:, slot]
-    own_ref[:, d : 2 * d] = mine_ref[:, grad]
-    piece = d // r
-    for n in range(r):
-        own_ref[n : n + 1, 2 * d :] = gain_ref[:, n * piece : (n + 1) * piece]
+    piece = rows_ref.shape[1] - 2 * d
+    for n in range(rows_ref.shape[0]):
+        rows_ref[n : n + 1, 2 * d :] = gain_ref[:, n * piece : (n + 1) * piece]
 
 
 def fetch(gate_hbm, up_hbm, both_ref, turned_ref, sems, up_sem):
@@ -124,26 +117,36 @@
         turned_ref[:, n : n + step] = both_ref[n : n + step, h:].T
 
 
-def collect(turns, own_ref, *refs):
-    *blocks, after, out_ref = refs
-    r = own_ref.shape[0]
+def collect(turns, *refs):
+    *blocks, after, out_ref, gain_ref = refs
+    r = blocks[0].shape[0]
     first, turned = on_first_core(), on_chip_with(turns)
-    came = [ref[...] for ref in blocks[::-1]]
-    nearer = [own_ref[...]] + came[:-1]
+    came = [ref[:, : out_ref.shape[1]] for ref in blocks]
+    nearer = came[-1:] + came[:-1]
     farther = crossed(came, turned) if turns else came
     for n, (a, b) in enumerate(zip(nearer, farther)):
         out_ref[n * r : (n + 1) * r] = jnp.where(first, a, b)
-
-
-def arrange(near_ref, far_ref, normed_ref, grad_ref, rows_ref):
+    width = out_ref.shape[1]
+    piece = blocks[0].shape[1] - width
+    for n in range(r):
+        gain_ref[:, n * piece : (n + 1) * piece] = blocks[0][n : n + 1, width:].astype(jnp.float32)
+
+
+def arrange(near_ref, far_ref, gain_ref, normed_ref, grad_ref, own_ref, rows_ref):
     d = normed_ref.shape[1]
-    half = near_ref.shape[0]
+    half, r = near_ref.shape[0], own_ref.shape[0]
     first = on_first_core()
     near, far = near_ref[...].astype(jnp.float32), far_ref[...].astype(jnp.float32)
     rows_ref[:half] = jnp.where(first, near, far)
     rows_ref[half:] = jnp.where(first, far, near)
-    normed_ref[...] = rows_ref[:, :d].astype(jnp.bfloat16)
     grad_ref[...] = rows_ref[:, d:].astype(jnp.bfloat16)
+    wide = rows_ref[:, :d]
+    recip = lax.rsqrt(jnp.mean(wide * wide, axis=-1, keepdims=True) + EPS)
+    normed_ref[...] = (wide * recip * gain_ref[...]).astype(jnp.bfloat16)
+    own_ref[:, : 2 * d] = jnp.where(first, rows_ref[:r], rows_ref[r : 2 * r]).astype(jnp.bfloat16)
+    piece = d // r
+    for n in range(r):
+        own_ref[n : n + 1, 2 * d :] = gain_ref[:, n * piece : (n + 1) * piece].astype(jnp.bfloat16)
 
 
 def expert(rows, normed_ref, hidden_ref, both_ref, gate_ref, up_ref, mine_ref, other_ref):
@@ -174,22 +177,26 @@
         ref[...] = jnp.where(first, a, b)
 
 
-def add_chips(*refs):
+def add_chips(stays, local_ref, *refs):
     *parts, keep_ref, send_ref = refs
-    total = sum(ref[...].astype(jnp.float32) for ref in parts)
+    first = on_first_core()
+    stayed = jnp.logical_and(first, stays(lax.axis_index("section")))
+    total = jnp.where(stayed, local_ref[...], parts[-1][...]).astype(jnp.float32)
+    for ref in parts[:-1]:
+        total = total + ref[...].astype(jnp.float32)
     r = keep_ref.shape[0]
-    first = on_first_core()
     keep_ref[...] = jnp.where(first, total[:r], total[r:])
     send_ref[...] = jnp.where(first, total[r:], total[:r])
 
 
-def finish(own_ref, keep_ref, got_ref, out_ref, gain_ref):
+def finish(stays, stayed_ref, moved_ref, keep_ref, got_ref, out_ref, gain_ref):
     r, d = keep_ref.shape
+    here = stays(lax.axis_index("section"))
+    own = jnp.where(here, stayed_ref[...].astype(jnp.float32), moved_ref[...].astype(jnp.float32))
     piece = d // r
     for n in range(r):
-        gain_ref[:, n * piece : (n + 1) * piece] = own_ref[n : n + 1, 2 * d :].astype(jnp.float32)
-    wide = own_ref[:, :d].astype(jnp.float32)
-    grad = own_ref[:, d : 2 * d].astype(jnp.float32)
+        gain_ref[:, n * piece : (n + 1) * piece] = own[n : n + 1, 2 * d :]
+    wide, grad = own[:, :d], own[:, d : 2 * d]
     recip = lax.rsqrt(jnp.mean(wide * wide, axis=-1, keepdims=True) + EPS)
     scaled = gain_ref[...] * (keep_ref[...] + got_ref[...])
     unit = wide * recip
@@ -217,48 +224,56 @@
                 pairs.append((s * members + i, to % sections * members + chip % chips * CORES + i % CORES))
         return pairs
 
+    even = sections % 2 == 0
+
+    def beside(s):
+        return s ^ 1 if even else s - 1
+
+    def before(s):
+        return s - 2 * (s % 2) if even else s
+
+    def stays(section):
+        return lax.rem(section, 2) == 0 if even else section >= 0
+
     def ahead(x, t):
         def goal(s, chip, core):
-            if core:
-                k = half + swapped(half, t, out_turns, chip)
-            else:
-                k = (t + 1) % half
-            aside = s if k else s ^ 1 if sections % 2 == 0 else s + 1
-            return aside, chip ^ k if power else chip + k
+            k = half + swapped(half, t, out_turns, chip) if core else (t + 1) % half
+            return beside(s), chip ^ k if power else chip + k
 
         return lax.ppermute(x, ("section", "seqtp"), route(goal))
 
     def home(x, t):
         def goal(s, chip, core):
             k = 2 * swapped(half, t, home_turns, chip) + 1 if core else 2 * (half - 1 - t)
-            return s - 1, chip ^ k if power else chip - k
+            to = before(s) if k else s - 2 if even else s - 1
+            return to, chip ^ k if power else chip - k
 
         return lax.ppermute(x, ("section", "seqtp"), route(goal))
 
     def back(x):
-        return lax.ppermute(x, ("section", "seqtp"), route(lambda s, chip, core: (s - 1, chip)))
+        return lax.ppermute(x, ("section", "seqtp"), route(lambda s, chip, core: (s - 2 if even else s - 1, chip)))
 
     def to_core(x):
         return lax.ppermute(x, "seqtp", [(i, i ^ 1) for i in range(members)])
 
     slots = saved_in.shape[1]
-    sent, raw, gain_row = pl.pallas_call(
+    sent, gain_row = pl.pallas_call(
         prepare,
-        out_shape=[VMEM((r, (slots + 1) * d), bf16), VMEM((r, slots * d), bf16), VMEM(gain.shape, bf16)],
+        out_shape=[VMEM((r, (slots + 1) * d), bf16), VMEM(gain.shape, bf16)],
         in_specs=anywhere(3),
-        out_specs=whole(3),
+        out_specs=whole(2),
         scratch_shapes=[pltpu.SemaphoreType.DMA((slots + 2,))],
         compiler_params=params(4),
         name="prepare",
     )(*far_off(saved_in, grad_in, gain))
-    chip_rows, own = pl.pallas_call(
+    chip_rows = pl.pallas_call(
         join,
-        out_shape=[VMEM((CORES * r, 2 * d), bf16), VMEM((r, 2 * d + d // r), bf16)],
-        in_specs=[pl.BlockSpec(memory_space=pltpu.SMEM)] + whole(4),
-        out_specs=whole(2),
+        out_shape=VMEM((CORES * r, 2 * d + d // (CORES * r)), bf16),
+        in_specs=[pl.BlockSpec(memory_space=pltpu.SMEM)] + whole(3),
+        out_specs=pl.BlockSpec(memory_space=VMEM),
         compiler_params=params(4),
         name="join",
-    )(slot_table, *near_core(sent, to_core(sent), raw, gain_row))
+    )(slot_table, *near_core(sent, to_core(sent), gain_row))
     both, gate_turned = pl.pallas_call(
         fetch,
         out_shape=[VMEM((d, 2 * hidden), bf16), VMEM((hidden, d), bf16)],
@@ -271,14 +286,14 @@
     )(*far_off(w_gate, w_up))
     blocks = [ahead(chip_rows, t) for t in range(half)]
     rows = chips * r
-    block = pl.pallas_call(
+    block, gain_wide = pl.pallas_call(
         functools.partial(collect, out_turns),
-        out_shape=VMEM((rows, 2 * d), bf16),
-        in_specs=whole(1 + len(blocks)) + anywhere(1),
-        out_specs=pl.BlockSpec(memory_space=VMEM),
+        out_shape=[VMEM((rows, 2 * d), bf16), VMEM((1, d), f32)],
+        in_specs=whole(len(blocks)) + anywhere(1),
+        out_specs=whole(2),
         compiler_params=params(4),
         name="collect",
-    )(*near_core(chip_rows, *blocks[::-1], both))
+    )(*near_core(*blocks, both))
     far = to_core(block)
     up_turned = pl.pallas_call(
         turn,
@@ -289,15 +304,15 @@
         cost_estimate=cost(4 * d * hidden),
         name="turn",
     )(*near_core(both, block))
-    normed, grad = pl.pallas_call(
+    normed, grad, own = pl.pallas_call(
         arrange,
-        out_shape=[VMEM((2 * rows, d), bf16)] * 2,
-        in_specs=whole(2),
-        out_specs=whole(2),
+        out_shape=[VMEM((2 * rows, d), bf16)] * 2 + [VMEM((r, 2 * d + d // r), bf16)],
+        in_specs=whole(3),
+        out_specs=whole(3),
         scratch_shapes=[VMEM((2 * rows, 2 * d), f32)],
-        compiler_params=params(4),
+        compiler_params=params(16),
         name="arrange",
-    )(*near_core(block, far))
+    )(*near_core(block, far, gain_wide))
     mine, other = pl.pallas_call(
         functools.partial(expert, CORES * r),
         out_shape=[VMEM((rows, d), f32)] * 2,
@@ -315,24 +330,24 @@
         name="add_cores",
     )(*near_core(mine, to_core(other)))
     landed = [home(x, t) for t, x in enumerate(sums)]
-    own = back(own)
+    moved = back(own)
     keep, send = pl.pallas_call(
-        add_chips,
+        functools.partial(add_chips, stays),
         out_shape=[VMEM((r, d), f32)] * 2,
-        in_specs=whole(half),
+        in_specs=whole(1 + half),
         out_specs=whole(2),
         compiler_params=params(4),
         name="add_chips",
-    )(*near_core(*landed))
+    )(*near_core(sums[-1], *landed))
     return pl.pallas_call(
-        finish,
+        functools.partial(finish, stays),
         out_shape=jax.ShapeDtypeStruct((1, r, d), bf16),
-        in_specs=whole(3),
+        in_specs=whole(4),
         out_specs=pl.BlockSpec(memory_space=VMEM),
         scratch_shapes=[VMEM((1, d), f32)],
         compiler_params=params(4),
         name="finish",
-    )(*near_core(own, keep, to_core(send)))
+    )(*near_core(own, moved, keep, to_core(send)))
 
 
 def solution(mesh):

time: 26.8 us -> 26.2 us (0.978)
  starting transfers between devices: 12.3 us -> 10.6 us
  waiting for transfers between devices: 4.63 us -> 5.87 us
    ppermute x2, starting transfers between devices: 4.94 us -> 3.35 us  [home(): return lax.ppermute(x, ('section', 'seqtp'), route(goal))]
    ppermute x2, waiting for transfers between devices: 0.01 us -> 1.16 us  [ahead(): return lax.ppermute(x, ('section', 'seqtp'), route(goal))]
    ppermute x1, starting transfers between devices: 1.4 us -> 0.51 us  [back(): lax.ppermute(x, ('section', 'seqtp'), route(lambda s, chip, core: (s - 2...]
    ppermute x1, waiting for transfers between devices: 0.61 us -> 1.48 us  [back(): lax.ppermute(x, ('section', 'seqtp'), route(lambda s, chip, core: (s - 2...]
    ppermute x4, starting transfers between devices: 1.53 us -> 2.33 us  [to_core(): return lax.ppermute(x, 'seqtp', [(i, i ^ 1) for i in range(members)])]
    ppermute x4, waiting for transfers between devices: 1.92 us -> 1.34 us  [to_core(): return lax.ppermute(x, 'seqtp', [(i, i ^ 1) for i in range(members)])]
  transfers between devices with their start and end apart: 9 -> 9, of which waited for: 6 -> 6; matrix products, arithmetic and copies ran while one was open for 0% -> 0% of each run, Pallas kernels for 14% -> 15%
where the time goes in v6:
time: 26.2 us; the launch traced here: 26 us
  starting transfers between devices  10.6 us (40%)
  Pallas kernels  7.82 us (30%)
  waiting for transfers between devices  5.87 us (22%)
  matrix products  0.91 us (3%)
  between operations  0.73 us (3%)
    ppermute x2, starting transfers between devices, ahead(): return lax.ppermute(x, ('section', 'seqtp'), route(goal))  4.44 us
    ppermute x2, starting transfers between devices, home(): return lax.ppermute(x, ('section', 'seqtp'), route(goal))  3.35 us
    pallas_call x1, Pallas kernels, on_device(): pl.pallas_call(fetch, out_shape=[VMEM((d, 2 * hidden), bf16), VMEM((hidde...  2.9 us
    ppermute x4, starting transfers between devices, to_core(): return lax.ppermute(x, 'seqtp', [(i, i ^ 1) for i in range(members)])  2.33 us
    ppermute x2, waiting for transfers between devices, home(): return lax.ppermute(x, ('section', 'seqtp'), route(goal))  1.89 us
    pallas_call x1, Pallas kernels, on_device(): pl.pallas_call(functools.partial(expert, CORES * r), out_shape=[VMEM((row...  1.76 us
    ppermute x1, waiting for transfers between devices, back(): lax.ppermute(x, ('section', 'seqtp'), route(lambda s, chip, core: (s - 2...  1.48 us
    ppermute x4, waiting for transfers between devices, to_core(): return lax.ppermute(x, 'seqtp', [(i, i ^ 1) for i in range(members)])  1.34 us
  transfers between devices with their start and end apart: 9, of which 6 were waited for; matrix products, arithmetic and copies ran while one was open for 0% of the time, Pallas kernels for 15%

profile of v6, /device:TPU:0, one launch (start us, length us, event | category | flops | bytes accessed | tf_op | source)
XLA Modules:
  0.0 26.0 jit_solution(16551118080460953738)
XLA Ops:
  0.0 0.0 copy-start
  0.0 1.0 %prepare.1 = (bf16[2,20480]{1,0:T(2,128)(2,1)S(1)}, bf16[1,4096]{1,0:T(2,128)(2,1)S(1)}) custom-call(bf16[1,4,2,4096]{3,2,1,0:T(2,128)(2,1)} %saved_hbm.1, bf16[1,2,4096]{2,1,0:T(2,128)(2,1)} %grad_hbm.1, bf16[1,4096]{1,0:T(2,128)(2,1)} %gain_hbm.1), custom_call_target="tpu_custom_call" | custom-call | tf_op jit(solution)/shard_map/prepare/pallas_call | solution.py:260
  1.0 0.5 %collective-permute-start = (bf16[2,20480]{1,0:T(2,128)(2,1)S(1)}, bf16[2,20480]{1,0:T(2,128)(2,1)S(1)}, u32[]{:S(2)}, u32[]{:S(2)}) collective-permute-start(bf16[2,20480]{1,0:T(2,128)(2,1)S(1)} %get-tuple-element.20.mine_ref), channel_id=1, source_target_pairs={{0,1},{1,0},{2,3},{3,2},{4,5},{5,4},{6,7},{7,6},{8,9},{9,8},{10,11... | collective-permute-start | bytes 245768 | tf_op jit(solution)/shard_map/ppermute | solution.py:257
  2.2 0.3 %collective-permute-done.other_ref = bf16[2,20480]{1,0:T(2,128)(2,1)S(1)} collective-permute-done((bf16[2,20480]{1,0:T(2,128)(2,1)S(1)}, bf16[2,20480]{1,0:T(2,128)(2,1)S(1)}, u32[]{:S(2)}, u32[]{:S(2)}) %collective-permute-start) | collective-permute-done | bytes 81952 | tf_op jit(solution)/shard_map/ppermute | solution.py:257
  2.5 3.9 %collective-permute-start.1 = (bf16[4,9216]{1,0:T(4,128)(2,1)S(1)}, bf16[4,9216]{1,0:T(4,128)(2,1)S(1)}, u32[]{:S(2)}, u32[]{:S(2)}) collective-permute-start(bf16[4,9216]{1,0:T(4,128)(2,1)S(1)} %join.1), channel_id=1, source_target_pairs={{0,10},{1,13},{2,8},{3,15},{4,14},{5,11},{6,12},{7,9},{8,2},{9,5},... | collective-permute-start | bytes 221192 | tf_op jit(solution)/shard_map/ppermute | solution.py:243
  6.4 0.5 %collective-permute-start.2 = (bf16[4,9216]{1,0:T(4,128)(2,1)S(1)}, bf16[4,9216]{1,0:T(4,128)(2,1)S(1)}, u32[]{:S(2)}, u32[]{:S(2)}) collective-permute-start(bf16[4,9216]{1,0:T(4,128)(2,1)S(1)} %join.1), channel_id=1, source_target_pairs={{0,8},{1,15},{2,10},{3,13},{4,12},{5,9},{6,14},{7,11},{8,0},{9,7},... | collective-permute-start | bytes 221192 | tf_op jit(solution)/shard_map/ppermute | solution.py:243
  6.9 2.9 %fetch.1 = (bf16[4096,768]{1,0:T(8,128)(2,1)S(1)}, bf16[384,4096]{1,0:T(8,128)(2,1)S(1)}) custom-call(bf16[4096,384]{1,0:T(8,128)(2,1)} %gate_hbm.1, bf16[4096,384]{1,0:T(8,128)(2,1)} %up_hbm.1), custom_call_target="tpu_custom_call" | custom-call | bytes 12582912 | tf_op jit(solution)/shard_map/fetch/pallas_call | solution.py:277
  9.8 0.0 collective-permute-done.1.refs_0_
  9.8 1.2 %collective-permute-done.2.refs_1_ = bf16[4,9216]{1,0:T(4,128)(2,1)S(1)} collective-permute-done((bf16[4,9216]{1,0:T(4,128)(2,1)S(1)}, bf16[4,9216]{1,0:T(4,128)(2,1)S(1)}, u32[]{:S(2)}, u32[]{:S(2)}) %collective-permute-start.2) | collective-permute-done | bytes 73760 | tf_op jit(solution)/shard_map/ppermute | solution.py:243
  11.1 1.3 %collective-permute-start.3 = (bf16[8,8192]{1,0:T(8,128)(2,1)S(1)}, bf16[8,8192]{1,0:T(8,128)(2,1)S(1)}, u32[]{:S(2)}, u32[]{:S(2)}) collective-permute-start(bf16[8,8192]{1,0:T(8,128)(2,1)S(1)} %get-tuple-element.23.near_ref.after), channel_id=1, source_target_pairs={{0,1},{1,0},{2,3},{3,2},{4,5},{5,4},{6,7},{7,6},{8,9},{9,8},{10,11... | collective-permute-start | bytes 393224 | tf_op jit(solution)/shard_map/ppermute | solution.py:257
  12.4 0.9 %turn.1.up_ref = bf16[384,4096]{1,0:T(8,128)(2,1)S(1)} custom-call(bf16[4096,768]{1,0:T(8,128)(2,1)S(1)} %get-tuple-element.22.refs_2_.both_ref, bf16[8,8192]{1,0:T(8,128)(2,1)S(1)} %get-tuple-element.23.near_ref.after), custom_call_target="tpu_custom_call" | custom-call | bytes 6291456 | tf_op jit(solution)/shard_map/turn/pallas_call | solution.py:298
  13.3 0.1 collective-permute-done.3.far_ref
  13.4 0.2 arrange.1
  13.6 0.0 copy-done
  13.6 0.9 %fusion.hidden_ref = f32[16,384]{1,0:T(8,128)S(1)} fusion(bf16[16,4096]{1,0:T(8,128)(2,1)S(1)} %get-tuple-element.27, bf16[384,4096]{1,0:T(8,128)(2,1)S(1)} %copy-done), kind=kOutput, calls=%fused_computation | convolution fusion | flops 50331648 | bytes 3301376 | tf_op jit(solution)/shard_map/dot_general | solution.py:60
  14.5 1.8 %expert.1 = (f32[8,4096]{1,0:T(8,128)S(1)}, f32[8,4096]{1,0:T(8,128)S(1)}) custom-call(bf16[16,4096]{1,0:T(8,128)(2,1)S(1)} %get-tuple-element.26.normed_ref, f32[16,384]{1,0:T(8,128)S(1)} %fusion.hidden_ref, bf16[4096,768]{1,0:T(8,128)(2,1)S(1)} %get-tuple-element.22.refs_2_.both_ref, bf16[384,4096]{1,0:T(8,128)(2,1)S(1)} %get-tuple-element.28.gate_ref, ...), custom_call_target="tpu_custom_call" | custom-call | tf_op jit(solution)/shard_map/expert/pallas_call | solution.py:316
  16.3 0.4 %collective-permute-start.5 = (f32[8,4096]{1,0:T(8,128)S(1)}, f32[8,4096]{1,0:T(8,128)S(1)}, u32[]{:S(2)}, u32[]{:S(2)}) collective-permute-start(f32[8,4096]{1,0:T(8,128)S(1)} %get-tuple-element.30), channel_id=1, source_target_pairs={{0,1},{1,0},{2,3},{3,2},{4,5},{5,4},{6,7},{7,6},{8,9},{9,8},{10,11... | collective-permute-start | bytes 393224 | tf_op jit(solution)/shard_map/ppermute | solution.py:257
  16.7 1.0 %collective-permute-done.5.got_ref = f32[8,4096]{1,0:T(8,128)S(1)} collective-permute-done((f32[8,4096]{1,0:T(8,128)S(1)}, f32[8,4096]{1,0:T(8,128)S(1)}, u32[]{:S(2)}, u32[]{:S(2)}) %collective-permute-start.5) | collective-permute-done | bytes 131104 | tf_op jit(solution)/shard_map/ppermute | solution.py:257
  17.7 0.1 add_cores.1
  17.7 1.8 %collective-permute-start.6 = (bf16[4,4096]{1,0:T(4,128)(2,1)S(1)}, bf16[4,4096]{1,0:T(4,128)(2,1)S(1)}, u32[]{:S(2)}, u32[]{:S(2)}) collective-permute-start(bf16[4,4096]{1,0:T(4,128)(2,1)S(1)} %get-tuple-element.32), channel_id=1, source_target_pairs={{0,4},{1,3},{2,6},{3,5},{4,0},{5,7},{6,2},{7,1},{8,28},{9,27},{10,... | collective-permute-start | bytes 98312 | tf_op jit(solution)/shard_map/ppermute | solution.py:251
  19.5 1.5 %collective-permute-start.7 = (bf16[4,4096]{1,0:T(4,128)(2,1)S(1)}, bf16[4,4096]{1,0:T(4,128)(2,1)S(1)}, u32[]{:S(2)}, u32[]{:S(2)}) collective-permute-start(bf16[4,4096]{1,0:T(4,128)(2,1)S(1)} %get-tuple-element.31.local_ref), channel_id=1, source_target_pairs={{0,16},{1,7},{2,18},{3,1},{4,20},{5,3},{6,22},{7,5},{8,24},{9,31},... | collective-permute-start | bytes 98312 | tf_op jit(solution)/shard_map/ppermute | solution.py:251
  21.1 0.5 %collective-permute-start.4 = (bf16[2,10240]{1,0:T(2,128)(2,1)S(1)}, bf16[2,10240]{1,0:T(2,128)(2,1)S(1)}, u32[]{:S(2)}, u32[]{:S(2)}) collective-permute-start(bf16[2,10240]{1,0:T(2,128)(2,1)S(1)} %get-tuple-element.25.stayed_ref), channel_id=1, source_target_pairs={{0,16},{1,17},{2,18},{3,19},{4,20},{5,21},{6,22},{7,23},{8,24},{9,... | collective-permute-start | bytes 122888 | tf_op jit(solution)/shard_map/ppermute | solution.py:254
  21.6 1.9 %collective-permute-done.6.refs_0_ = bf16[4,4096]{1,0:T(4,128)(2,1)S(1)} collective-permute-done((bf16[4,4096]{1,0:T(4,128)(2,1)S(1)}, bf16[4,4096]{1,0:T(4,128)(2,1)S(1)}, u32[]{:S(2)}, u32[]{:S(2)}) %collective-permute-start.6) | collective-permute-done | bytes 32800 | tf_op jit(solution)/shard_map/ppermute | solution.py:251
  23.5 0.0 collective-permute-done.7.refs_1_
  23.5 0.1 collective-permute-start.8
  23.6 1.5 %collective-permute-done.4.moved_ref = bf16[2,10240]{1,0:T(2,128)(2,1)S(1)} collective-permute-done((bf16[2,10240]{1,0:T(2,128)(2,1)S(1)}, bf16[2,10240]{1,0:T(2,128)(2,1)S(1)}, u32[]{:S(2)}, u32[]{:S(2)}) %collective-permute-start.4) | collective-permute-done | bytes 40992 | tf_op jit(solution)/shard_map/ppermute | solution.py:254
  25.1 0.0 collective-permute-done.8.got_ref
  25.1 0.9 %finish.1 = bf16[1,2,4096]{2,1,0:T(2,128)(2,1)} custom-call(bf16[2,10240]{1,0:T(2,128)(2,1)S(1)} %get-tuple-element.25.stayed_ref, bf16[2,10240]{1,0:T(2,128)(2,1)S(1)} %collective-permute-done.4.moved_ref, f32[2,4096]{1,0:T(2,128)S(1)} %get-tuple-element.33.keep_ref, f32[2,4096]{1,0:T(2,128)S(1)} %collective-permute-done.8.got_ref), custom_call_target="tpu_custom_call" | custom-call | tf_op jit(solution)/shard_map/finish/pallas_call | solution.py:342
  (3 shorter events, 0.1 us)
Async XLA Ops:
  0.0 13.6 %copy-start = (bf16[384,4096]{1,0:T(8,128)(2,1)S(1)}, bf16[384,4096]{1,0:T(8,128)(2,1)}, u32[]{:S(2)}) copy-start(bf16[384,4096]{1,0:T(8,128)(2,1)} %param.13) | copy-start | bytes 9437188
  1.0 1.4 %collective-permute-start = (bf16[2,20480]{1,0:T(2,128)(2,1)S(1)}, bf16[2,20480]{1,0:T(2,128)(2,1)S(1)}, u32[]{:S(2)}, u32[]{:S(2)}) collective-permute-start(bf16[2,20480]{1,0:T(2,128)(2,1)S(1)} %get-tuple-element.20.mine_ref), channel_id=1, source_target_pairs={{0,1},{1,0},{2,3},{3,2},{4,5},{5,4},{6,7},{7,6},{8,9},{9,8},{10,11... | collective-permute-start | bytes 245768 | tf_op jit(solution)/shard_map/ppermute | solution.py:257
  2.5 7.3 %collective-permute-start.1 = (bf16[4,9216]{1,0:T(4,128)(2,1)S(1)}, bf16[4,9216]{1,0:T(4,128)(2,1)S(1)}, u32[]{:S(2)}, u32[]{:S(2)}) collective-permute-start(bf16[4,9216]{1,0:T(4,128)(2,1)S(1)} %join.1), channel_id=1, source_target_pairs={{0,10},{1,13},{2,8},{3,15},{4,14},{5,11},{6,12},{7,9},{8,2},{9,5},... | collective-permute-start | bytes 221192 | tf_op jit(solution)/shard_map/ppermute | solution.py:243
  6.4 4.6 %collective-permute-start.2 = (bf16[4,9216]{1,0:T(4,128)(2,1)S(1)}, bf16[4,9216]{1,0:T(4,128)(2,1)S(1)}, u32[]{:S(2)}, u32[]{:S(2)}) collective-permute-start(bf16[4,9216]{1,0:T(4,128)(2,1)S(1)} %join.1), channel_id=1, source_target_pairs={{0,8},{1,15},{2,10},{3,13},{4,12},{5,9},{6,14},{7,11},{8,0},{9,7},... | collective-permute-start | bytes 221192 | tf_op jit(solution)/shard_map/ppermute | solution.py:243
  11.1 2.3 %collective-permute-start.3 = (bf16[8,8192]{1,0:T(8,128)(2,1)S(1)}, bf16[8,8192]{1,0:T(8,128)(2,1)S(1)}, u32[]{:S(2)}, u32[]{:S(2)}) collective-permute-start(bf16[8,8192]{1,0:T(8,128)(2,1)S(1)} %get-tuple-element.23.near_ref.after), channel_id=1, source_target_pairs={{0,1},{1,0},{2,3},{3,2},{4,5},{5,4},{6,7},{7,6},{8,9},{9,8},{10,11... | collective-permute-start | bytes 393224 | tf_op jit(solution)/shard_map/ppermute | solution.py:257
  16.3 1.4 %collective-permute-start.5 = (f32[8,4096]{1,0:T(8,128)S(1)}, f32[8,4096]{1,0:T(8,128)S(1)}, u32[]{:S(2)}, u32[]{:S(2)}) collective-permute-start(f32[8,4096]{1,0:T(8,128)S(1)} %get-tuple-element.30), channel_id=1, source_target_pairs={{0,1},{1,0},{2,3},{3,2},{4,5},{5,4},{6,7},{7,6},{8,9},{9,8},{10,11... | collective-permute-start | bytes 393224 | tf_op jit(solution)/shard_map/ppermute | solution.py:257
  17.7 5.7 %collective-permute-start.6 = (bf16[4,4096]{1,0:T(4,128)(2,1)S(1)}, bf16[4,4096]{1,0:T(4,128)(2,1)S(1)}, u32[]{:S(2)}, u32[]{:S(2)}) collective-permute-start(bf16[4,4096]{1,0:T(4,128)(2,1)S(1)} %get-tuple-element.32), channel_id=1, source_target_pairs={{0,4},{1,3},{2,6},{3,5},{4,0},{5,7},{6,2},{7,1},{8,28},{9,27},{10,... | collective-permute-start | bytes 98312 | tf_op jit(solution)/shard_map/ppermute | solution.py:251
  19.5 3.9 %collective-permute-start.7 = (bf16[4,4096]{1,0:T(4,128)(2,1)S(1)}, bf16[4,4096]{1,0:T(4,128)(2,1)S(1)}, u32[]{:S(2)}, u32[]{:S(2)}) collective-permute-start(bf16[4,4096]{1,0:T(4,128)(2,1)S(1)} %get-tuple-element.31.local_ref), channel_id=1, source_target_pairs={{0,16},{1,7},{2,18},{3,1},{4,20},{5,3},{6,22},{7,5},{8,24},{9,31},... | collective-permute-start | bytes 98312 | tf_op jit(solution)/shard_map/ppermute | solution.py:251
  21.1 4.0 %collective-permute-start.4 = (bf16[2,10240]{1,0:T(2,128)(2,1)S(1)}, bf16[2,10240]{1,0:T(2,128)(2,1)S(1)}, u32[]{:S(2)}, u32[]{:S(2)}) collective-permute-start(bf16[2,10240]{1,0:T(2,128)(2,1)S(1)} %get-tuple-element.25.stayed_ref), channel_id=1, source_target_pairs={{0,16},{1,17},{2,18},{3,19},{4,20},{5,21},{6,22},{7,23},{8,24},{9,... | collective-permute-start | bytes 122888 | tf_op jit(solution)/shard_map/ppermute | solution.py:254
  23.5 1.6 %collective-permute-start.8 = (f32[2,4096]{1,0:T(2,128)S(1)}, f32[2,4096]{1,0:T(2,128)S(1)}, u32[]{:S(2)}, u32[]{:S(2)}) collective-permute-start(f32[2,4096]{1,0:T(2,128)S(1)} %get-tuple-element.34), channel_id=1, source_target_pairs={{0,1},{1,0},{2,3},{3,2},{4,5},{5,4},{6,7},{7,6},{8,9},{9,8},{10,11... | collective-permute-start | bytes 98312 | tf_op jit(solution)/shard_map/ppermute | solution.py:257

commit v7 on v6

--- a/solution.py
+++ b/solution.py
@@ -54,12 +54,6 @@
 
 def nn(left, weight):
     return jnp.dot(left, weight, preferred_element_type=jnp.float32)
-
-
-def nt(left, weight):
-    return lax.dot_general(
-        left, weight, (((1,), (1,)), ((), ())), preferred_element_type=jnp.float32
-    )
 
 
 def prepare(saved_hbm, grad_hbm, gain_hbm, sent_ref, gain_ref, sems):
@@ -91,37 +85,43 @@
         rows_ref[n : n + 1, 2 * d :] = gain_ref[:, n * piece : (n + 1) * piece]
 
 
-def fetch(gate_hbm, up_hbm, both_ref, turned_ref, sems, up_sem):
+def fetch(gate_hbm, up_hbm, down_hbm, both_ref, gate_ref, up_ref, down_ref, sems, last_sem):
     d, h = gate_hbm.shape
-    parts = sems.shape[0]
+    parts = sems.shape[1]
     rows = d // parts
+    columns = (gate_hbm, up_hbm)
     copies = [
-        pltpu.make_async_copy(
-            gate_hbm.at[pl.ds(n * rows, rows)], both_ref.at[pl.ds(n * rows, rows), pl.ds(0, h)], sems.at[n]
-        )
-        for n in range(parts)
+        [
+            pltpu.make_async_copy(
+                src.at[pl.ds(n * rows, rows)], both_ref.at[pl.ds(n * rows, rows), pl.ds(k * h, h)], sems.at[k, n]
+            )
+            for n in range(parts)
+        ]
+        for k, src in enumerate(columns)
     ]
-    up = pltpu.make_async_copy(up_hbm, both_ref.at[:, pl.ds(h, h)], up_sem)
-    for copy in copies + [up]:
+    last = pltpu.make_async_copy(down_hbm, down_ref, last_sem)
+    for copy in copies[0] + copies[1] + [last]:
         copy.start()
-    for n, copy in enumerate(copies):
-        copy.wait()
-        turned_ref[:, n * rows : (n + 1) * rows] = both_ref[n * rows : (n + 1) * rows, :h].T
-    up.wait()
-
-
-def turn(both_ref, after, turned_ref):
-    h, d = turned_ref.shape
+    for k, turned_ref in enumerate((gate_ref, up_ref)):
+        for n, copy in enumerate(copies[k]):
+            copy.wait()
+            here = slice(n * rows, (n + 1) * rows)
+            turned_ref[:, here] = both_ref[here, k * h : (k + 1) * h].T
+    last.wait()
+
+
+def turn(down_ref, after, turned_ref):
+    d = turned_ref.shape[0]
     step = d // 8
     for n in range(0, d, step):
-        turned_ref[:, n : n + step] = both_ref[n : n + step, h:].T
+        turned_ref[n : n + step] = down_ref[:, n : n + step].T
 
 
 def collect(turns, *refs):
     *blocks, after, out_ref, gain_ref = refs
     r = blocks[0].shape[0]
     first, turned = on_first_core(), on_chip_with(turns)
-    came = [ref[:, : out_ref.shape[1]] for ref in blocks]
+    came = [ref[:, : out_ref.shape[1]] for ref in blocks[::-1]]
     nearer = came[-1:] + came[:-1]
     farther = crossed(came, turned) if turns else came
     for n, (a, b) in enumerate(zip(nearer, farther)):
@@ -149,11 +149,11 @@
         own_ref[n : n + 1, 2 * d :] = gain_ref[:, n * piece : (n + 1) * piece].astype(jnp.bfloat16)
 
 
-def expert(rows, normed_ref, hidden_ref, both_ref, gate_ref, up_ref, mine_ref, other_ref):
-    h = hidden_ref.shape[1]
-    gate = nn(normed_ref[...], both_ref[:, :h])
-    up = nn(normed_ref[...], both_ref[:, h:])
-    d_hidden = hidden_ref[...]
+def expert(rows, normed_ref, grad_ref, both_ref, gate_ref, up_ref, down_ref, mine_ref, other_ref):
+    h = down_ref.shape[1]
+    both = nn(normed_ref[...], both_ref[...])
+    gate, up = both[:, :h], both[:, h:]
+    d_hidden = nn(grad_ref[...], down_ref[...])
     p = jax.nn.sigmoid(gate)
     d_gate = d_hidden * up * p * (1.0 + gate * (1.0 - p))
     d_up = d_hidden * gate * p
@@ -220,8 +220,9 @@
         pairs = []
         for s in range(sections):
             for i in range(members):
-                to, chip = goal(s, *divmod(i, CORES))
-                pairs.append((s * members + i, to % sections * members + chip % chips * CORES + i % CORES))
+                to, chip, *core = goal(s, *divmod(i, CORES))
+                core = core[0] if core else i % CORES
+                pairs.append((s * members + i, to % sections * members + chip % chips * CORES + core))
         return pairs
 
     even = sections % 2 == 0
@@ -251,7 +252,7 @@
         return lax.ppermute(x, ("section", "seqtp"), route(goal))
 
     def back(x):
-        return lax.ppermute(x, ("section", "seqtp"), route(lambda s, chip, core: (s - 2 if even else s - 1, chip)))
+        return lax.ppermute(x, ("section", "seqtp"), route(lambda s, chip, core: (s, chip, core ^ 1) if before(s) == s else (before(s), chip)))
 
     def to_core(x):
         return lax.ppermute(x, "seqtp", [(i, i ^ 1) for i in range(members)])
@@ -274,16 +275,16 @@
         compiler_params=params(4),
         name="join",
     )(slot_table, *near_core(sent, to_core(sent), gain_row))
-    both, gate_turned = pl.pallas_call(
+    both, gate_turned, up_turned, down = pl.pallas_call(
         fetch,
-        out_shape=[VMEM((d, 2 * hidden), bf16), VMEM((hidden, d), bf16)],
-        in_specs=anywhere(2),
-        out_specs=whole(2),
-        scratch_shapes=[pltpu.SemaphoreType.DMA((4,)), pltpu.SemaphoreType.DMA],
-        compiler_params=params(4),
-        cost_estimate=cost(8 * d * hidden),
+        out_shape=[VMEM((d, 2 * hidden), bf16)] + [VMEM((hidden, d), bf16)] * 3,
+        in_specs=anywhere(3),
+        out_specs=whole(4),
+        scratch_shapes=[pltpu.SemaphoreType.DMA((2, 4)), pltpu.SemaphoreType.DMA],
+        compiler_params=params(4),
+        cost_estimate=cost(12 * d * hidden),
         name="fetch",
-    )(*far_off(w_gate, w_up))
+    )(*far_off(w_gate, w_up, w_down))
     blocks = [ahead(chip_rows, t) for t in range(half)]
     rows = chips * r
     block, gain_wide = pl.pallas_call(
@@ -293,17 +294,17 @@
         out_specs=whole(2),
         compiler_params=params(4),
         name="collect",
-    )(*near_core(*blocks, both))
+    )(*near_core(*blocks[::-1], both))
     far = to_core(block)
-    up_turned = pl.pallas_call(
+    down_turned = pl.pallas_call(
         turn,
-        out_shape=VMEM((hidden, d), bf16),
+        out_shape=VMEM((d, hidden), bf16),
         in_specs=whole(1) + anywhere(1),
         out_specs=pl.BlockSpec(memory_space=VMEM),
         compiler_params=params(4),
         cost_estimate=cost(4 * d * hidden),
         name="turn",
-    )(*near_core(both, block))
+    )(*near_core(down, block))
     normed, grad, own = pl.pallas_call(
         arrange,
         out_shape=[VMEM((2 * rows, d), bf16)] * 2 + [VMEM((r, 2 * d + d // r), bf16)],
@@ -316,11 +317,11 @@
     mine, other = pl.pallas_call(
         functools.partial(expert, CORES * r),
         out_shape=[VMEM((rows, d), f32)] * 2,
-        in_specs=whole(5),
+        in_specs=whole(6),
         out_specs=whole(2),
         compiler_params=params(16),
         name="expert",
-    )(*near_core(normed, nt(grad, w_down), both, gate_turned, up_turned))
+    )(*near_core(normed, grad, both, gate_turned, up_turned, down_turned))
     sums = pl.pallas_call(
         functools.partial(add_cores, home_turns),
         out_shape=[VMEM((CORES * r, d), bf16)] * half,

time: 26.2 us -> 25.4 us (0.969)
  Pallas kernels: 7.82 us -> 9.05 us
  waiting for transfers between devices: 5.87 us -> 4.83 us
  matrix products: 0.91 us -> 0 us
    ppermute x1, waiting for transfers between devices: 1.48 us -> 0.01 us  [back(): lax.ppermute(x, ('section', 'seqtp'), route(lambda s, chip, core: (s, chi...]
    ppermute x4, waiting for transfers between devices: 1.34 us -> 2.56 us  [to_core(): return lax.ppermute(x, 'seqtp', [(i, i ^ 1) for i in range(members)])]
    ppermute x2, waiting for transfers between devices: 1.16 us -> 0.19 us  [ahead(): return lax.ppermute(x, ('section', 'seqtp'), route(goal))]
    pallas_call x2, Pallas kernels: 3.8 us -> 4.73 us  [the longest x1 3.87 us: on_device(): pl.pallas_call(fetch, out_shape=[VMEM((d, 2 * hidden), bf16)] + [VMEM((hi...]
    dot_general x1 -> x0, matrix products: 0.91 us -> none  [nt(): lax.dot_general(left, weight, (((1,), (1,)), ((), ())), preferred_element...]
    pallas_call x1, Pallas kernels: 1.76 us -> 2.22 us  [on_device(): pl.pallas_call(functools.partial(expert, CORES * r), out_shape=[VMEM((row...]
  transfers between devices with their start and end apart: 9 -> 9, of which waited for: 6 -> 6; matrix products, arithmetic and copies ran while one was open for 0% -> 0% of each run, Pallas kernels for 15% -> 19%
where the time goes in v7:
time: 25.4 us; the launch traced here: 25 us
  starting transfers between devices  10.4 us (41%)
  Pallas kernels  9.05 us (36%)
  waiting for transfers between devices  4.83 us (19%)
  between operations  0.73 us (3%)
    ppermute x2, starting transfers between devices, ahead(): return lax.ppermute(x, ('section', 'seqtp'), route(goal))  4.44 us
    pallas_call x1, Pallas kernels, on_device(): pl.pallas_call(fetch, out_shape=[VMEM((d, 2 * hidden), bf16)] + [VMEM((hi...  3.87 us
    ppermute x2, starting transfers between devices, home(): return lax.ppermute(x, ('section', 'seqtp'), route(goal))  3.35 us
    ppermute x4, waiting for transfers between devices, to_core(): return lax.ppermute(x, 'seqtp', [(i, i ^ 1) for i in range(members)])  2.56 us
    ppermute x4, starting transfers between devices, to_core(): return lax.ppermute(x, 'seqtp', [(i, i ^ 1) for i in range(members)])  2.33 us
    pallas_call x1, Pallas kernels, on_device(): pl.pallas_call(functools.partial(expert, CORES * r), out_shape=[VMEM((row...  2.22 us
    ppermute x2, waiting for transfers between devices, home(): return lax.ppermute(x, ('section', 'seqtp'), route(goal))  2.07 us
    pallas_call x1, Pallas kernels, on_device(): pl.pallas_call(functools.partial(finish, stays), out_shape=jax.ShapeDtype...  0.88 us
  transfers between devices with their start and end apart: 9, of which 6 were waited for; matrix products, arithmetic and copies ran while one was open for 0% of the time, Pallas kernels for 19%

profile of v7, /device:TPU:0, one launch (start us, length us, event | category | flops | bytes accessed | tf_op | source)
XLA Modules:
  0.0 25.0 jit_solution(8781593362297441219)
XLA Ops:
  0.0 0.9 %prepare.1 = (bf16[2,20480]{1,0:T(2,128)(2,1)S(1)}, bf16[1,4096]{1,0:T(2,128)(2,1)S(1)}) custom-call(bf16[1,4,2,4096]{3,2,1,0:T(2,128)(2,1)} %saved_hbm.1, bf16[1,2,4096]{2,1,0:T(2,128)(2,1)} %grad_hbm.1, bf16[1,4096]{1,0:T(2,128)(2,1)} %gain_hbm.1), custom_call_target="tpu_custom_call" | custom-call | tf_op jit(solution)/shard_map/prepare/pallas_call | solution.py:261
  0.9 0.5 %collective-permute-start = (bf16[2,20480]{1,0:T(2,128)(2,1)S(1)}, bf16[2,20480]{1,0:T(2,128)(2,1)S(1)}, u32[]{:S(2)}, u32[]{:S(2)}) collective-permute-start(bf16[2,20480]{1,0:T(2,128)(2,1)S(1)} %get-tuple-element.22.mine_ref), channel_id=1, source_target_pairs={{0,1},{1,0},{2,3},{3,2},{4,5},{5,4},{6,7},{7,6},{8,9},{9,8},{10,11... | collective-permute-start | bytes 245768 | tf_op jit(solution)/shard_map/ppermute | solution.py:258
  2.0 0.3 %collective-permute-done.other_ref = bf16[2,20480]{1,0:T(2,128)(2,1)S(1)} collective-permute-done((bf16[2,20480]{1,0:T(2,128)(2,1)S(1)}, bf16[2,20480]{1,0:T(2,128)(2,1)S(1)}, u32[]{:S(2)}, u32[]{:S(2)}) %collective-permute-start) | collective-permute-done | bytes 81952 | tf_op jit(solution)/shard_map/ppermute | solution.py:258
  2.3 3.9 %collective-permute-start.2 = (bf16[4,9216]{1,0:T(4,128)(2,1)S(1)}, bf16[4,9216]{1,0:T(4,128)(2,1)S(1)}, u32[]{:S(2)}, u32[]{:S(2)}) collective-permute-start(bf16[4,9216]{1,0:T(4,128)(2,1)S(1)} %join.1), channel_id=1, source_target_pairs={{0,10},{1,13},{2,8},{3,15},{4,14},{5,11},{6,12},{7,9},{8,2},{9,5},... | collective-permute-start | bytes 221192 | tf_op jit(solution)/shard_map/ppermute | solution.py:244
  6.2 0.5 %collective-permute-start.1 = (bf16[4,9216]{1,0:T(4,128)(2,1)S(1)}, bf16[4,9216]{1,0:T(4,128)(2,1)S(1)}, u32[]{:S(2)}, u32[]{:S(2)}) collective-permute-start(bf16[4,9216]{1,0:T(4,128)(2,1)S(1)} %join.1), channel_id=1, source_target_pairs={{0,8},{1,15},{2,10},{3,13},{4,12},{5,9},{6,14},{7,11},{8,0},{9,7},... | collective-permute-start | bytes 221192 | tf_op jit(solution)/shard_map/ppermute | solution.py:244
  6.8 3.9 %fetch.1 = (bf16[4096,768]{1,0:T(8,128)(2,1)S(1)}, bf16[384,4096]{1,0:T(8,128)(2,1)S(1)}, bf16[384,4096]{1,0:T(8,128)(2,1)S(1)}, bf16[384,4096]{1,0:T(8,128)(2,1)S(1)}) custom-call(bf16[4096,384]{1,0:T(8,128)(2,1)} %gate_hbm.1, bf16[4096,384]{1,0:T(8,128)(2,1)} %up_hbm.1, bf16[384,4096]{1,0:T(8,128)(2,1)} %down_hbm.1), custom_call_target="tpu_custom_call" | custom-call | bytes 18874368 | tf_op jit(solution)/shard_map/fetch/pallas_call | solution.py:278
  10.7 0.0 collective-permute-done.2.refs_1_
  10.7 0.2 collective-permute-done.1.refs_0_
  10.9 0.1 collect.1
  10.9 1.3 %collective-permute-start.3 = (bf16[8,8192]{1,0:T(8,128)(2,1)S(1)}, bf16[8,8192]{1,0:T(8,128)(2,1)S(1)}, u32[]{:S(2)}, u32[]{:S(2)}) collective-permute-start(bf16[8,8192]{1,0:T(8,128)(2,1)S(1)} %get-tuple-element.25.near_ref.after), channel_id=1, source_target_pairs={{0,1},{1,0},{2,3},{3,2},{4,5},{5,4},{6,7},{7,6},{8,9},{9,8},{10,11... | collective-permute-start | bytes 393224 | tf_op jit(solution)/shard_map/ppermute | solution.py:258
  12.3 0.9 %turn.1.down_ref = bf16[4096,384]{1,0:T(8,128)(2,1)S(1)} custom-call(bf16[384,4096]{1,0:T(8,128)(2,1)S(1)} %get-tuple-element.32.down_ref, bf16[8,8192]{1,0:T(8,128)(2,1)S(1)} %get-tuple-element.25.near_ref.after), custom_call_target="tpu_custom_call" | custom-call | bytes 6291456 | tf_op jit(solution)/shard_map/turn/pallas_call | solution.py:299
  13.1 0.1 collective-permute-done.3.far_ref
  13.2 0.2 arrange.1
  13.4 2.2 %expert.1 = (f32[8,4096]{1,0:T(8,128)S(1)}, f32[8,4096]{1,0:T(8,128)S(1)}) custom-call(bf16[16,4096]{1,0:T(8,128)(2,1)S(1)} %get-tuple-element.28.normed_ref, bf16[16,4096]{1,0:T(8,128)(2,1)S(1)} %get-tuple-element.29.grad_ref, bf16[4096,768]{1,0:T(8,128)(2,1)S(1)} %get-tuple-element.24.refs_2_.both_ref, bf16[384,4096]{1,0:T(8,128)(2,1)S(1)} %get-tuple-element.30.gate_ref, ...), custom_call_target="tpu_custom_call" | custom-call | tf_op jit(solution)/shard_map/expert/pallas_call | solution.py:317
  15.7 0.4 %collective-permute-start.5 = (f32[8,4096]{1,0:T(8,128)S(1)}, f32[8,4096]{1,0:T(8,128)S(1)}, u32[]{:S(2)}, u32[]{:S(2)}) collective-permute-start(f32[8,4096]{1,0:T(8,128)S(1)} %get-tuple-element.34), channel_id=1, source_target_pairs={{0,1},{1,0},{2,3},{3,2},{4,5},{5,4},{6,7},{7,6},{8,9},{9,8},{10,11... | collective-permute-start | bytes 393224 | tf_op jit(solution)/shard_map/ppermute | solution.py:258
  16.1 1.0 %collective-permute-done.5.got_ref = f32[8,4096]{1,0:T(8,128)S(1)} collective-permute-done((f32[8,4096]{1,0:T(8,128)S(1)}, f32[8,4096]{1,0:T(8,128)S(1)}, u32[]{:S(2)}, u32[]{:S(2)}) %collective-permute-start.5) | collective-permute-done | bytes 131104 | tf_op jit(solution)/shard_map/ppermute | solution.py:258
  17.0 0.1 add_cores.1
  17.1 1.8 %collective-permute-start.6 = (bf16[4,4096]{1,0:T(4,128)(2,1)S(1)}, bf16[4,4096]{1,0:T(4,128)(2,1)S(1)}, u32[]{:S(2)}, u32[]{:S(2)}) collective-permute-start(bf16[4,4096]{1,0:T(4,128)(2,1)S(1)} %get-tuple-element.36), channel_id=1, source_target_pairs={{0,4},{1,3},{2,6},{3,5},{4,0},{5,7},{6,2},{7,1},{8,28},{9,27},{10,... | collective-permute-start | bytes 98312 | tf_op jit(solution)/shard_map/ppermute | solution.py:252
  18.9 1.5 %collective-permute-start.7 = (bf16[4,4096]{1,0:T(4,128)(2,1)S(1)}, bf16[4,4096]{1,0:T(4,128)(2,1)S(1)}, u32[]{:S(2)}, u32[]{:S(2)}) collective-permute-start(bf16[4,4096]{1,0:T(4,128)(2,1)S(1)} %get-tuple-element.35.local_ref), channel_id=1, source_target_pairs={{0,16},{1,7},{2,18},{3,1},{4,20},{5,3},{6,22},{7,5},{8,24},{9,31},... | collective-permute-start | bytes 98312 | tf_op jit(solution)/shard_map/ppermute | solution.py:252
  20.4 0.3 %collective-permute-start.4 = (bf16[2,10240]{1,0:T(2,128)(2,1)S(1)}, bf16[2,10240]{1,0:T(2,128)(2,1)S(1)}, u32[]{:S(2)}, u32[]{:S(2)}) collective-permute-start(bf16[2,10240]{1,0:T(2,128)(2,1)S(1)} %get-tuple-element.27.stayed_ref), channel_id=1, source_target_pairs={{0,1},{1,0},{2,3},{3,2},{4,5},{5,4},{6,7},{7,6},{8,24},{9,25},{10,... | collective-permute-start | bytes 122888 | tf_op jit(solution)/shard_map/ppermute | solution.py:255
  20.8 2.1 %collective-permute-done.6.refs_0_ = bf16[4,4096]{1,0:T(4,128)(2,1)S(1)} collective-permute-done((bf16[4,4096]{1,0:T(4,128)(2,1)S(1)}, bf16[4,4096]{1,0:T(4,128)(2,1)S(1)}, u32[]{:S(2)}, u32[]{:S(2)}) %collective-permute-start.6) | collective-permute-done | bytes 32800 | tf_op jit(solution)/shard_map/ppermute | solution.py:252
  22.8 0.0 collective-permute-done.7.refs_1_
  22.9 0.1 collective-permute-start.8
  23.0 0.0 collective-permute-done.4.moved_ref
  23.0 1.2 %collective-permute-done.8.got_ref = f32[2,4096]{1,0:T(2,128)S(1)} collective-permute-done((f32[2,4096]{1,0:T(2,128)S(1)}, f32[2,4096]{1,0:T(2,128)S(1)}, u32[]{:S(2)}, u32[]{:S(2)}) %collective-permute-start.8) | collective-permute-done | bytes 32800 | tf_op jit(solution)/shard_map/ppermute | solution.py:258
  24.2 0.9 %finish.1 = bf16[1,2,4096]{2,1,0:T(2,128)(2,1)} custom-call(bf16[2,10240]{1,0:T(2,128)(2,1)S(1)} %get-tuple-element.27.stayed_ref, bf16[2,10240]{1,0:T(2,128)(2,1)S(1)} %collective-permute-done.4.moved_ref, f32[2,4096]{1,0:T(2,128)S(1)} %get-tuple-element.37.keep_ref, f32[2,4096]{1,0:T(2,128)S(1)} %collective-permute-done.8.got_ref), custom_call_target="tpu_custom_call" | custom-call | tf_op jit(solution)/shard_map/finish/pallas_call | solution.py:343
  (2 shorter events, 0.1 us)
Async XLA Ops:
  0.9 1.4 %collective-permute-start = (bf16[2,20480]{1,0:T(2,128)(2,1)S(1)}, bf16[2,20480]{1,0:T(2,128)(2,1)S(1)}, u32[]{:S(2)}, u32[]{:S(2)}) collective-permute-start(bf16[2,20480]{1,0:T(2,128)(2,1)S(1)} %get-tuple-element.22.mine_ref), channel_id=1, source_target_pairs={{0,1},{1,0},{2,3},{3,2},{4,5},{5,4},{6,7},{7,6},{8,9},{9,8},{10,11... | collective-permute-start | bytes 245768 | tf_op jit(solution)/shard_map/ppermute | solution.py:258
  2.3 8.3 %collective-permute-start.2 = (bf16[4,9216]{1,0:T(4,128)(2,1)S(1)}, bf16[4,9216]{1,0:T(4,128)(2,1)S(1)}, u32[]{:S(2)}, u32[]{:S(2)}) collective-permute-start(bf16[4,9216]{1,0:T(4,128)(2,1)S(1)} %join.1), channel_id=1, source_target_pairs={{0,10},{1,13},{2,8},{3,15},{4,14},{5,11},{6,12},{7,9},{8,2},{9,5},... | collective-permute-start | bytes 221192 | tf_op jit(solution)/shard_map/ppermute | solution.py:244
  6.2 4.6 %collective-permute-start.1 = (bf16[4,9216]{1,0:T(4,128)(2,1)S(1)}, bf16[4,9216]{1,0:T(4,128)(2,1)S(1)}, u32[]{:S(2)}, u32[]{:S(2)}) collective-permute-start(bf16[4,9216]{1,0:T(4,128)(2,1)S(1)} %join.1), channel_id=1, source_target_pairs={{0,8},{1,15},{2,10},{3,13},{4,12},{5,9},{6,14},{7,11},{8,0},{9,7},... | collective-permute-start | bytes 221192 | tf_op jit(solution)/shard_map/ppermute | solution.py:244
  10.9 2.3 %collective-permute-start.3 = (bf16[8,8192]{1,0:T(8,128)(2,1)S(1)}, bf16[8,8192]{1,0:T(8,128)(2,1)S(1)}, u32[]{:S(2)}, u32[]{:S(2)}) collective-permute-start(bf16[8,8192]{1,0:T(8,128)(2,1)S(1)} %get-tuple-element.25.near_ref.after), channel_id=1, source_target_pairs={{0,1},{1,0},{2,3},{3,2},{4,5},{5,4},{6,7},{7,6},{8,9},{9,8},{10,11... | collective-permute-start | bytes 393224 | tf_op jit(solution)/shard_map/ppermute | solution.py:258
  15.7 1.4 %collective-permute-start.5 = (f32[8,4096]{1,0:T(8,128)S(1)}, f32[8,4096]{1,0:T(8,128)S(1)}, u32[]{:S(2)}, u32[]{:S(2)}) collective-permute-start(f32[8,4096]{1,0:T(8,128)S(1)} %get-tuple-element.34), channel_id=1, source_target_pairs={{0,1},{1,0},{2,3},{3,2},{4,5},{5,4},{6,7},{7,6},{8,9},{9,8},{10,11... | collective-permute-start | bytes 393224 | tf_op jit(solution)/shard_map/ppermute | solution.py:258
  17.1 5.7 %collective-permute-start.6 = (bf16[4,4096]{1,0:T(4,128)(2,1)S(1)}, bf16[4,4096]{1,0:T(4,128)(2,1)S(1)}, u32[]{:S(2)}, u32[]{:S(2)}) collective-permute-start(bf16[4,4096]{1,0:T(4,128)(2,1)S(1)} %get-tuple-element.36), channel_id=1, source_target_pairs={{0,4},{1,3},{2,6},{3,5},{4,0},{5,7},{6,2},{7,1},{8,28},{9,27},{10,... | collective-permute-start | bytes 98312 | tf_op jit(solution)/shard_map/ppermute | solution.py:252
  18.9 3.9 %collective-permute-start.7 = (bf16[4,4096]{1,0:T(4,128)(2,1)S(1)}, bf16[4,4096]{1,0:T(4,128)(2,1)S(1)}, u32[]{:S(2)}, u32[]{:S(2)}) collective-permute-start(bf16[4,4096]{1,0:T(4,128)(2,1)S(1)} %get-tuple-element.35.local_ref), channel_id=1, source_target_pairs={{0,16},{1,7},{2,18},{3,1},{4,20},{5,3},{6,22},{7,5},{8,24},{9,31},... | collective-permute-start | bytes 98312 | tf_op jit(solution)/shard_map/ppermute | solution.py:252
  20.4 2.5 %collective-permute-start.4 = (bf16[2,10240]{1,0:T(2,128)(2,1)S(1)}, bf16[2,10240]{1,0:T(2,128)(2,1)S(1)}, u32[]{:S(2)}, u32[]{:S(2)}) collective-permute-start(bf16[2,10240]{1,0:T(2,128)(2,1)S(1)} %get-tuple-element.27.stayed_ref), channel_id=1, source_target_pairs={{0,1},{1,0},{2,3},{3,2},{4,5},{5,4},{6,7},{7,6},{8,24},{9,25},{10,... | collective-permute-start | bytes 122888 | tf_op jit(solution)/shard_map/ppermute | solution.py:255
  22.9 1.3 %collective-permute-start.8 = (f32[2,4096]{1,0:T(2,128)S(1)}, f32[2,4096]{1,0:T(2,128)S(1)}, u32[]{:S(2)}, u32[]{:S(2)}) collective-permute-start(f32[2,4096]{1,0:T(2,128)S(1)} %get-tuple-element.38), channel_id=1, source_target_pairs={{0,1},{1,0},{2,3},{3,2},{4,5},{5,4},{6,7},{7,6},{8,9},{9,8},{10,11... | collective-permute-start | bytes 98312 | tf_op jit(solution)/shard_map/ppermute | solution.py:258

commit v8 on v7

--- a/solution.py
+++ b/solution.py
@@ -56,14 +56,10 @@
     return jnp.dot(left, weight, preferred_element_type=jnp.float32)
 
 
-def prepare(saved_hbm, grad_hbm, gain_hbm, sent_ref, gain_ref, sems):
-    slots, r, d = saved_hbm.shape[1:]
+def prepare(saved_hbm, grad_hbm, gain_hbm, saved_ref, grad_ref, gain_ref, sems):
     copies = [
-        pltpu.make_async_copy(saved_hbm.at[0, n], sent_ref.at[:, pl.ds(n * d, d)], sems.at[n]) for n in range(slots)
-    ]
-    copies += [
-        pltpu.make_async_copy(grad_hbm.at[0], sent_ref.at[:, pl.ds(slots * d, d)], sems.at[slots]),
-        pltpu.make_async_copy(gain_hbm, gain_ref, sems.at[slots + 1]),
+        pltpu.make_async_copy(src, dst, sems.at[n])
+        for n, (src, dst) in enumerate(((saved_hbm, saved_ref), (grad_hbm, grad_ref), (gain_hbm, gain_ref)))
     ]
     for copy in copies:
         copy.start()
@@ -71,15 +67,14 @@
         copy.wait()
 
 
-def join(slot_ref, mine_ref, other_ref, gain_ref, rows_ref):
-    r, d = mine_ref.shape[0], gain_ref.shape[1]
-    first = on_first_core()
-    slot = pl.ds(pl.multiple_of(slot_ref[0] * d, d), d)
-    grad = pl.ds(mine_ref.shape[1] - d, d)
-    for part, at in ((slot, 0), (grad, d)):
-        mine, other = mine_ref[:, part], other_ref[:, part]
-        rows_ref[:r, at : at + d] = jnp.where(first, mine, other)
-        rows_ref[r:, at : at + d] = jnp.where(first, other, mine)
+def join(slot_ref, saved_ref, other_saved_ref, grad_ref, other_grad_ref, gain_ref, rows_ref):
+    r, d = grad_ref.shape[1:]
+    first = on_first_core()
+    slot = slot_ref[0]
+    pairs = ((saved_ref[0, slot], other_saved_ref[0, slot]), (grad_ref[0], other_grad_ref[0]))
+    for at, (mine, other) in enumerate(pairs):
+        rows_ref[:r, at * d : (at + 1) * d] = jnp.where(first, mine, other)
+        rows_ref[r:, at * d : (at + 1) * d] = jnp.where(first, other, mine)
     piece = rows_ref.shape[1] - 2 * d
     for n in range(rows_ref.shape[0]):
         rows_ref[n : n + 1, 2 * d :] = gain_ref[:, n * piece : (n + 1) * piece]
@@ -257,24 +252,23 @@
     def to_core(x):
         return lax.ppermute(x, "seqtp", [(i, i ^ 1) for i in range(members)])
 
-    slots = saved_in.shape[1]
-    sent, gain_row = pl.pallas_call(
+    saved, grads, gain_row = pl.pallas_call(
         prepare,
-        out_shape=[VMEM((r, (slots + 1) * d), bf16), VMEM(gain.shape, bf16)],
+        out_shape=[VMEM(saved_in.shape, bf16), VMEM(grad_in.shape, bf16), VMEM(gain.shape, bf16)],
         in_specs=anywhere(3),
-        out_specs=whole(2),
-        scratch_shapes=[pltpu.SemaphoreType.DMA((slots + 2,))],
+        out_specs=whole(3),
+        scratch_shapes=[pltpu.SemaphoreType.DMA((3,))],
         compiler_params=params(4),
         name="prepare",
     )(*far_off(saved_in, grad_in, gain))
     chip_rows = pl.pallas_call(
         join,
         out_shape=VMEM((CORES * r, 2 * d + d // (CORES * r)), bf16),
-        in_specs=[pl.BlockSpec(memory_space=pltpu.SMEM)] + whole(3),
+        in_specs=[pl.BlockSpec(memory_space=pltpu.SMEM)] + whole(5),
         out_specs=pl.BlockSpec(memory_space=VMEM),
         compiler_params=params(4),
         name="join",
-    )(slot_table, *near_core(sent, to_core(sent), gain_row))
+    )(slot_table, *near_core(saved, to_core(saved_in), grads, to_core(grad_in), gain_row))
     both, gate_turned, up_turned, down = pl.pallas_call(
         fetch,
         out_shape=[VMEM((d, 2 * hidden), bf16)] + [VMEM((hidden, d), bf16)] * 3,

time: 25.4 us -> 24.9 us (0.980)
  waiting for transfers between devices: 4.83 us -> 4.41 us
    ppermute x4 -> x5, waiting for transfers between devices: 2.56 us -> 2.3 us  [to_core(): return lax.ppermute(x, 'seqtp', [(i, i ^ 1) for i in range(members)])]
    ppermute x4 -> x5, starting transfers between devices: 2.33 us -> 2.32 us  [to_core(): return lax.ppermute(x, 'seqtp', [(i, i ^ 1) for i in range(members)])]
  transfers between devices with their start and end apart: 9 -> 10, of which waited for: 6 -> 5; matrix products, arithmetic and copies ran while one was open for 0% -> 0% of each run, Pallas kernels for 19% -> 23%
where the time goes in v8:
time: 24.9 us; the launch traced here: 24.7 us
  starting transfers between devices  10.5 us (42%)
  Pallas kernels  9.06 us (36%)
  waiting for transfers between devices  4.41 us (18%)
  between operations  0.74 us (3%)
    ppermute x2, starting transfers between devices, ahead(): return lax.ppermute(x, ('section', 'seqtp'), route(goal))  4.54 us
    pallas_call x1, Pallas kernels, on_device(): pl.pallas_call(fetch, out_shape=[VMEM((d, 2 * hidden), bf16)] + [VMEM((hi...  3.87 us
    ppermute x2, starting transfers between devices, home(): return lax.ppermute(x, ('section', 'seqtp'), route(goal))  3.35 us
    ppermute x5, starting transfers between devices, to_core(): return lax.ppermute(x, 'seqtp', [(i, i ^ 1) for i in range(members)])  2.32 us
    ppermute x5, waiting for transfers between devices, to_core(): return lax.ppermute(x, 'seqtp', [(i, i ^ 1) for i in range(members)])  2.3 us
    pallas_call x1, Pallas kernels, on_device(): pl.pallas_call(functools.partial(expert, CORES * r), out_shape=[VMEM((row...  2.22 us
    ppermute x2, waiting for transfers between devices, home(): return lax.ppermute(x, ('section', 'seqtp'), route(goal))  2.07 us
    pallas_call x1, Pallas kernels, on_device(): pl.pallas_call(functools.partial(finish, stays), out_shape=jax.ShapeDtype...  0.88 us
  transfers between devices with their start and end apart: 10, of which 5 were waited for; matrix products, arithmetic and copies ran while one was open for 0% of the time, Pallas kernels for 23%

profile of v8, /device:TPU:0, one launch (start us, length us, event | category | flops | bytes accessed | tf_op | source)
XLA Modules:
  0.0 24.7 jit_solution(5185671916977824125)
XLA Ops:
  0.0 0.5 %collective-permute-start = (bf16[1,4,2,4096]{3,2,1,0:T(2,128)(2,1)}, bf16[1,4,2,4096]{3,2,1,0:T(2,128)(2,1)S(1)}, u32[]{:S(2)}, u32[]{:S(2)}) collective-permute-start(bf16[1,4,2,4096]{3,2,1,0:T(2,128)(2,1)} %saved_hbm.1), channel_id=1, source_target_pairs={{0,1},{1,0},{2,3},{3,2},{4,5},{5,4},{6,7},{7,6},{8,9},{9,8},{10,11... | collective-permute-start | bytes 196616 | tf_op jit(solution)/shard_map/ppermute | solution.py:253
  0.5 0.1 collective-permute-start.1
  1.2 0.9 %prepare.1 = (bf16[1,4,2,4096]{3,2,1,0:T(2,128)(2,1)S(1)}, bf16[1,2,4096]{2,1,0:T(2,128)(2,1)S(1)}, bf16[1,4096]{1,0:T(2,128)(2,1)S(1)}) custom-call(bf16[1,4,2,4096]{3,2,1,0:T(2,128)(2,1)} %saved_hbm.1, bf16[1,2,4096]{2,1,0:T(2,128)(2,1)} %grad_hbm.1, bf16[1,4096]{1,0:T(2,128)(2,1)} %gain_hbm.1), custom_call_target="tpu_custom_call" | custom-call | tf_op jit(solution)/shard_map/prepare/pallas_call | solution.py:255
  2.0 0.0 collective-permute-done.1.other_grad_ref
  2.1 0.0 collective-permute-done.other_saved_ref
  2.1 4.0 %collective-permute-start.3 = (bf16[4,9216]{1,0:T(4,128)(2,1)S(1)}, bf16[4,9216]{1,0:T(4,128)(2,1)S(1)}, u32[]{:S(2)}, u32[]{:S(2)}) collective-permute-start(bf16[4,9216]{1,0:T(4,128)(2,1)S(1)} %join.1), channel_id=1, source_target_pairs={{0,10},{1,13},{2,8},{3,15},{4,14},{5,11},{6,12},{7,9},{8,2},{9,5},... | collective-permute-start | bytes 221192 | tf_op jit(solution)/shard_map/ppermute | solution.py:239
  6.1 0.5 %collective-permute-start.2 = (bf16[4,9216]{1,0:T(4,128)(2,1)S(1)}, bf16[4,9216]{1,0:T(4,128)(2,1)S(1)}, u32[]{:S(2)}, u32[]{:S(2)}) collective-permute-start(bf16[4,9216]{1,0:T(4,128)(2,1)S(1)} %join.1), channel_id=1, source_target_pairs={{0,8},{1,15},{2,10},{3,13},{4,12},{5,9},{6,14},{7,11},{8,0},{9,7},... | collective-permute-start | bytes 221192 | tf_op jit(solution)/shard_map/ppermute | solution.py:239
  6.6 3.9 %fetch.1 = (bf16[4096,768]{1,0:T(8,128)(2,1)S(1)}, bf16[384,4096]{1,0:T(8,128)(2,1)S(1)}, bf16[384,4096]{1,0:T(8,128)(2,1)S(1)}, bf16[384,4096]{1,0:T(8,128)(2,1)S(1)}) custom-call(bf16[4096,384]{1,0:T(8,128)(2,1)} %gate_hbm.1, bf16[4096,384]{1,0:T(8,128)(2,1)} %up_hbm.1, bf16[384,4096]{1,0:T(8,128)(2,1)} %down_hbm.1), custom_call_target="tpu_custom_call" | custom-call | bytes 18874368 | tf_op jit(solution)/shard_map/fetch/pallas_call | solution.py:272
  10.5 0.0 collective-permute-done.3.refs_1_
  10.5 0.0 collective-permute-done.2.refs_0_
  10.6 0.1 collect.1
  10.6 1.3 %collective-permute-start.4 = (bf16[8,8192]{1,0:T(8,128)(2,1)S(1)}, bf16[8,8192]{1,0:T(8,128)(2,1)S(1)}, u32[]{:S(2)}, u32[]{:S(2)}) collective-permute-start(bf16[8,8192]{1,0:T(8,128)(2,1)S(1)} %get-tuple-element.27.near_ref.after), channel_id=1, source_target_pairs={{0,1},{1,0},{2,3},{3,2},{4,5},{5,4},{6,7},{7,6},{8,9},{9,8},{10,11... | collective-permute-start | bytes 393224 | tf_op jit(solution)/shard_map/ppermute | solution.py:253
  12.0 0.9 %turn.1.down_ref = bf16[4096,384]{1,0:T(8,128)(2,1)S(1)} custom-call(bf16[384,4096]{1,0:T(8,128)(2,1)S(1)} %get-tuple-element.34.down_ref, bf16[8,8192]{1,0:T(8,128)(2,1)S(1)} %get-tuple-element.27.near_ref.after), custom_call_target="tpu_custom_call" | custom-call | bytes 6291456 | tf_op jit(solution)/shard_map/turn/pallas_call | solution.py:293
  12.8 0.1 collective-permute-done.4.far_ref
  13.0 0.2 arrange.1
  13.1 2.2 %expert.1 = (f32[8,4096]{1,0:T(8,128)S(1)}, f32[8,4096]{1,0:T(8,128)S(1)}) custom-call(bf16[16,4096]{1,0:T(8,128)(2,1)S(1)} %get-tuple-element.30.normed_ref, bf16[16,4096]{1,0:T(8,128)(2,1)S(1)} %get-tuple-element.31.grad_ref, bf16[4096,768]{1,0:T(8,128)(2,1)S(1)} %get-tuple-element.26.refs_2_.both_ref, bf16[384,4096]{1,0:T(8,128)(2,1)S(1)} %get-tuple-element.32.gate_ref, ...), custom_call_target="tpu_custom_call" | custom-call | tf_op jit(solution)/shard_map/expert/pallas_call | solution.py:311
  15.4 0.4 %collective-permute-start.6 = (f32[8,4096]{1,0:T(8,128)S(1)}, f32[8,4096]{1,0:T(8,128)S(1)}, u32[]{:S(2)}, u32[]{:S(2)}) collective-permute-start(f32[8,4096]{1,0:T(8,128)S(1)} %get-tuple-element.36), channel_id=1, source_target_pairs={{0,1},{1,0},{2,3},{3,2},{4,5},{5,4},{6,7},{7,6},{8,9},{9,8},{10,11... | collective-permute-start | bytes 393224 | tf_op jit(solution)/shard_map/ppermute | solution.py:253
  15.8 1.0 %collective-permute-done.6.got_ref = f32[8,4096]{1,0:T(8,128)S(1)} collective-permute-done((f32[8,4096]{1,0:T(8,128)S(1)}, f32[8,4096]{1,0:T(8,128)S(1)}, u32[]{:S(2)}, u32[]{:S(2)}) %collective-permute-start.6) | collective-permute-done | bytes 131104 | tf_op jit(solution)/shard_map/ppermute | solution.py:253
  16.7 0.1 add_cores.1
  16.8 1.8 %collective-permute-start.7 = (bf16[4,4096]{1,0:T(4,128)(2,1)S(1)}, bf16[4,4096]{1,0:T(4,128)(2,1)S(1)}, u32[]{:S(2)}, u32[]{:S(2)}) collective-permute-start(bf16[4,4096]{1,0:T(4,128)(2,1)S(1)} %get-tuple-element.38), channel_id=1, source_target_pairs={{0,4},{1,3},{2,6},{3,5},{4,0},{5,7},{6,2},{7,1},{8,28},{9,27},{10,... | collective-permute-start | bytes 98312 | tf_op jit(solution)/shard_map/ppermute | solution.py:247
  18.6 1.5 %collective-permute-start.8 = (bf16[4,4096]{1,0:T(4,128)(2,1)S(1)}, bf16[4,4096]{1,0:T(4,128)(2,1)S(1)}, u32[]{:S(2)}, u32[]{:S(2)}) collective-permute-start(bf16[4,4096]{1,0:T(4,128)(2,1)S(1)} %get-tuple-element.37.local_ref), channel_id=1, source_target_pairs={{0,16},{1,7},{2,18},{3,1},{4,20},{5,3},{6,22},{7,5},{8,24},{9,31},... | collective-permute-start | bytes 98312 | tf_op jit(solution)/shard_map/ppermute | solution.py:247
  20.2 0.3 %collective-permute-start.5 = (bf16[2,10240]{1,0:T(2,128)(2,1)S(1)}, bf16[2,10240]{1,0:T(2,128)(2,1)S(1)}, u32[]{:S(2)}, u32[]{:S(2)}) collective-permute-start(bf16[2,10240]{1,0:T(2,128)(2,1)S(1)} %get-tuple-element.29.stayed_ref), channel_id=1, source_target_pairs={{0,1},{1,0},{2,3},{3,2},{4,5},{5,4},{6,7},{7,6},{8,24},{9,25},{10,... | collective-permute-start | bytes 122888 | tf_op jit(solution)/shard_map/ppermute | solution.py:250
  20.5 1.8 %collective-permute-done.7.refs_0_ = bf16[4,4096]{1,0:T(4,128)(2,1)S(1)} collective-permute-done((bf16[4,4096]{1,0:T(4,128)(2,1)S(1)}, bf16[4,4096]{1,0:T(4,128)(2,1)S(1)}, u32[]{:S(2)}, u32[]{:S(2)}) %collective-permute-start.7) | collective-permute-done | bytes 32800 | tf_op jit(solution)/shard_map/ppermute | solution.py:247
  22.2 0.3 %collective-permute-done.8.refs_1_ = bf16[4,4096]{1,0:T(4,128)(2,1)S(1)} collective-permute-done((bf16[4,4096]{1,0:T(4,128)(2,1)S(1)}, bf16[4,4096]{1,0:T(4,128)(2,1)S(1)}, u32[]{:S(2)}, u32[]{:S(2)}) %collective-permute-start.8) | collective-permute-done | bytes 32800 | tf_op jit(solution)/shard_map/ppermute | solution.py:247
  22.6 0.1 collective-permute-start.9
  22.7 0.0 collective-permute-done.5.moved_ref
  22.7 1.2 %collective-permute-done.9.got_ref = f32[2,4096]{1,0:T(2,128)S(1)} collective-permute-done((f32[2,4096]{1,0:T(2,128)S(1)}, f32[2,4096]{1,0:T(2,128)S(1)}, u32[]{:S(2)}, u32[]{:S(2)}) %collective-permute-start.9) | collective-permute-done | bytes 32800 | tf_op jit(solution)/shard_map/ppermute | solution.py:253
  23.9 0.9 %finish.1 = bf16[1,2,4096]{2,1,0:T(2,128)(2,1)} custom-call(bf16[2,10240]{1,0:T(2,128)(2,1)S(1)} %get-tuple-element.29.stayed_ref, bf16[2,10240]{1,0:T(2,128)(2,1)S(1)} %collective-permute-done.5.moved_ref, f32[2,4096]{1,0:T(2,128)S(1)} %get-tuple-element.39.keep_ref, f32[2,4096]{1,0:T(2,128)S(1)} %collective-permute-done.9.got_ref), custom_call_target="tpu_custom_call" | custom-call | tf_op jit(solution)/shard_map/finish/pallas_call | solution.py:337
  (2 shorter events, 0.1 us)
Async XLA Ops:
  0.0 2.1 %collective-permute-start = (bf16[1,4,2,4096]{3,2,1,0:T(2,128)(2,1)}, bf16[1,4,2,4096]{3,2,1,0:T(2,128)(2,1)S(1)}, u32[]{:S(2)}, u32[]{:S(2)}) collective-permute-start(bf16[1,4,2,4096]{3,2,1,0:T(2,128)(2,1)} %saved_hbm.1), channel_id=1, source_target_pairs={{0,1},{1,0},{2,3},{3,2},{4,5},{5,4},{6,7},{7,6},{8,9},{9,8},{10,11... | collective-permute-start | bytes 196616 | tf_op jit(solution)/shard_map/ppermute | solution.py:253
  0.5 1.6 %collective-permute-start.1 = (bf16[1,2,4096]{2,1,0:T(2,128)(2,1)}, bf16[1,2,4096]{2,1,0:T(2,128)(2,1)S(1)}, u32[]{:S(2)}, u32[]{:S(2)}) collective-permute-start(bf16[1,2,4096]{2,1,0:T(2,128)(2,1)} %grad_hbm.1), channel_id=1, source_target_pairs={{0,1},{1,0},{2,3},{3,2},{4,5},{5,4},{6,7},{7,6},{8,9},{9,8},{10,11... | collective-permute-start | bytes 49160 | tf_op jit(solution)/shard_map/ppermute | solution.py:253
  2.1 8.4 %collective-permute-start.3 = (bf16[4,9216]{1,0:T(4,128)(2,1)S(1)}, bf16[4,9216]{1,0:T(4,128)(2,1)S(1)}, u32[]{:S(2)}, u32[]{:S(2)}) collective-permute-start(bf16[4,9216]{1,0:T(4,128)(2,1)S(1)} %join.1), channel_id=1, source_target_pairs={{0,10},{1,13},{2,8},{3,15},{4,14},{5,11},{6,12},{7,9},{8,2},{9,5},... | collective-permute-start | bytes 221192 | tf_op jit(solution)/shard_map/ppermute | solution.py:239
  6.1 4.5 %collective-permute-start.2 = (bf16[4,9216]{1,0:T(4,128)(2,1)S(1)}, bf16[4,9216]{1,0:T(4,128)(2,1)S(1)}, u32[]{:S(2)}, u32[]{:S(2)}) collective-permute-start(bf16[4,9216]{1,0:T(4,128)(2,1)S(1)} %join.1), channel_id=1, source_target_pairs={{0,8},{1,15},{2,10},{3,13},{4,12},{5,9},{6,14},{7,11},{8,0},{9,7},... | collective-permute-start | bytes 221192 | tf_op jit(solution)/shard_map/ppermute | solution.py:239
  10.6 2.3 %collective-permute-start.4 = (bf16[8,8192]{1,0:T(8,128)(2,1)S(1)}, bf16[8,8192]{1,0:T(8,128)(2,1)S(1)}, u32[]{:S(2)}, u32[]{:S(2)}) collective-permute-start(bf16[8,8192]{1,0:T(8,128)(2,1)S(1)} %get-tuple-element.27.near_ref.after), channel_id=1, source_target_pairs={{0,1},{1,0},{2,3},{3,2},{4,5},{5,4},{6,7},{7,6},{8,9},{9,8},{10,11... | collective-permute-start | bytes 393224 | tf_op jit(solution)/shard_map/ppermute | solution.py:253
  15.4 1.4 %collective-permute-start.6 = (f32[8,4096]{1,0:T(8,128)S(1)}, f32[8,4096]{1,0:T(8,128)S(1)}, u32[]{:S(2)}, u32[]{:S(2)}) collective-permute-start(f32[8,4096]{1,0:T(8,128)S(1)} %get-tuple-element.36), channel_id=1, source_target_pairs={{0,1},{1,0},{2,3},{3,2},{4,5},{5,4},{6,7},{7,6},{8,9},{9,8},{10,11... | collective-permute-start | bytes 393224 | tf_op jit(solution)/shard_map/ppermute | solution.py:253
  16.8 5.4 %collective-permute-start.7 = (bf16[4,4096]{1,0:T(4,128)(2,1)S(1)}, bf16[4,4096]{1,0:T(4,128)(2,1)S(1)}, u32[]{:S(2)}, u32[]{:S(2)}) collective-permute-start(bf16[4,4096]{1,0:T(4,128)(2,1)S(1)} %get-tuple-element.38), channel_id=1, source_target_pairs={{0,4},{1,3},{2,6},{3,5},{4,0},{5,7},{6,2},{7,1},{8,28},{9,27},{10,... | collective-permute-start | bytes 98312 | tf_op jit(solution)/shard_map/ppermute | solution.py:247
  18.6 3.9 %collective-permute-start.8 = (bf16[4,4096]{1,0:T(4,128)(2,1)S(1)}, bf16[4,4096]{1,0:T(4,128)(2,1)S(1)}, u32[]{:S(2)}, u32[]{:S(2)}) collective-permute-start(bf16[4,4096]{1,0:T(4,128)(2,1)S(1)} %get-tuple-element.37.local_ref), channel_id=1, source_target_pairs={{0,16},{1,7},{2,18},{3,1},{4,20},{5,3},{6,22},{7,5},{8,24},{9,31},... | collective-permute-start | bytes 98312 | tf_op jit(solution)/shard_map/ppermute | solution.py:247
  20.2 2.5 %collective-permute-start.5 = (bf16[2,10240]{1,0:T(2,128)(2,1)S(1)}, bf16[2,10240]{1,0:T(2,128)(2,1)S(1)}, u32[]{:S(2)}, u32[]{:S(2)}) collective-permute-start(bf16[2,10240]{1,0:T(2,128)(2,1)S(1)} %get-tuple-element.29.stayed_ref), channel_id=1, source_target_pairs={{0,1},{1,0},{2,3},{3,2},{4,5},{5,4},{6,7},{7,6},{8,24},{9,25},{10,... | collective-permute-start | bytes 122888 | tf_op jit(solution)/shard_map/ppermute | solution.py:250
  22.6 1.3 %collective-permute-start.9 = (f32[2,4096]{1,0:T(2,128)S(1)}, f32[2,4096]{1,0:T(2,128)S(1)}, u32[]{:S(2)}, u32[]{:S(2)}) collective-permute-start(f32[2,4096]{1,0:T(2,128)S(1)} %get-tuple-element.40), channel_id=1, source_target_pairs={{0,1},{1,0},{2,3},{3,2},{4,5},{5,4},{6,7},{7,6},{8,9},{9,8},{10,11... | collective-permute-start | bytes 98312 | tf_op jit(solution)/shard_map/ppermute | solution.py:253

commit v9 on v8

--- a/solution.py
+++ b/solution.py
@@ -56,10 +56,17 @@
     return jnp.dot(left, weight, preferred_element_type=jnp.float32)
 
 
-def prepare(saved_hbm, grad_hbm, gain_hbm, saved_ref, grad_ref, gain_ref, sems):
+def prepare(slot_ref, saved_hbm, grad_hbm, gain_hbm, mine_ref, gain_ref, sems):
+    d = grad_hbm.shape[-1]
     copies = [
         pltpu.make_async_copy(src, dst, sems.at[n])
-        for n, (src, dst) in enumerate(((saved_hbm, saved_ref), (grad_hbm, grad_ref), (gain_hbm, gain_ref)))
+        for n, (src, dst) in enumerate(
+            (
+                (saved_hbm.at[0, slot_ref[0]], mine_ref.at[:, pl.ds(0, d)]),
+                (grad_hbm.at[0], mine_ref.at[:, pl.ds(d, d)]),
+                (gain_hbm, gain_ref),
+            )
+        )
     ]
     for copy in copies:
         copy.start()
@@ -67,14 +74,14 @@
         copy.wait()
 
 
-def join(slot_ref, saved_ref, other_saved_ref, grad_ref, other_grad_ref, gain_ref, rows_ref):
+def join(slot_ref, mine_ref, saved_ref, grad_ref, gain_ref, rows_ref):
     r, d = grad_ref.shape[1:]
     first = on_first_core()
-    slot = slot_ref[0]
-    pairs = ((saved_ref[0, slot], other_saved_ref[0, slot]), (grad_ref[0], other_grad_ref[0]))
-    for at, (mine, other) in enumerate(pairs):
-        rows_ref[:r, at * d : (at + 1) * d] = jnp.where(first, mine, other)
-        rows_ref[r:, at * d : (at + 1) * d] = jnp.where(first, other, mine)
+    for at, other in enumerate((saved_ref[0, slot_ref[0]], grad_ref[0])):
+        part = slice(at * d, (at + 1) * d)
+        mine = mine_ref[:, part]
+        rows_ref[:r, part] = jnp.where(first, mine, other)
+        rows_ref[r:, part] = jnp.where(first, other, mine)
     piece = rows_ref.shape[1] - 2 * d
     for n in range(rows_ref.shape[0]):
         rows_ref[n : n + 1, 2 * d :] = gain_ref[:, n * piece : (n + 1) * piece]
@@ -184,19 +191,26 @@
     send_ref[...] = jnp.where(first, total[r:], total[:r])
 
 
-def finish(stays, stayed_ref, moved_ref, keep_ref, got_ref, out_ref, gain_ref):
+def settle(stays, stayed_ref, moved_ref, keep_ref, unit_ref, gain_ref, kept_ref, base_ref, recip_ref):
     r, d = keep_ref.shape
     here = stays(lax.axis_index("section"))
     own = jnp.where(here, stayed_ref[...].astype(jnp.float32), moved_ref[...].astype(jnp.float32))
     piece = d // r
     for n in range(r):
         gain_ref[:, n * piece : (n + 1) * piece] = own[n : n + 1, 2 * d :]
-    wide, grad = own[:, :d], own[:, d : 2 * d]
+    wide = own[:, :d]
     recip = lax.rsqrt(jnp.mean(wide * wide, axis=-1, keepdims=True) + EPS)
-    scaled = gain_ref[...] * (keep_ref[...] + got_ref[...])
-    unit = wide * recip
+    unit_ref[...] = wide * recip
+    kept_ref[...] = gain_ref[...] * keep_ref[...]
+    base_ref[...] = own[:, d : 2 * d]
+    recip_ref[...] = jnp.broadcast_to(recip, recip_ref.shape)
+
+
+def finish(unit_ref, gain_ref, kept_ref, base_ref, recip_ref, got_ref, out_ref):
+    unit, recip = unit_ref[...], recip_ref[:, :1]
+    scaled = kept_ref[...] + gain_ref[...] * got_ref[...]
     mean = jnp.mean(scaled * unit, axis=-1, keepdims=True)
-    out_ref[0] = (grad + recip * (scaled - unit * mean)).astype(out_ref.dtype)
+    out_ref[0] = (base_ref[...] + recip * (scaled - unit * mean)).astype(out_ref.dtype)
 
 
 def on_device(sections, members, saved_in, grad_in, slot_table, gain, w_gate, w_up, w_down):
@@ -252,23 +266,24 @@
     def to_core(x):
         return lax.ppermute(x, "seqtp", [(i, i ^ 1) for i in range(members)])
 
-    saved, grads, gain_row = pl.pallas_call(
+    scalar = pl.BlockSpec(memory_space=pltpu.SMEM)
+    mine, gain_row = pl.pallas_call(
         prepare,
-        out_shape=[VMEM(saved_in.shape, bf16), VMEM(grad_in.shape, bf16), VMEM(gain.shape, bf16)],
-        in_specs=anywhere(3),
-        out_specs=whole(3),
+        out_shape=[VMEM((r, 2 * d), bf16), VMEM(gain.shape, bf16)],
+        in_specs=[scalar] + anywhere(3),
+        out_specs=whole(2),
         scratch_shapes=[pltpu.SemaphoreType.DMA((3,))],
         compiler_params=params(4),
         name="prepare",
-    )(*far_off(saved_in, grad_in, gain))
+    )(slot_table, *far_off(saved_in, grad_in, gain))
     chip_rows = pl.pallas_call(
         join,
         out_shape=VMEM((CORES * r, 2 * d + d // (CORES * r)), bf16),
-        in_specs=[pl.BlockSpec(memory_space=pltpu.SMEM)] + whole(5),
+        in_specs=[scalar] + whole(4),
         out_specs=pl.BlockSpec(memory_space=VMEM),
         compiler_params=params(4),
         name="join",
-    )(slot_table, *near_core(saved, to_core(saved_in), grads, to_core(grad_in), gain_row))
+    )(slot_table, *near_core(mine, to_core(saved_in), to_core(grad_in), gain_row))
     both, gate_turned, up_turned, down = pl.pallas_call(
         fetch,
         out_shape=[VMEM((d, 2 * hidden), bf16)] + [VMEM((hidden, d), bf16)] * 3,
@@ -334,15 +349,22 @@
         compiler_params=params(4),
         name="add_chips",
     )(*near_core(sums[-1], *landed))
+    settled = pl.pallas_call(
+        functools.partial(settle, stays),
+        out_shape=[VMEM(dims, f32) for dims in ((r, d), (1, d), (r, d), (r, d), (r, 128))],
+        in_specs=whole(3),
+        out_specs=whole(5),
+        compiler_params=params(4),
+        name="settle",
+    )(*near_core(own, moved, keep))
     return pl.pallas_call(
-        functools.partial(finish, stays),
+        finish,
         out_shape=jax.ShapeDtypeStruct((1, r, d), bf16),
-        in_specs=whole(4),
+        in_specs=whole(6),
         out_specs=pl.BlockSpec(memory_space=VMEM),
-        scratch_shapes=[VMEM((1, d), f32)],
         compiler_params=params(4),
         name="finish",
-    )(*near_core(own, moved, keep, to_core(send)))
+    )(*near_core(*settled, to_core(send)))
 
 
 def solution(mesh):

time: 24.9 us -> 24.9 us (level)
    pallas_call x2 -> x3, Pallas kernels: 1.75 us -> 1.68 us  [the longest x1 0.78 us: on_device(): pl.pallas_call(prepare, out_shape=[VMEM((r, 2 * d), bf16), VMEM(gain.shap...]
where the time goes in v9:
time: 24.9 us; the launch traced here: 24.5 us
  starting transfers between devices  10.5 us (42%)
  Pallas kernels  8.99 us (36%)
  waiting for transfers between devices  4.27 us (17%)
  between operations  0.74 us (3%)
    ppermute x2, starting transfers between devices, ahead(): return lax.ppermute(x, ('section', 'seqtp'), route(goal))  4.54 us
    pallas_call x1, Pallas kernels, on_device(): pl.pallas_call(fetch, out_shape=[VMEM((d, 2 * hidden), bf16)] + [VMEM((hi...  3.87 us
    ppermute x2, starting transfers between devices, home(): return lax.ppermute(x, ('section', 'seqtp'), route(goal))  3.35 us
    ppermute x5, starting transfers between devices, to_core(): return lax.ppermute(x, 'seqtp', [(i, i ^ 1) for i in range(members)])  2.32 us
    pallas_call x1, Pallas kernels, on_device(): pl.pallas_call(functools.partial(expert, CORES * r), out_shape=[VMEM((row...  2.22 us
    ppermute x5, waiting for transfers between devices, to_core(): return lax.ppermute(x, 'seqtp', [(i, i ^ 1) for i in range(members)])  2.16 us
    ppermute x2, waiting for transfers between devices, home(): return lax.ppermute(x, ('section', 'seqtp'), route(goal))  2.07 us
    pallas_call x1, Pallas kernels, on_device(): pl.pallas_call(turn, out_shape=VMEM((d, hidden), bf16), in_specs=whole(1)...  0.86 us
  transfers between devices with their start and end apart: 10, of which 5 were waited for; matrix products, arithmetic and copies ran while one was open for 0% of the time, Pallas kernels for 23%

profile of v9, /device:TPU:0, one launch (start us, length us, event | category | flops | bytes accessed | tf_op | source)
XLA Modules:
  0.0 24.5 jit_solution(8828517457794868809)
XLA Ops:
  0.0 0.5 %collective-permute-start = (bf16[1,4,2,4096]{3,2,1,0:T(2,128)(2,1)}, bf16[1,4,2,4096]{3,2,1,0:T(2,128)(2,1)S(1)}, u32[]{:S(2)}, u32[]{:S(2)}) collective-permute-start(bf16[1,4,2,4096]{3,2,1,0:T(2,128)(2,1)} %saved_hbm.1), channel_id=1, source_target_pairs={{0,1},{1,0},{2,3},{3,2},{4,5},{5,4},{6,7},{7,6},{8,9},{9,8},{10,11... | collective-permute-start | bytes 196616 | tf_op jit(solution)/shard_map/ppermute | solution.py:267
  0.5 0.1 collective-permute-start.1
  1.2 0.8 %prepare.1 = (bf16[2,8192]{1,0:T(2,128)(2,1)S(1)}, bf16[1,4096]{1,0:T(2,128)(2,1)S(1)}) custom-call(s32[1]{0:T(128)S(6)} %copy.8.slot_ref, bf16[1,4,2,4096]{3,2,1,0:T(2,128)(2,1)} %saved_hbm.1, bf16[1,2,4096]{2,1,0:T(2,128)(2,1)} %grad_hbm.1, bf16[1,4096]{1,0:T(2,128)(2,1)} %gain_hbm.1), custom_call_target="tpu_custom_call" | custom-call | tf_op jit(solution)/shard_map/prepare/pallas_call | solution.py:270
  1.9 0.0 collective-permute-done.1.grad_ref
  2.0 0.0 collective-permute-done.saved_ref
  2.0 4.0 %collective-permute-start.3 = (bf16[4,9216]{1,0:T(4,128)(2,1)S(1)}, bf16[4,9216]{1,0:T(4,128)(2,1)S(1)}, u32[]{:S(2)}, u32[]{:S(2)}) collective-permute-start(bf16[4,9216]{1,0:T(4,128)(2,1)S(1)} %join.1), channel_id=1, source_target_pairs={{0,10},{1,13},{2,8},{3,15},{4,14},{5,11},{6,12},{7,9},{8,2},{9,5},... | collective-permute-start | bytes 221192 | tf_op jit(solution)/shard_map/ppermute | solution.py:253
  6.0 0.5 %collective-permute-start.2 = (bf16[4,9216]{1,0:T(4,128)(2,1)S(1)}, bf16[4,9216]{1,0:T(4,128)(2,1)S(1)}, u32[]{:S(2)}, u32[]{:S(2)}) collective-permute-start(bf16[4,9216]{1,0:T(4,128)(2,1)S(1)} %join.1), channel_id=1, source_target_pairs={{0,8},{1,15},{2,10},{3,13},{4,12},{5,9},{6,14},{7,11},{8,0},{9,7},... | collective-permute-start | bytes 221192 | tf_op jit(solution)/shard_map/ppermute | solution.py:253
  6.6 3.9 %fetch.1 = (bf16[4096,768]{1,0:T(8,128)(2,1)S(1)}, bf16[384,4096]{1,0:T(8,128)(2,1)S(1)}, bf16[384,4096]{1,0:T(8,128)(2,1)S(1)}, bf16[384,4096]{1,0:T(8,128)(2,1)S(1)}) custom-call(bf16[4096,384]{1,0:T(8,128)(2,1)} %gate_hbm.1, bf16[4096,384]{1,0:T(8,128)(2,1)} %up_hbm.1, bf16[384,4096]{1,0:T(8,128)(2,1)} %down_hbm.1), custom_call_target="tpu_custom_call" | custom-call | bytes 18874368 | tf_op jit(solution)/shard_map/fetch/pallas_call | solution.py:287
  10.4 0.0 collective-permute-done.3.refs_1_
  10.4 0.0 collective-permute-done.2.refs_0_
  10.5 0.1 collect.1
  10.5 1.3 %collective-permute-start.4 = (bf16[8,8192]{1,0:T(8,128)(2,1)S(1)}, bf16[8,8192]{1,0:T(8,128)(2,1)S(1)}, u32[]{:S(2)}, u32[]{:S(2)}) collective-permute-start(bf16[8,8192]{1,0:T(8,128)(2,1)S(1)} %get-tuple-element.30.near_ref.after), channel_id=1, source_target_pairs={{0,1},{1,0},{2,3},{3,2},{4,5},{5,4},{6,7},{7,6},{8,9},{9,8},{10,11... | collective-permute-start | bytes 393224 | tf_op jit(solution)/shard_map/ppermute | solution.py:267
  11.9 0.9 %turn.1.down_ref = bf16[4096,384]{1,0:T(8,128)(2,1)S(1)} custom-call(bf16[384,4096]{1,0:T(8,128)(2,1)S(1)} %get-tuple-element.37.down_ref, bf16[8,8192]{1,0:T(8,128)(2,1)S(1)} %get-tuple-element.30.near_ref.after), custom_call_target="tpu_custom_call" | custom-call | bytes 6291456 | tf_op jit(solution)/shard_map/turn/pallas_call | solution.py:308
  12.7 0.1 collective-permute-done.4.far_ref
  12.9 0.2 arrange.1
  13.1 2.2 %expert.1 = (f32[8,4096]{1,0:T(8,128)S(1)}, f32[8,4096]{1,0:T(8,128)S(1)}) custom-call(bf16[16,4096]{1,0:T(8,128)(2,1)S(1)} %get-tuple-element.33.normed_ref, bf16[16,4096]{1,0:T(8,128)(2,1)S(1)} %get-tuple-element.34.grad_ref, bf16[4096,768]{1,0:T(8,128)(2,1)S(1)} %get-tuple-element.29.refs_2_.both_ref, bf16[384,4096]{1,0:T(8,128)(2,1)S(1)} %get-tuple-element.35.gate_ref, ...), custom_call_target="tpu_custom_call" | custom-call | tf_op jit(solution)/shard_map/expert/pallas_call | solution.py:326
  15.3 0.4 %collective-permute-start.6 = (f32[8,4096]{1,0:T(8,128)S(1)}, f32[8,4096]{1,0:T(8,128)S(1)}, u32[]{:S(2)}, u32[]{:S(2)}) collective-permute-start(f32[8,4096]{1,0:T(8,128)S(1)} %get-tuple-element.39), channel_id=1, source_target_pairs={{0,1},{1,0},{2,3},{3,2},{4,5},{5,4},{6,7},{7,6},{8,9},{9,8},{10,11... | collective-permute-start | bytes 393224 | tf_op jit(solution)/shard_map/ppermute | solution.py:267
  15.7 1.0 %collective-permute-done.6.got_ref = f32[8,4096]{1,0:T(8,128)S(1)} collective-permute-done((f32[8,4096]{1,0:T(8,128)S(1)}, f32[8,4096]{1,0:T(8,128)S(1)}, u32[]{:S(2)}, u32[]{:S(2)}) %collective-permute-start.6) | collective-permute-done | bytes 131104 | tf_op jit(solution)/shard_map/ppermute | solution.py:267
  16.7 0.1 add_cores.1
  16.7 1.8 %collective-permute-start.7 = (bf16[4,4096]{1,0:T(4,128)(2,1)S(1)}, bf16[4,4096]{1,0:T(4,128)(2,1)S(1)}, u32[]{:S(2)}, u32[]{:S(2)}) collective-permute-start(bf16[4,4096]{1,0:T(4,128)(2,1)S(1)} %get-tuple-element.41), channel_id=1, source_target_pairs={{0,4},{1,3},{2,6},{3,5},{4,0},{5,7},{6,2},{7,1},{8,28},{9,27},{10,... | collective-permute-start | bytes 98312 | tf_op jit(solution)/shard_map/ppermute | solution.py:261
  18.5 1.5 %collective-permute-start.8 = (bf16[4,4096]{1,0:T(4,128)(2,1)S(1)}, bf16[4,4096]{1,0:T(4,128)(2,1)S(1)}, u32[]{:S(2)}, u32[]{:S(2)}) collective-permute-start(bf16[4,4096]{1,0:T(4,128)(2,1)S(1)} %get-tuple-element.40.local_ref), channel_id=1, source_target_pairs={{0,16},{1,7},{2,18},{3,1},{4,20},{5,3},{6,22},{7,5},{8,24},{9,31},... | collective-permute-start | bytes 98312 | tf_op jit(solution)/shard_map/ppermute | solution.py:261
  20.1 0.3 %collective-permute-start.5 = (bf16[2,10240]{1,0:T(2,128)(2,1)S(1)}, bf16[2,10240]{1,0:T(2,128)(2,1)S(1)}, u32[]{:S(2)}, u32[]{:S(2)}) collective-permute-start(bf16[2,10240]{1,0:T(2,128)(2,1)S(1)} %get-tuple-element.32.stayed_ref), channel_id=1, source_target_pairs={{0,1},{1,0},{2,3},{3,2},{4,5},{5,4},{6,7},{7,6},{8,24},{9,25},{10,... | collective-permute-start | bytes 122888 | tf_op jit(solution)/shard_map/ppermute | solution.py:264
  20.4 1.8 %collective-permute-done.7.refs_0_ = bf16[4,4096]{1,0:T(4,128)(2,1)S(1)} collective-permute-done((bf16[4,4096]{1,0:T(4,128)(2,1)S(1)}, bf16[4,4096]{1,0:T(4,128)(2,1)S(1)}, u32[]{:S(2)}, u32[]{:S(2)}) %collective-permute-start.7) | collective-permute-done | bytes 32800 | tf_op jit(solution)/shard_map/ppermute | solution.py:261
  22.1 0.3 %collective-permute-done.8.refs_1_ = bf16[4,4096]{1,0:T(4,128)(2,1)S(1)} collective-permute-done((bf16[4,4096]{1,0:T(4,128)(2,1)S(1)}, bf16[4,4096]{1,0:T(4,128)(2,1)S(1)}, u32[]{:S(2)}, u32[]{:S(2)}) %collective-permute-start.8) | collective-permute-done | bytes 32800 | tf_op jit(solution)/shard_map/ppermute | solution.py:261
  22.5 0.1 collective-permute-start.9
  22.6 0.0 collective-permute-done.5.moved_ref
  22.6 0.1 settle.1
  22.7 1.0 %collective-permute-done.9.got_ref = f32[2,4096]{1,0:T(2,128)S(1)} collective-permute-done((f32[2,4096]{1,0:T(2,128)S(1)}, f32[2,4096]{1,0:T(2,128)S(1)}, u32[]{:S(2)}, u32[]{:S(2)}) %collective-permute-start.9) | collective-permute-done | bytes 32800 | tf_op jit(solution)/shard_map/ppermute | solution.py:267
  23.8 0.8 %finish.1 = bf16[1,2,4096]{2,1,0:T(2,128)(2,1)} custom-call(f32[2,4096]{1,0:T(2,128)S(1)} %get-tuple-element.43.unit_ref, f32[1,4096]{1,0:T(1,128)S(1)} %get-tuple-element.44.gain_ref, f32[2,4096]{1,0:T(2,128)S(1)} %get-tuple-element.45.kept_ref, f32[2,4096]{1,0:T(2,128)S(1)} %get-tuple-element.46.base_ref, f32[2,128]{1,0:T(2,128)S(1)} %get-tuple-element.47.recip_ref, ...), custom_call_target="tpu_custom_call" | custom-call | tf_op jit(solution)/shard_map/finish/pallas_call | solution.py:360
  (2 shorter events, 0.1 us)
Async XLA Ops:
  0.0 2.0 %collective-permute-start = (bf16[1,4,2,4096]{3,2,1,0:T(2,128)(2,1)}, bf16[1,4,2,4096]{3,2,1,0:T(2,128)(2,1)S(1)}, u32[]{:S(2)}, u32[]{:S(2)}) collective-permute-start(bf16[1,4,2,4096]{3,2,1,0:T(2,128)(2,1)} %saved_hbm.1), channel_id=1, source_target_pairs={{0,1},{1,0},{2,3},{3,2},{4,5},{5,4},{6,7},{7,6},{8,9},{9,8},{10,11... | collective-permute-start | bytes 196616 | tf_op jit(solution)/shard_map/ppermute | solution.py:267
  0.5 1.5 %collective-permute-start.1 = (bf16[1,2,4096]{2,1,0:T(2,128)(2,1)}, bf16[1,2,4096]{2,1,0:T(2,128)(2,1)S(1)}, u32[]{:S(2)}, u32[]{:S(2)}) collective-permute-start(bf16[1,2,4096]{2,1,0:T(2,128)(2,1)} %grad_hbm.1), channel_id=1, source_target_pairs={{0,1},{1,0},{2,3},{3,2},{4,5},{5,4},{6,7},{7,6},{8,9},{9,8},{10,11... | collective-permute-start | bytes 49160 | tf_op jit(solution)/shard_map/ppermute | solution.py:267
  2.0 8.4 %collective-permute-start.3 = (bf16[4,9216]{1,0:T(4,128)(2,1)S(1)}, bf16[4,9216]{1,0:T(4,128)(2,1)S(1)}, u32[]{:S(2)}, u32[]{:S(2)}) collective-permute-start(bf16[4,9216]{1,0:T(4,128)(2,1)S(1)} %join.1), channel_id=1, source_target_pairs={{0,10},{1,13},{2,8},{3,15},{4,14},{5,11},{6,12},{7,9},{8,2},{9,5},... | collective-permute-start | bytes 221192 | tf_op jit(solution)/shard_map/ppermute | solution.py:253
  6.0 4.5 %collective-permute-start.2 = (bf16[4,9216]{1,0:T(4,128)(2,1)S(1)}, bf16[4,9216]{1,0:T(4,128)(2,1)S(1)}, u32[]{:S(2)}, u32[]{:S(2)}) collective-permute-start(bf16[4,9216]{1,0:T(4,128)(2,1)S(1)} %join.1), channel_id=1, source_target_pairs={{0,8},{1,15},{2,10},{3,13},{4,12},{5,9},{6,14},{7,11},{8,0},{9,7},... | collective-permute-start | bytes 221192 | tf_op jit(solution)/shard_map/ppermute | solution.py:253
  10.5 2.3 %collective-permute-start.4 = (bf16[8,8192]{1,0:T(8,128)(2,1)S(1)}, bf16[8,8192]{1,0:T(8,128)(2,1)S(1)}, u32[]{:S(2)}, u32[]{:S(2)}) collective-permute-start(bf16[8,8192]{1,0:T(8,128)(2,1)S(1)} %get-tuple-element.30.near_ref.after), channel_id=1, source_target_pairs={{0,1},{1,0},{2,3},{3,2},{4,5},{5,4},{6,7},{7,6},{8,9},{9,8},{10,11... | collective-permute-start | bytes 393224 | tf_op jit(solution)/shard_map/ppermute | solution.py:267
  15.3 1.4 %collective-permute-start.6 = (f32[8,4096]{1,0:T(8,128)S(1)}, f32[8,4096]{1,0:T(8,128)S(1)}, u32[]{:S(2)}, u32[]{:S(2)}) collective-permute-start(f32[8,4096]{1,0:T(8,128)S(1)} %get-tuple-element.39), channel_id=1, source_target_pairs={{0,1},{1,0},{2,3},{3,2},{4,5},{5,4},{6,7},{7,6},{8,9},{9,8},{10,11... | collective-permute-start | bytes 393224 | tf_op jit(solution)/shard_map/ppermute | solution.py:267
  16.7 5.4 %collective-permute-start.7 = (bf16[4,4096]{1,0:T(4,128)(2,1)S(1)}, bf16[4,4096]{1,0:T(4,128)(2,1)S(1)}, u32[]{:S(2)}, u32[]{:S(2)}) collective-permute-start(bf16[4,4096]{1,0:T(4,128)(2,1)S(1)} %get-tuple-element.41), channel_id=1, source_target_pairs={{0,4},{1,3},{2,6},{3,5},{4,0},{5,7},{6,2},{7,1},{8,28},{9,27},{10,... | collective-permute-start | bytes 98312 | tf_op jit(solution)/shard_map/ppermute | solution.py:261
  18.5 3.9 %collective-permute-start.8 = (bf16[4,4096]{1,0:T(4,128)(2,1)S(1)}, bf16[4,4096]{1,0:T(4,128)(2,1)S(1)}, u32[]{:S(2)}, u32[]{:S(2)}) collective-permute-start(bf16[4,4096]{1,0:T(4,128)(2,1)S(1)} %get-tuple-element.40.local_ref), channel_id=1, source_target_pairs={{0,16},{1,7},{2,18},{3,1},{4,20},{5,3},{6,22},{7,5},{8,24},{9,31},... | collective-permute-start | bytes 98312 | tf_op jit(solution)/shard_map/ppermute | solution.py:261
  20.1 2.5 %collective-permute-start.5 = (bf16[2,10240]{1,0:T(2,128)(2,1)S(1)}, bf16[2,10240]{1,0:T(2,128)(2,1)S(1)}, u32[]{:S(2)}, u32[]{:S(2)}) collective-permute-start(bf16[2,10240]{1,0:T(2,128)(2,1)S(1)} %get-tuple-element.32.stayed_ref), channel_id=1, source_target_pairs={{0,1},{1,0},{2,3},{3,2},{4,5},{5,4},{6,7},{7,6},{8,24},{9,25},{10,... | collective-permute-start | bytes 122888 | tf_op jit(solution)/shard_map/ppermute | solution.py:264
  22.5 1.3 %collective-permute-start.9 = (f32[2,4096]{1,0:T(2,128)S(1)}, f32[2,4096]{1,0:T(2,128)S(1)}, u32[]{:S(2)}, u32[]{:S(2)}) collective-permute-start(f32[2,4096]{1,0:T(2,128)S(1)} %get-tuple-element.48), channel_id=1, source_target_pairs={{0,1},{1,0},{2,3},{3,2},{4,5},{5,4},{6,7},{7,6},{8,9},{9,8},{10,11... | collective-permute-start | bytes 98312 | tf_op jit(solution)/shard_map/ppermute | solution.py:267

commit v10 on v9

--- a/solution.py
+++ b/solution.py
@@ -166,11 +166,11 @@
         even = total[2 * n * rows : (2 * n + 1) * rows]
         odd = total[(2 * n + 1) * rows : (2 * n + 2) * rows]
         mine_ref[n * rows : (n + 1) * rows] = jnp.where(first, even, odd)
-        other_ref[n * rows : (n + 1) * rows] = jnp.where(first, odd, even)
+        other_ref[n * rows : (n + 1) * rows] = jnp.where(first, odd, even).astype(other_ref.dtype)
 
 
 def add_cores(turns, mine_ref, got_ref, *out_refs):
-    total = (mine_ref[...] + got_ref[...]).astype(jnp.bfloat16)
+    total = (mine_ref[...] + got_ref[...].astype(jnp.float32)).astype(jnp.bfloat16)
     r = out_refs[0].shape[0]
     parts = [total[k * r : (k + 1) * r] for k in range(len(out_refs))]
     first = on_first_core()
@@ -325,7 +325,7 @@
     )(*near_core(block, far, gain_wide))
     mine, other = pl.pallas_call(
         functools.partial(expert, CORES * r),
-        out_shape=[VMEM((rows, d), f32)] * 2,
+        out_shape=[VMEM((rows, d), f32), VMEM((rows, d), bf16)],
         in_specs=whole(6),
         out_specs=whole(2),
         compiler_params=params(16),

time: 24.9 us -> 24.8 us (level)
  no operation moved by 1% of the time
where the time goes in v10:
time: 24.8 us; the launch traced here: 24.4 us
  starting transfers between devices  10.5 us (42%)
  Pallas kernels  9 us (36%)
  waiting for transfers between devices  4.19 us (17%)
  between operations  0.74 us (3%)
    ppermute x2, starting transfers between devices, ahead(): return lax.ppermute(x, ('section', 'seqtp'), route(goal))  4.54 us
    pallas_call x1, Pallas kernels, on_device(): pl.pallas_call(fetch, out_shape=[VMEM((d, 2 * hidden), bf16)] + [VMEM((hi...  3.87 us
    ppermute x2, starting transfers between devices, home(): return lax.ppermute(x, ('section', 'seqtp'), route(goal))  3.35 us
    ppermute x5, starting transfers between devices, to_core(): return lax.ppermute(x, 'seqtp', [(i, i ^ 1) for i in range(members)])  2.32 us
    pallas_call x1, Pallas kernels, on_device(): pl.pallas_call(functools.partial(expert, CORES * r), out_shape=[VMEM((row...  2.22 us
    ppermute x2, waiting for transfers between devices, home(): return lax.ppermute(x, ('section', 'seqtp'), route(goal))  2.08 us
    ppermute x5, waiting for transfers between devices, to_core(): return lax.ppermute(x, 'seqtp', [(i, i ^ 1) for i in range(members)])  2.07 us
    pallas_call x1, Pallas kernels, on_device(): pl.pallas_call(turn, out_shape=VMEM((d, hidden), bf16), in_specs=whole(1)...  0.86 us
  transfers between devices with their start and end apart: 10, of which 5 were waited for; matrix products, arithmetic and copies ran while one was open for 0% of the time, Pallas kernels for 23%

profile of v10, /device:TPU:0, one launch (start us, length us, event | category | flops | bytes accessed | tf_op | source)
XLA Modules:
  0.0 24.4 jit_solution(5240339554772120549)
XLA Ops:
  0.0 0.5 %collective-permute-start = (bf16[1,4,2,4096]{3,2,1,0:T(2,128)(2,1)}, bf16[1,4,2,4096]{3,2,1,0:T(2,128)(2,1)S(1)}, u32[]{:S(2)}, u32[]{:S(2)}) collective-permute-start(bf16[1,4,2,4096]{3,2,1,0:T(2,128)(2,1)} %saved_hbm.1), channel_id=1, source_target_pairs={{0,1},{1,0},{2,3},{3,2},{4,5},{5,4},{6,7},{7,6},{8,9},{9,8},{10,11... | collective-permute-start | bytes 196616 | tf_op jit(solution)/shard_map/ppermute | solution.py:267
  0.5 0.1 collective-permute-start.1
  1.2 0.8 %prepare.1 = (bf16[2,8192]{1,0:T(2,128)(2,1)S(1)}, bf16[1,4096]{1,0:T(2,128)(2,1)S(1)}) custom-call(s32[1]{0:T(128)S(6)} %copy.8.slot_ref, bf16[1,4,2,4096]{3,2,1,0:T(2,128)(2,1)} %saved_hbm.1, bf16[1,2,4096]{2,1,0:T(2,128)(2,1)} %grad_hbm.1, bf16[1,4096]{1,0:T(2,128)(2,1)} %gain_hbm.1), custom_call_target="tpu_custom_call" | custom-call | tf_op jit(solution)/shard_map/prepare/pallas_call | solution.py:270
  1.9 0.0 collective-permute-done.1.grad_ref
  2.0 0.0 collective-permute-done.saved_ref
  2.0 4.0 %collective-permute-start.3 = (bf16[4,9216]{1,0:T(4,128)(2,1)S(1)}, bf16[4,9216]{1,0:T(4,128)(2,1)S(1)}, u32[]{:S(2)}, u32[]{:S(2)}) collective-permute-start(bf16[4,9216]{1,0:T(4,128)(2,1)S(1)} %join.1), channel_id=1, source_target_pairs={{0,10},{1,13},{2,8},{3,15},{4,14},{5,11},{6,12},{7,9},{8,2},{9,5},... | collective-permute-start | bytes 221192 | tf_op jit(solution)/shard_map/ppermute | solution.py:253
  6.0 0.5 %collective-permute-start.2 = (bf16[4,9216]{1,0:T(4,128)(2,1)S(1)}, bf16[4,9216]{1,0:T(4,128)(2,1)S(1)}, u32[]{:S(2)}, u32[]{:S(2)}) collective-permute-start(bf16[4,9216]{1,0:T(4,128)(2,1)S(1)} %join.1), channel_id=1, source_target_pairs={{0,8},{1,15},{2,10},{3,13},{4,12},{5,9},{6,14},{7,11},{8,0},{9,7},... | collective-permute-start | bytes 221192 | tf_op jit(solution)/shard_map/ppermute | solution.py:253
  6.6 3.9 %fetch.1 = (bf16[4096,768]{1,0:T(8,128)(2,1)S(1)}, bf16[384,4096]{1,0:T(8,128)(2,1)S(1)}, bf16[384,4096]{1,0:T(8,128)(2,1)S(1)}, bf16[384,4096]{1,0:T(8,128)(2,1)S(1)}) custom-call(bf16[4096,384]{1,0:T(8,128)(2,1)} %gate_hbm.1, bf16[4096,384]{1,0:T(8,128)(2,1)} %up_hbm.1, bf16[384,4096]{1,0:T(8,128)(2,1)} %down_hbm.1), custom_call_target="tpu_custom_call" | custom-call | bytes 18874368 | tf_op jit(solution)/shard_map/fetch/pallas_call | solution.py:287
  10.4 0.0 collective-permute-done.3.refs_1_
  10.4 0.0 collective-permute-done.2.refs_0_
  10.5 0.1 collect.1
  10.5 1.3 %collective-permute-start.4 = (bf16[8,8192]{1,0:T(8,128)(2,1)S(1)}, bf16[8,8192]{1,0:T(8,128)(2,1)S(1)}, u32[]{:S(2)}, u32[]{:S(2)}) collective-permute-start(bf16[8,8192]{1,0:T(8,128)(2,1)S(1)} %get-tuple-element.30.near_ref.after), channel_id=1, source_target_pairs={{0,1},{1,0},{2,3},{3,2},{4,5},{5,4},{6,7},{7,6},{8,9},{9,8},{10,11... | collective-permute-start | bytes 393224 | tf_op jit(solution)/shard_map/ppermute | solution.py:267
  11.9 0.9 %turn.1.down_ref = bf16[4096,384]{1,0:T(8,128)(2,1)S(1)} custom-call(bf16[384,4096]{1,0:T(8,128)(2,1)S(1)} %get-tuple-element.37.down_ref, bf16[8,8192]{1,0:T(8,128)(2,1)S(1)} %get-tuple-element.30.near_ref.after), custom_call_target="tpu_custom_call" | custom-call | bytes 6291456 | tf_op jit(solution)/shard_map/turn/pallas_call | solution.py:308
  12.7 0.1 collective-permute-done.4.far_ref
  12.9 0.2 arrange.1
  13.1 2.2 %expert.1 = (f32[8,4096]{1,0:T(8,128)S(1)}, bf16[8,4096]{1,0:T(8,128)(2,1)S(1)}) custom-call(bf16[16,4096]{1,0:T(8,128)(2,1)S(1)} %get-tuple-element.33.normed_ref, bf16[16,4096]{1,0:T(8,128)(2,1)S(1)} %get-tuple-element.34.grad_ref, bf16[4096,768]{1,0:T(8,128)(2,1)S(1)} %get-tuple-element.29.refs_2_.both_ref, ...), custom_call_target="tpu_custom_call" | custom-call | tf_op jit(solution)/shard_map/expert/pallas_call | solution.py:326
  15.3 0.4 %collective-permute-start.6 = (bf16[8,4096]{1,0:T(8,128)(2,1)S(1)}, bf16[8,4096]{1,0:T(8,128)(2,1)S(1)}, u32[]{:S(2)}, u32[]{:S(2)}) collective-permute-start(bf16[8,4096]{1,0:T(8,128)(2,1)S(1)} %get-tuple-element.39), channel_id=1, source_target_pairs={{0,1},{1,0},{2,3},{3,2},{4,5},{5,4},{6,7},{7,6},{8,9},{9,8},{10,11... | collective-permute-start | bytes 196616 | tf_op jit(solution)/shard_map/ppermute | solution.py:267
  15.7 0.9 %collective-permute-done.6.got_ref = bf16[8,4096]{1,0:T(8,128)(2,1)S(1)} collective-permute-done((bf16[8,4096]{1,0:T(8,128)(2,1)S(1)}, bf16[8,4096]{1,0:T(8,128)(2,1)S(1)}, u32[]{:S(2)}, u32[]{:S(2)}) %collective-permute-start.6) | collective-permute-done | bytes 65568 | tf_op jit(solution)/shard_map/ppermute | solution.py:267
  16.6 0.1 add_cores.1
  16.6 1.8 %collective-permute-start.7 = (bf16[4,4096]{1,0:T(4,128)(2,1)S(1)}, bf16[4,4096]{1,0:T(4,128)(2,1)S(1)}, u32[]{:S(2)}, u32[]{:S(2)}) collective-permute-start(bf16[4,4096]{1,0:T(4,128)(2,1)S(1)} %get-tuple-element.41), channel_id=1, source_target_pairs={{0,4},{1,3},{2,6},{3,5},{4,0},{5,7},{6,2},{7,1},{8,28},{9,27},{10,... | collective-permute-start | bytes 98312 | tf_op jit(solution)/shard_map/ppermute | solution.py:261
  18.5 1.5 %collective-permute-start.8 = (bf16[4,4096]{1,0:T(4,128)(2,1)S(1)}, bf16[4,4096]{1,0:T(4,128)(2,1)S(1)}, u32[]{:S(2)}, u32[]{:S(2)}) collective-permute-start(bf16[4,4096]{1,0:T(4,128)(2,1)S(1)} %get-tuple-element.40.local_ref), channel_id=1, source_target_pairs={{0,16},{1,7},{2,18},{3,1},{4,20},{5,3},{6,22},{7,5},{8,24},{9,31},... | collective-permute-start | bytes 98312 | tf_op jit(solution)/shard_map/ppermute | solution.py:261
  20.0 0.3 %collective-permute-start.5 = (bf16[2,10240]{1,0:T(2,128)(2,1)S(1)}, bf16[2,10240]{1,0:T(2,128)(2,1)S(1)}, u32[]{:S(2)}, u32[]{:S(2)}) collective-permute-start(bf16[2,10240]{1,0:T(2,128)(2,1)S(1)} %get-tuple-element.32.stayed_ref), channel_id=1, source_target_pairs={{0,1},{1,0},{2,3},{3,2},{4,5},{5,4},{6,7},{7,6},{8,24},{9,25},{10,... | collective-permute-start | bytes 122888 | tf_op jit(solution)/shard_map/ppermute | solution.py:264
  20.3 1.8 %collective-permute-done.7.refs_0_ = bf16[4,4096]{1,0:T(4,128)(2,1)S(1)} collective-permute-done((bf16[4,4096]{1,0:T(4,128)(2,1)S(1)}, bf16[4,4096]{1,0:T(4,128)(2,1)S(1)}, u32[]{:S(2)}, u32[]{:S(2)}) %collective-permute-start.7) | collective-permute-done | bytes 32800 | tf_op jit(solution)/shard_map/ppermute | solution.py:261
  22.1 0.3 %collective-permute-done.8.refs_1_ = bf16[4,4096]{1,0:T(4,128)(2,1)S(1)} collective-permute-done((bf16[4,4096]{1,0:T(4,128)(2,1)S(1)}, bf16[4,4096]{1,0:T(4,128)(2,1)S(1)}, u32[]{:S(2)}, u32[]{:S(2)}) %collective-permute-start.8) | collective-permute-done | bytes 32800 | tf_op jit(solution)/shard_map/ppermute | solution.py:261
  22.4 0.1 collective-permute-start.9
  22.5 0.0 collective-permute-done.5.moved_ref
  22.5 0.1 settle.1
  22.6 1.0 %collective-permute-done.9.got_ref = f32[2,4096]{1,0:T(2,128)S(1)} collective-permute-done((f32[2,4096]{1,0:T(2,128)S(1)}, f32[2,4096]{1,0:T(2,128)S(1)}, u32[]{:S(2)}, u32[]{:S(2)}) %collective-permute-start.9) | collective-permute-done | bytes 32800 | tf_op jit(solution)/shard_map/ppermute | solution.py:267
  23.7 0.8 %finish.1 = bf16[1,2,4096]{2,1,0:T(2,128)(2,1)} custom-call(f32[2,4096]{1,0:T(2,128)S(1)} %get-tuple-element.43.unit_ref, f32[1,4096]{1,0:T(1,128)S(1)} %get-tuple-element.44.gain_ref, f32[2,4096]{1,0:T(2,128)S(1)} %get-tuple-element.45.kept_ref, f32[2,4096]{1,0:T(2,128)S(1)} %get-tuple-element.46.base_ref, f32[2,128]{1,0:T(2,128)S(1)} %get-tuple-element.47.recip_ref, ...), custom_call_target="tpu_custom_call" | custom-call | tf_op jit(solution)/shard_map/finish/pallas_call | solution.py:360
  (2 shorter events, 0.1 us)
Async XLA Ops:
  0.0 2.0 %collective-permute-start = (bf16[1,4,2,4096]{3,2,1,0:T(2,128)(2,1)}, bf16[1,4,2,4096]{3,2,1,0:T(2,128)(2,1)S(1)}, u32[]{:S(2)}, u32[]{:S(2)}) collective-permute-start(bf16[1,4,2,4096]{3,2,1,0:T(2,128)(2,1)} %saved_hbm.1), channel_id=1, source_target_pairs={{0,1},{1,0},{2,3},{3,2},{4,5},{5,4},{6,7},{7,6},{8,9},{9,8},{10,11... | collective-permute-start | bytes 196616 | tf_op jit(solution)/shard_map/ppermute | solution.py:267
  0.5 1.5 %collective-permute-start.1 = (bf16[1,2,4096]{2,1,0:T(2,128)(2,1)}, bf16[1,2,4096]{2,1,0:T(2,128)(2,1)S(1)}, u32[]{:S(2)}, u32[]{:S(2)}) collective-permute-start(bf16[1,2,4096]{2,1,0:T(2,128)(2,1)} %grad_hbm.1), channel_id=1, source_target_pairs={{0,1},{1,0},{2,3},{3,2},{4,5},{5,4},{6,7},{7,6},{8,9},{9,8},{10,11... | collective-permute-start | bytes 49160 | tf_op jit(solution)/shard_map/ppermute | solution.py:267
  2.0 8.4 %collective-permute-start.3 = (bf16[4,9216]{1,0:T(4,128)(2,1)S(1)}, bf16[4,9216]{1,0:T(4,128)(2,1)S(1)}, u32[]{:S(2)}, u32[]{:S(2)}) collective-permute-start(bf16[4,9216]{1,0:T(4,128)(2,1)S(1)} %join.1), channel_id=1, source_target_pairs={{0,10},{1,13},{2,8},{3,15},{4,14},{5,11},{6,12},{7,9},{8,2},{9,5},... | collective-permute-start | bytes 221192 | tf_op jit(solution)/shard_map/ppermute | solution.py:253
  6.0 4.5 %collective-permute-start.2 = (bf16[4,9216]{1,0:T(4,128)(2,1)S(1)}, bf16[4,9216]{1,0:T(4,128)(2,1)S(1)}, u32[]{:S(2)}, u32[]{:S(2)}) collective-permute-start(bf16[4,9216]{1,0:T(4,128)(2,1)S(1)} %join.1), channel_id=1, source_target_pairs={{0,8},{1,15},{2,10},{3,13},{4,12},{5,9},{6,14},{7,11},{8,0},{9,7},... | collective-permute-start | bytes 221192 | tf_op jit(solution)/shard_map/ppermute | solution.py:253
  10.5 2.3 %collective-permute-start.4 = (bf16[8,8192]{1,0:T(8,128)(2,1)S(1)}, bf16[8,8192]{1,0:T(8,128)(2,1)S(1)}, u32[]{:S(2)}, u32[]{:S(2)}) collective-permute-start(bf16[8,8192]{1,0:T(8,128)(2,1)S(1)} %get-tuple-element.30.near_ref.after), channel_id=1, source_target_pairs={{0,1},{1,0},{2,3},{3,2},{4,5},{5,4},{6,7},{7,6},{8,9},{9,8},{10,11... | collective-permute-start | bytes 393224 | tf_op jit(solution)/shard_map/ppermute | solution.py:267
  15.3 1.3 %collective-permute-start.6 = (bf16[8,4096]{1,0:T(8,128)(2,1)S(1)}, bf16[8,4096]{1,0:T(8,128)(2,1)S(1)}, u32[]{:S(2)}, u32[]{:S(2)}) collective-permute-start(bf16[8,4096]{1,0:T(8,128)(2,1)S(1)} %get-tuple-element.39), channel_id=1, source_target_pairs={{0,1},{1,0},{2,3},{3,2},{4,5},{5,4},{6,7},{7,6},{8,9},{9,8},{10,11... | collective-permute-start | bytes 196616 | tf_op jit(solution)/shard_map/ppermute | solution.py:267
  16.6 5.4 %collective-permute-start.7 = (bf16[4,4096]{1,0:T(4,128)(2,1)S(1)}, bf16[4,4096]{1,0:T(4,128)(2,1)S(1)}, u32[]{:S(2)}, u32[]{:S(2)}) collective-permute-start(bf16[4,4096]{1,0:T(4,128)(2,1)S(1)} %get-tuple-element.41), channel_id=1, source_target_pairs={{0,4},{1,3},{2,6},{3,5},{4,0},{5,7},{6,2},{7,1},{8,28},{9,27},{10,... | collective-permute-start | bytes 98312 | tf_op jit(solution)/shard_map/ppermute | solution.py:261
  18.5 3.9 %collective-permute-start.8 = (bf16[4,4096]{1,0:T(4,128)(2,1)S(1)}, bf16[4,4096]{1,0:T(4,128)(2,1)S(1)}, u32[]{:S(2)}, u32[]{:S(2)}) collective-permute-start(bf16[4,4096]{1,0:T(4,128)(2,1)S(1)} %get-tuple-element.40.local_ref), channel_id=1, source_target_pairs={{0,16},{1,7},{2,18},{3,1},{4,20},{5,3},{6,22},{7,5},{8,24},{9,31},... | collective-permute-start | bytes 98312 | tf_op jit(solution)/shard_map/ppermute | solution.py:261
  20.0 2.5 %collective-permute-start.5 = (bf16[2,10240]{1,0:T(2,128)(2,1)S(1)}, bf16[2,10240]{1,0:T(2,128)(2,1)S(1)}, u32[]{:S(2)}, u32[]{:S(2)}) collective-permute-start(bf16[2,10240]{1,0:T(2,128)(2,1)S(1)} %get-tuple-element.32.stayed_ref), channel_id=1, source_target_pairs={{0,1},{1,0},{2,3},{3,2},{4,5},{5,4},{6,7},{7,6},{8,24},{9,25},{10,... | collective-permute-start | bytes 122888 | tf_op jit(solution)/shard_map/ppermute | solution.py:264
  22.4 1.3 %collective-permute-start.9 = (f32[2,4096]{1,0:T(2,128)S(1)}, f32[2,4096]{1,0:T(2,128)S(1)}, u32[]{:S(2)}, u32[]{:S(2)}) collective-permute-start(f32[2,4096]{1,0:T(2,128)S(1)} %get-tuple-element.48), channel_id=1, source_target_pairs={{0,1},{1,0},{2,3},{3,2},{4,5},{5,4},{6,7},{7,6},{8,9},{9,8},{10,11... | collective-permute-start | bytes 98312 | tf_op jit(solution)/shard_map/ppermute | solution.py:267

commit v11 on v9

--- a/solution.py
+++ b/solution.py
@@ -138,14 +138,15 @@
     d = normed_ref.shape[1]
     half, r = near_ref.shape[0], own_ref.shape[0]
     first = on_first_core()
-    near, far = near_ref[...].astype(jnp.float32), far_ref[...].astype(jnp.float32)
-    rows_ref[:half] = jnp.where(first, near, far)
-    rows_ref[half:] = jnp.where(first, far, near)
-    grad_ref[...] = rows_ref[:, d:].astype(jnp.bfloat16)
-    wide = rows_ref[:, :d]
+    near, far = near_ref[...], far_ref[...]
+    for at, rows in ((0, jnp.where(first, near, far)), (half, jnp.where(first, far, near))):
+        rows_ref[at : at + half] = rows[:, :d].astype(jnp.float32)
+        grad_ref[at : at + half] = rows[:, d:]
+        if at == 0:
+            own_ref[:, : 2 * d] = jnp.where(first, rows[:r], rows[r : 2 * r])
+    wide = rows_ref[...]
     recip = lax.rsqrt(jnp.mean(wide * wide, axis=-1, keepdims=True) + EPS)
     normed_ref[...] = (wide * recip * gain_ref[...]).astype(jnp.bfloat16)
-    own_ref[:, : 2 * d] = jnp.where(first, rows_ref[:r], rows_ref[r : 2 * r]).astype(jnp.bfloat16)
     piece = d // r
     for n in range(r):
         own_ref[n : n + 1, 2 * d :] = gain_ref[:, n * piece : (n + 1) * piece].astype(jnp.bfloat16)
@@ -319,7 +320,7 @@
         out_shape=[VMEM((2 * rows, d), bf16)] * 2 + [VMEM((r, 2 * d + d // r), bf16)],
         in_specs=whole(3),
         out_specs=whole(3),
-        scratch_shapes=[VMEM((2 * rows, 2 * d), f32)],
+        scratch_shapes=[VMEM((2 * rows, d), f32)],
         compiler_params=params(16),
         name="arrange",
     )(*near_core(block, far, gain_wide))

time: 24.9 us -> 24.8 us (level)
  no operation moved by 1% of the time
where the time goes in v11:
time: 24.8 us; the launch traced here: 24.5 us
  starting transfers between devices  10.5 us (42%)
  Pallas kernels  8.95 us (36%)
  waiting for transfers between devices  4.27 us (17%)
  between operations  0.75 us (3%)
    ppermute x2, starting transfers between devices, ahead(): return lax.ppermute(x, ('section', 'seqtp'), route(goal))  4.54 us
    pallas_call x1, Pallas kernels, on_device(): pl.pallas_call(fetch, out_shape=[VMEM((d, 2 * hidden), bf16)] + [VMEM((hi...  3.87 us
    ppermute x2, starting transfers between devices, home(): return lax.ppermute(x, ('section', 'seqtp'), route(goal))  3.35 us
    ppermute x5, starting transfers between devices, to_core(): return lax.ppermute(x, 'seqtp', [(i, i ^ 1) for i in range(members)])  2.32 us
    pallas_call x1, Pallas kernels, on_device(): pl.pallas_call(functools.partial(expert, CORES * r), out_shape=[VMEM((row...  2.22 us
    ppermute x5, waiting for transfers between devices, to_core(): return lax.ppermute(x, 'seqtp', [(i, i ^ 1) for i in range(members)])  2.16 us
    ppermute x2, waiting for transfers between devices, home(): return lax.ppermute(x, ('section', 'seqtp'), route(goal))  2.07 us
    pallas_call x1, Pallas kernels, on_device(): pl.pallas_call(turn, out_shape=VMEM((d, hidden), bf16), in_specs=whole(1)...  0.86 us
  transfers between devices with their start and end apart: 10, of which 5 were waited for; matrix products, arithmetic and copies ran while one was open for 0% of the time, Pallas kernels for 23%

profile of v11, /device:TPU:0, one launch (start us, length us, event | category | flops | bytes accessed | tf_op | source)
XLA Modules:
  0.0 24.5 jit_solution(11876816712353262490)
XLA Ops:
  0.0 0.5 %collective-permute-start = (bf16[1,4,2,4096]{3,2,1,0:T(2,128)(2,1)}, bf16[1,4,2,4096]{3,2,1,0:T(2,128)(2,1)S(1)}, u32[]{:S(2)}, u32[]{:S(2)}) collective-permute-start(bf16[1,4,2,4096]{3,2,1,0:T(2,128)(2,1)} %saved_hbm.1), channel_id=1, source_target_pairs={{0,1},{1,0},{2,3},{3,2},{4,5},{5,4},{6,7},{7,6},{8,9},{9,8},{10,11... | collective-permute-start | bytes 196616 | tf_op jit(solution)/shard_map/ppermute | solution.py:268
  0.5 0.1 collective-permute-start.1
  1.2 0.8 %prepare.1 = (bf16[2,8192]{1,0:T(2,128)(2,1)S(1)}, bf16[1,4096]{1,0:T(2,128)(2,1)S(1)}) custom-call(s32[1]{0:T(128)S(6)} %copy.8.slot_ref, bf16[1,4,2,4096]{3,2,1,0:T(2,128)(2,1)} %saved_hbm.1, bf16[1,2,4096]{2,1,0:T(2,128)(2,1)} %grad_hbm.1, bf16[1,4096]{1,0:T(2,128)(2,1)} %gain_hbm.1), custom_call_target="tpu_custom_call" | custom-call | tf_op jit(solution)/shard_map/prepare/pallas_call | solution.py:271
  1.9 0.0 collective-permute-done.1.grad_ref
  2.0 0.0 collective-permute-done.saved_ref
  2.0 4.0 %collective-permute-start.3 = (bf16[4,9216]{1,0:T(4,128)(2,1)S(1)}, bf16[4,9216]{1,0:T(4,128)(2,1)S(1)}, u32[]{:S(2)}, u32[]{:S(2)}) collective-permute-start(bf16[4,9216]{1,0:T(4,128)(2,1)S(1)} %join.1), channel_id=1, source_target_pairs={{0,10},{1,13},{2,8},{3,15},{4,14},{5,11},{6,12},{7,9},{8,2},{9,5},... | collective-permute-start | bytes 221192 | tf_op jit(solution)/shard_map/ppermute | solution.py:254
  6.0 0.5 %collective-permute-start.2 = (bf16[4,9216]{1,0:T(4,128)(2,1)S(1)}, bf16[4,9216]{1,0:T(4,128)(2,1)S(1)}, u32[]{:S(2)}, u32[]{:S(2)}) collective-permute-start(bf16[4,9216]{1,0:T(4,128)(2,1)S(1)} %join.1), channel_id=1, source_target_pairs={{0,8},{1,15},{2,10},{3,13},{4,12},{5,9},{6,14},{7,11},{8,0},{9,7},... | collective-permute-start | bytes 221192 | tf_op jit(solution)/shard_map/ppermute | solution.py:254
  6.6 3.9 %fetch.1 = (bf16[4096,768]{1,0:T(8,128)(2,1)S(1)}, bf16[384,4096]{1,0:T(8,128)(2,1)S(1)}, bf16[384,4096]{1,0:T(8,128)(2,1)S(1)}, bf16[384,4096]{1,0:T(8,128)(2,1)S(1)}) custom-call(bf16[4096,384]{1,0:T(8,128)(2,1)} %gate_hbm.1, bf16[4096,384]{1,0:T(8,128)(2,1)} %up_hbm.1, bf16[384,4096]{1,0:T(8,128)(2,1)} %down_hbm.1), custom_call_target="tpu_custom_call" | custom-call | bytes 18874368 | tf_op jit(solution)/shard_map/fetch/pallas_call | solution.py:288
  10.4 0.0 collective-permute-done.3.refs_1_
  10.4 0.0 collective-permute-done.2.refs_0_
  10.5 0.1 collect.1
  10.5 1.3 %collective-permute-start.4 = (bf16[8,8192]{1,0:T(8,128)(2,1)S(1)}, bf16[8,8192]{1,0:T(8,128)(2,1)S(1)}, u32[]{:S(2)}, u32[]{:S(2)}) collective-permute-start(bf16[8,8192]{1,0:T(8,128)(2,1)S(1)} %get-tuple-element.30.near_ref.after), channel_id=1, source_target_pairs={{0,1},{1,0},{2,3},{3,2},{4,5},{5,4},{6,7},{7,6},{8,9},{9,8},{10,11... | collective-permute-start | bytes 393224 | tf_op jit(solution)/shard_map/ppermute | solution.py:268
  11.9 0.9 %turn.1.down_ref = bf16[4096,384]{1,0:T(8,128)(2,1)S(1)} custom-call(bf16[384,4096]{1,0:T(8,128)(2,1)S(1)} %get-tuple-element.37.down_ref, bf16[8,8192]{1,0:T(8,128)(2,1)S(1)} %get-tuple-element.30.near_ref.after), custom_call_target="tpu_custom_call" | custom-call | bytes 6291456 | tf_op jit(solution)/shard_map/turn/pallas_call | solution.py:309
  12.7 0.1 collective-permute-done.4.far_ref
  12.9 0.1 arrange.1
  13.0 2.2 %expert.1 = (f32[8,4096]{1,0:T(8,128)S(1)}, f32[8,4096]{1,0:T(8,128)S(1)}) custom-call(bf16[16,4096]{1,0:T(8,128)(2,1)S(1)} %get-tuple-element.33.normed_ref, bf16[16,4096]{1,0:T(8,128)(2,1)S(1)} %get-tuple-element.34.grad_ref, bf16[4096,768]{1,0:T(8,128)(2,1)S(1)} %get-tuple-element.29.refs_2_.both_ref, bf16[384,4096]{1,0:T(8,128)(2,1)S(1)} %get-tuple-element.35.gate_ref, ...), custom_call_target="tpu_custom_call" | custom-call | tf_op jit(solution)/shard_map/expert/pallas_call | solution.py:327
  15.2 0.4 %collective-permute-start.6 = (f32[8,4096]{1,0:T(8,128)S(1)}, f32[8,4096]{1,0:T(8,128)S(1)}, u32[]{:S(2)}, u32[]{:S(2)}) collective-permute-start(f32[8,4096]{1,0:T(8,128)S(1)} %get-tuple-element.39), channel_id=1, source_target_pairs={{0,1},{1,0},{2,3},{3,2},{4,5},{5,4},{6,7},{7,6},{8,9},{9,8},{10,11... | collective-permute-start | bytes 393224 | tf_op jit(solution)/shard_map/ppermute | solution.py:268
  15.6 1.0 %collective-permute-done.6.got_ref = f32[8,4096]{1,0:T(8,128)S(1)} collective-permute-done((f32[8,4096]{1,0:T(8,128)S(1)}, f32[8,4096]{1,0:T(8,128)S(1)}, u32[]{:S(2)}, u32[]{:S(2)}) %collective-permute-start.6) | collective-permute-done | bytes 131104 | tf_op jit(solution)/shard_map/ppermute | solution.py:268
  16.6 0.1 add_cores.1
  16.7 1.8 %collective-permute-start.7 = (bf16[4,4096]{1,0:T(4,128)(2,1)S(1)}, bf16[4,4096]{1,0:T(4,128)(2,1)S(1)}, u32[]{:S(2)}, u32[]{:S(2)}) collective-permute-start(bf16[4,4096]{1,0:T(4,128)(2,1)S(1)} %get-tuple-element.41), channel_id=1, source_target_pairs={{0,4},{1,3},{2,6},{3,5},{4,0},{5,7},{6,2},{7,1},{8,28},{9,27},{10,... | collective-permute-start | bytes 98312 | tf_op jit(solution)/shard_map/ppermute | solution.py:262
  18.5 1.5 %collective-permute-start.8 = (bf16[4,4096]{1,0:T(4,128)(2,1)S(1)}, bf16[4,4096]{1,0:T(4,128)(2,1)S(1)}, u32[]{:S(2)}, u32[]{:S(2)}) collective-permute-start(bf16[4,4096]{1,0:T(4,128)(2,1)S(1)} %get-tuple-element.40.local_ref), channel_id=1, source_target_pairs={{0,16},{1,7},{2,18},{3,1},{4,20},{5,3},{6,22},{7,5},{8,24},{9,31},... | collective-permute-start | bytes 98312 | tf_op jit(solution)/shard_map/ppermute | solution.py:262
  20.0 0.3 %collective-permute-start.5 = (bf16[2,10240]{1,0:T(2,128)(2,1)S(1)}, bf16[2,10240]{1,0:T(2,128)(2,1)S(1)}, u32[]{:S(2)}, u32[]{:S(2)}) collective-permute-start(bf16[2,10240]{1,0:T(2,128)(2,1)S(1)} %get-tuple-element.32.stayed_ref), channel_id=1, source_target_pairs={{0,1},{1,0},{2,3},{3,2},{4,5},{5,4},{6,7},{7,6},{8,24},{9,25},{10,... | collective-permute-start | bytes 122888 | tf_op jit(solution)/shard_map/ppermute | solution.py:265
  20.4 1.8 %collective-permute-done.7.refs_0_ = bf16[4,4096]{1,0:T(4,128)(2,1)S(1)} collective-permute-done((bf16[4,4096]{1,0:T(4,128)(2,1)S(1)}, bf16[4,4096]{1,0:T(4,128)(2,1)S(1)}, u32[]{:S(2)}, u32[]{:S(2)}) %collective-permute-start.7) | collective-permute-done | bytes 32800 | tf_op jit(solution)/shard_map/ppermute | solution.py:262
  22.1 0.3 %collective-permute-done.8.refs_1_ = bf16[4,4096]{1,0:T(4,128)(2,1)S(1)} collective-permute-done((bf16[4,4096]{1,0:T(4,128)(2,1)S(1)}, bf16[4,4096]{1,0:T(4,128)(2,1)S(1)}, u32[]{:S(2)}, u32[]{:S(2)}) %collective-permute-start.8) | collective-permute-done | bytes 32800 | tf_op jit(solution)/shard_map/ppermute | solution.py:262
  22.5 0.1 collective-permute-start.9
  22.5 0.0 collective-permute-done.5.moved_ref
  22.5 0.1 settle.1
  22.7 1.0 %collective-permute-done.9.got_ref = f32[2,4096]{1,0:T(2,128)S(1)} collective-permute-done((f32[2,4096]{1,0:T(2,128)S(1)}, f32[2,4096]{1,0:T(2,128)S(1)}, u32[]{:S(2)}, u32[]{:S(2)}) %collective-permute-start.9) | collective-permute-done | bytes 32800 | tf_op jit(solution)/shard_map/ppermute | solution.py:268
  23.7 0.8 %finish.1 = bf16[1,2,4096]{2,1,0:T(2,128)(2,1)} custom-call(f32[2,4096]{1,0:T(2,128)S(1)} %get-tuple-element.43.unit_ref, f32[1,4096]{1,0:T(1,128)S(1)} %get-tuple-element.44.gain_ref, f32[2,4096]{1,0:T(2,128)S(1)} %get-tuple-element.45.kept_ref, f32[2,4096]{1,0:T(2,128)S(1)} %get-tuple-element.46.base_ref, f32[2,128]{1,0:T(2,128)S(1)} %get-tuple-element.47.recip_ref, ...), custom_call_target="tpu_custom_call" | custom-call | tf_op jit(solution)/shard_map/finish/pallas_call | solution.py:361
  (2 shorter events, 0.1 us)
Async XLA Ops:
  0.0 2.0 %collective-permute-start = (bf16[1,4,2,4096]{3,2,1,0:T(2,128)(2,1)}, bf16[1,4,2,4096]{3,2,1,0:T(2,128)(2,1)S(1)}, u32[]{:S(2)}, u32[]{:S(2)}) collective-permute-start(bf16[1,4,2,4096]{3,2,1,0:T(2,128)(2,1)} %saved_hbm.1), channel_id=1, source_target_pairs={{0,1},{1,0},{2,3},{3,2},{4,5},{5,4},{6,7},{7,6},{8,9},{9,8},{10,11... | collective-permute-start | bytes 196616 | tf_op jit(solution)/shard_map/ppermute | solution.py:268
  0.5 1.5 %collective-permute-start.1 = (bf16[1,2,4096]{2,1,0:T(2,128)(2,1)}, bf16[1,2,4096]{2,1,0:T(2,128)(2,1)S(1)}, u32[]{:S(2)}, u32[]{:S(2)}) collective-permute-start(bf16[1,2,4096]{2,1,0:T(2,128)(2,1)} %grad_hbm.1), channel_id=1, source_target_pairs={{0,1},{1,0},{2,3},{3,2},{4,5},{5,4},{6,7},{7,6},{8,9},{9,8},{10,11... | collective-permute-start | bytes 49160 | tf_op jit(solution)/shard_map/ppermute | solution.py:268
  2.0 8.4 %collective-permute-start.3 = (bf16[4,9216]{1,0:T(4,128)(2,1)S(1)}, bf16[4,9216]{1,0:T(4,128)(2,1)S(1)}, u32[]{:S(2)}, u32[]{:S(2)}) collective-permute-start(bf16[4,9216]{1,0:T(4,128)(2,1)S(1)} %join.1), channel_id=1, source_target_pairs={{0,10},{1,13},{2,8},{3,15},{4,14},{5,11},{6,12},{7,9},{8,2},{9,5},... | collective-permute-start | bytes 221192 | tf_op jit(solution)/shard_map/ppermute | solution.py:254
  6.0 4.5 %collective-permute-start.2 = (bf16[4,9216]{1,0:T(4,128)(2,1)S(1)}, bf16[4,9216]{1,0:T(4,128)(2,1)S(1)}, u32[]{:S(2)}, u32[]{:S(2)}) collective-permute-start(bf16[4,9216]{1,0:T(4,128)(2,1)S(1)} %join.1), channel_id=1, source_target_pairs={{0,8},{1,15},{2,10},{3,13},{4,12},{5,9},{6,14},{7,11},{8,0},{9,7},... | collective-permute-start | bytes 221192 | tf_op jit(solution)/shard_map/ppermute | solution.py:254
  10.5 2.3 %collective-permute-start.4 = (bf16[8,8192]{1,0:T(8,128)(2,1)S(1)}, bf16[8,8192]{1,0:T(8,128)(2,1)S(1)}, u32[]{:S(2)}, u32[]{:S(2)}) collective-permute-start(bf16[8,8192]{1,0:T(8,128)(2,1)S(1)} %get-tuple-element.30.near_ref.after), channel_id=1, source_target_pairs={{0,1},{1,0},{2,3},{3,2},{4,5},{5,4},{6,7},{7,6},{8,9},{9,8},{10,11... | collective-permute-start | bytes 393224 | tf_op jit(solution)/shard_map/ppermute | solution.py:268
  15.2 1.4 %collective-permute-start.6 = (f32[8,4096]{1,0:T(8,128)S(1)}, f32[8,4096]{1,0:T(8,128)S(1)}, u32[]{:S(2)}, u32[]{:S(2)}) collective-permute-start(f32[8,4096]{1,0:T(8,128)S(1)} %get-tuple-element.39), channel_id=1, source_target_pairs={{0,1},{1,0},{2,3},{3,2},{4,5},{5,4},{6,7},{7,6},{8,9},{9,8},{10,11... | collective-permute-start | bytes 393224 | tf_op jit(solution)/shard_map/ppermute | solution.py:268
  16.7 5.4 %collective-permute-start.7 = (bf16[4,4096]{1,0:T(4,128)(2,1)S(1)}, bf16[4,4096]{1,0:T(4,128)(2,1)S(1)}, u32[]{:S(2)}, u32[]{:S(2)}) collective-permute-start(bf16[4,4096]{1,0:T(4,128)(2,1)S(1)} %get-tuple-element.41), channel_id=1, source_target_pairs={{0,4},{1,3},{2,6},{3,5},{4,0},{5,7},{6,2},{7,1},{8,28},{9,27},{10,... | collective-permute-start | bytes 98312 | tf_op jit(solution)/shard_map/ppermute | solution.py:262
  18.5 3.9 %collective-permute-start.8 = (bf16[4,4096]{1,0:T(4,128)(2,1)S(1)}, bf16[4,4096]{1,0:T(4,128)(2,1)S(1)}, u32[]{:S(2)}, u32[]{:S(2)}) collective-permute-start(bf16[4,4096]{1,0:T(4,128)(2,1)S(1)} %get-tuple-element.40.local_ref), channel_id=1, source_target_pairs={{0,16},{1,7},{2,18},{3,1},{4,20},{5,3},{6,22},{7,5},{8,24},{9,31},... | collective-permute-start | bytes 98312 | tf_op jit(solution)/shard_map/ppermute | solution.py:262
  20.0 2.5 %collective-permute-start.5 = (bf16[2,10240]{1,0:T(2,128)(2,1)S(1)}, bf16[2,10240]{1,0:T(2,128)(2,1)S(1)}, u32[]{:S(2)}, u32[]{:S(2)}) collective-permute-start(bf16[2,10240]{1,0:T(2,128)(2,1)S(1)} %get-tuple-element.32.stayed_ref), channel_id=1, source_target_pairs={{0,1},{1,0},{2,3},{3,2},{4,5},{5,4},{6,7},{7,6},{8,24},{9,25},{10,... | collective-permute-start | bytes 122888 | tf_op jit(solution)/shard_map/ppermute | solution.py:265
  22.5 1.3 %collective-permute-start.9 = (f32[2,4096]{1,0:T(2,128)S(1)}, f32[2,4096]{1,0:T(2,128)S(1)}, u32[]{:S(2)}, u32[]{:S(2)}) collective-permute-start(f32[2,4096]{1,0:T(2,128)S(1)} %get-tuple-element.48), channel_id=1, source_target_pairs={{0,1},{1,0},{2,3},{3,2},{4,5},{5,4},{6,7},{7,6},{8,9},{9,8},{10,11... | collective-permute-start | bytes 98312 | tf_op jit(solution)/shard_map/ppermute | solution.py:268

commit v12 on v11

--- a/solution.py
+++ b/solution.py
@@ -290,7 +290,7 @@
         out_shape=[VMEM((d, 2 * hidden), bf16)] + [VMEM((hidden, d), bf16)] * 3,
         in_specs=anywhere(3),
         out_specs=whole(4),
-        scratch_shapes=[pltpu.SemaphoreType.DMA((2, 4)), pltpu.SemaphoreType.DMA],
+        scratch_shapes=[pltpu.SemaphoreType.DMA((2, 2)), pltpu.SemaphoreType.DMA],
         compiler_params=params(4),
         cost_estimate=cost(12 * d * hidden),
         name="fetch",

time: 24.8 us -> 24.8 us (level)
  transfers between devices with their start and end apart: 10 -> 10, of which waited for: 5 -> 6; matrix products, arithmetic and copies ran while one was open for 0% -> 0% of each run, Pallas kernels for 23% -> 23%
where the time goes in v12:
time: 24.8 us; the launch traced here: 24.5 us
  starting transfers between devices  10.5 us (42%)
  Pallas kernels  8.9 us (36%)
  waiting for transfers between devices  4.32 us (17%)
  between operations  0.75 us (3%)
    ppermute x2, starting transfers between devices, ahead(): return lax.ppermute(x, ('section', 'seqtp'), route(goal))  4.54 us
    pallas_call x1, Pallas kernels, on_device(): pl.pallas_call(fetch, out_shape=[VMEM((d, 2 * hidden), bf16)] + [VMEM((hi...  3.82 us
    ppermute x2, starting transfers between devices, home(): return lax.ppermute(x, ('section', 'seqtp'), route(goal))  3.35 us
    ppermute x5, starting transfers between devices, to_core(): return lax.ppermute(x, 'seqtp', [(i, i ^ 1) for i in range(members)])  2.32 us
    pallas_call x1, Pallas kernels, on_device(): pl.pallas_call(functools.partial(expert, CORES * r), out_shape=[VMEM((row...  2.22 us
    ppermute x5, waiting for transfers between devices, to_core(): return lax.ppermute(x, 'seqtp', [(i, i ^ 1) for i in range(members)])  2.16 us
    ppermute x2, waiting for transfers between devices, home(): return lax.ppermute(x, ('section', 'seqtp'), route(goal))  2.07 us
    pallas_call x1, Pallas kernels, on_device(): pl.pallas_call(turn, out_shape=VMEM((d, hidden), bf16), in_specs=whole(1)...  0.86 us
  transfers between devices with their start and end apart: 10, of which 6 were waited for; matrix products, arithmetic and copies ran while one was open for 0% of the time, Pallas kernels for 23%

profile of v12, /device:TPU:0, one launch (start us, length us, event | category | flops | bytes accessed | tf_op | source)
XLA Modules:
  0.0 24.5 jit_solution(2790265011825959731)
XLA Ops:
  0.0 0.5 %collective-permute-start = (bf16[1,4,2,4096]{3,2,1,0:T(2,128)(2,1)}, bf16[1,4,2,4096]{3,2,1,0:T(2,128)(2,1)S(1)}, u32[]{:S(2)}, u32[]{:S(2)}) collective-permute-start(bf16[1,4,2,4096]{3,2,1,0:T(2,128)(2,1)} %saved_hbm.1), channel_id=1, source_target_pairs={{0,1},{1,0},{2,3},{3,2},{4,5},{5,4},{6,7},{7,6},{8,9},{9,8},{10,11... | collective-permute-start | bytes 196616 | tf_op jit(solution)/shard_map/ppermute | solution.py:268
  0.5 0.1 collective-permute-start.1
  1.2 0.8 %prepare.1 = (bf16[2,8192]{1,0:T(2,128)(2,1)S(1)}, bf16[1,4096]{1,0:T(2,128)(2,1)S(1)}) custom-call(s32[1]{0:T(128)S(6)} %copy.8.slot_ref, bf16[1,4,2,4096]{3,2,1,0:T(2,128)(2,1)} %saved_hbm.1, bf16[1,2,4096]{2,1,0:T(2,128)(2,1)} %grad_hbm.1, bf16[1,4096]{1,0:T(2,128)(2,1)} %gain_hbm.1), custom_call_target="tpu_custom_call" | custom-call | tf_op jit(solution)/shard_map/prepare/pallas_call | solution.py:271
  1.9 0.0 collective-permute-done.1.grad_ref
  2.0 0.0 collective-permute-done.saved_ref
  2.0 4.0 %collective-permute-start.3 = (bf16[4,9216]{1,0:T(4,128)(2,1)S(1)}, bf16[4,9216]{1,0:T(4,128)(2,1)S(1)}, u32[]{:S(2)}, u32[]{:S(2)}) collective-permute-start(bf16[4,9216]{1,0:T(4,128)(2,1)S(1)} %join.1), channel_id=1, source_target_pairs={{0,10},{1,13},{2,8},{3,15},{4,14},{5,11},{6,12},{7,9},{8,2},{9,5},... | collective-permute-start | bytes 221192 | tf_op jit(solution)/shard_map/ppermute | solution.py:254
  6.0 0.5 %collective-permute-start.2 = (bf16[4,9216]{1,0:T(4,128)(2,1)S(1)}, bf16[4,9216]{1,0:T(4,128)(2,1)S(1)}, u32[]{:S(2)}, u32[]{:S(2)}) collective-permute-start(bf16[4,9216]{1,0:T(4,128)(2,1)S(1)} %join.1), channel_id=1, source_target_pairs={{0,8},{1,15},{2,10},{3,13},{4,12},{5,9},{6,14},{7,11},{8,0},{9,7},... | collective-permute-start | bytes 221192 | tf_op jit(solution)/shard_map/ppermute | solution.py:254
  6.6 3.8 %fetch.1 = (bf16[4096,768]{1,0:T(8,128)(2,1)S(1)}, bf16[384,4096]{1,0:T(8,128)(2,1)S(1)}, bf16[384,4096]{1,0:T(8,128)(2,1)S(1)}, bf16[384,4096]{1,0:T(8,128)(2,1)S(1)}) custom-call(bf16[4096,384]{1,0:T(8,128)(2,1)} %gate_hbm.1, bf16[4096,384]{1,0:T(8,128)(2,1)} %up_hbm.1, bf16[384,4096]{1,0:T(8,128)(2,1)} %down_hbm.1), custom_call_target="tpu_custom_call" | custom-call | bytes 18874368 | tf_op jit(solution)/shard_map/fetch/pallas_call | solution.py:288
  10.4 0.0 collective-permute-done.3.refs_1_
  10.4 0.1 collective-permute-done.2.refs_0_
  10.5 0.1 collect.1
  10.5 1.3 %collective-permute-start.4 = (bf16[8,8192]{1,0:T(8,128)(2,1)S(1)}, bf16[8,8192]{1,0:T(8,128)(2,1)S(1)}, u32[]{:S(2)}, u32[]{:S(2)}) collective-permute-start(bf16[8,8192]{1,0:T(8,128)(2,1)S(1)} %get-tuple-element.30.near_ref.after), channel_id=1, source_target_pairs={{0,1},{1,0},{2,3},{3,2},{4,5},{5,4},{6,7},{7,6},{8,9},{9,8},{10,11... | collective-permute-start | bytes 393224 | tf_op jit(solution)/shard_map/ppermute | solution.py:268
  11.9 0.9 %turn.1.down_ref = bf16[4096,384]{1,0:T(8,128)(2,1)S(1)} custom-call(bf16[384,4096]{1,0:T(8,128)(2,1)S(1)} %get-tuple-element.37.down_ref, bf16[8,8192]{1,0:T(8,128)(2,1)S(1)} %get-tuple-element.30.near_ref.after), custom_call_target="tpu_custom_call" | custom-call | bytes 6291456 | tf_op jit(solution)/shard_map/turn/pallas_call | solution.py:309
  12.7 0.1 collective-permute-done.4.far_ref
  12.9 0.1 arrange.1
  13.0 2.2 %expert.1 = (f32[8,4096]{1,0:T(8,128)S(1)}, f32[8,4096]{1,0:T(8,128)S(1)}) custom-call(bf16[16,4096]{1,0:T(8,128)(2,1)S(1)} %get-tuple-element.33.normed_ref, bf16[16,4096]{1,0:T(8,128)(2,1)S(1)} %get-tuple-element.34.grad_ref, bf16[4096,768]{1,0:T(8,128)(2,1)S(1)} %get-tuple-element.29.refs_2_.both_ref, bf16[384,4096]{1,0:T(8,128)(2,1)S(1)} %get-tuple-element.35.gate_ref, ...), custom_call_target="tpu_custom_call" | custom-call | tf_op jit(solution)/shard_map/expert/pallas_call | solution.py:327
  15.2 0.4 %collective-permute-start.6 = (f32[8,4096]{1,0:T(8,128)S(1)}, f32[8,4096]{1,0:T(8,128)S(1)}, u32[]{:S(2)}, u32[]{:S(2)}) collective-permute-start(f32[8,4096]{1,0:T(8,128)S(1)} %get-tuple-element.39), channel_id=1, source_target_pairs={{0,1},{1,0},{2,3},{3,2},{4,5},{5,4},{6,7},{7,6},{8,9},{9,8},{10,11... | collective-permute-start | bytes 393224 | tf_op jit(solution)/shard_map/ppermute | solution.py:268
  15.6 1.0 %collective-permute-done.6.got_ref = f32[8,4096]{1,0:T(8,128)S(1)} collective-permute-done((f32[8,4096]{1,0:T(8,128)S(1)}, f32[8,4096]{1,0:T(8,128)S(1)}, u32[]{:S(2)}, u32[]{:S(2)}) %collective-permute-start.6) | collective-permute-done | bytes 131104 | tf_op jit(solution)/shard_map/ppermute | solution.py:268
  16.6 0.1 add_cores.1
  16.7 1.8 %collective-permute-start.7 = (bf16[4,4096]{1,0:T(4,128)(2,1)S(1)}, bf16[4,4096]{1,0:T(4,128)(2,1)S(1)}, u32[]{:S(2)}, u32[]{:S(2)}) collective-permute-start(bf16[4,4096]{1,0:T(4,128)(2,1)S(1)} %get-tuple-element.41), channel_id=1, source_target_pairs={{0,4},{1,3},{2,6},{3,5},{4,0},{5,7},{6,2},{7,1},{8,28},{9,27},{10,... | collective-permute-start | bytes 98312 | tf_op jit(solution)/shard_map/ppermute | solution.py:262
  18.5 1.5 %collective-permute-start.8 = (bf16[4,4096]{1,0:T(4,128)(2,1)S(1)}, bf16[4,4096]{1,0:T(4,128)(2,1)S(1)}, u32[]{:S(2)}, u32[]{:S(2)}) collective-permute-start(bf16[4,4096]{1,0:T(4,128)(2,1)S(1)} %get-tuple-element.40.local_ref), channel_id=1, source_target_pairs={{0,16},{1,7},{2,18},{3,1},{4,20},{5,3},{6,22},{7,5},{8,24},{9,31},... | collective-permute-start | bytes 98312 | tf_op jit(solution)/shard_map/ppermute | solution.py:262
  20.0 0.3 %collective-permute-start.5 = (bf16[2,10240]{1,0:T(2,128)(2,1)S(1)}, bf16[2,10240]{1,0:T(2,128)(2,1)S(1)}, u32[]{:S(2)}, u32[]{:S(2)}) collective-permute-start(bf16[2,10240]{1,0:T(2,128)(2,1)S(1)} %get-tuple-element.32.stayed_ref), channel_id=1, source_target_pairs={{0,1},{1,0},{2,3},{3,2},{4,5},{5,4},{6,7},{7,6},{8,24},{9,25},{10,... | collective-permute-start | bytes 122888 | tf_op jit(solution)/shard_map/ppermute | solution.py:265
  20.4 1.8 %collective-permute-done.7.refs_0_ = bf16[4,4096]{1,0:T(4,128)(2,1)S(1)} collective-permute-done((bf16[4,4096]{1,0:T(4,128)(2,1)S(1)}, bf16[4,4096]{1,0:T(4,128)(2,1)S(1)}, u32[]{:S(2)}, u32[]{:S(2)}) %collective-permute-start.7) | collective-permute-done | bytes 32800 | tf_op jit(solution)/shard_map/ppermute | solution.py:262
  22.1 0.3 %collective-permute-done.8.refs_1_ = bf16[4,4096]{1,0:T(4,128)(2,1)S(1)} collective-permute-done((bf16[4,4096]{1,0:T(4,128)(2,1)S(1)}, bf16[4,4096]{1,0:T(4,128)(2,1)S(1)}, u32[]{:S(2)}, u32[]{:S(2)}) %collective-permute-start.8) | collective-permute-done | bytes 32800 | tf_op jit(solution)/shard_map/ppermute | solution.py:262
  22.5 0.1 collective-permute-start.9
  22.5 0.0 collective-permute-done.5.moved_ref
  22.5 0.1 settle.1
  22.7 1.0 %collective-permute-done.9.got_ref = f32[2,4096]{1,0:T(2,128)S(1)} collective-permute-done((f32[2,4096]{1,0:T(2,128)S(1)}, f32[2,4096]{1,0:T(2,128)S(1)}, u32[]{:S(2)}, u32[]{:S(2)}) %collective-permute-start.9) | collective-permute-done | bytes 32800 | tf_op jit(solution)/shard_map/ppermute | solution.py:268
  23.7 0.8 %finish.1 = bf16[1,2,4096]{2,1,0:T(2,128)(2,1)} custom-call(f32[2,4096]{1,0:T(2,128)S(1)} %get-tuple-element.43.unit_ref, f32[1,4096]{1,0:T(1,128)S(1)} %get-tuple-element.44.gain_ref, f32[2,4096]{1,0:T(2,128)S(1)} %get-tuple-element.45.kept_ref, f32[2,4096]{1,0:T(2,128)S(1)} %get-tuple-element.46.base_ref, f32[2,128]{1,0:T(2,128)S(1)} %get-tuple-element.47.recip_ref, ...), custom_call_target="tpu_custom_call" | custom-call | tf_op jit(solution)/shard_map/finish/pallas_call | solution.py:361
  (2 shorter events, 0.1 us)
Async XLA Ops:
  0.0 2.0 %collective-permute-start = (bf16[1,4,2,4096]{3,2,1,0:T(2,128)(2,1)}, bf16[1,4,2,4096]{3,2,1,0:T(2,128)(2,1)S(1)}, u32[]{:S(2)}, u32[]{:S(2)}) collective-permute-start(bf16[1,4,2,4096]{3,2,1,0:T(2,128)(2,1)} %saved_hbm.1), channel_id=1, source_target_pairs={{0,1},{1,0},{2,3},{3,2},{4,5},{5,4},{6,7},{7,6},{8,9},{9,8},{10,11... | collective-permute-start | bytes 196616 | tf_op jit(solution)/shard_map/ppermute | solution.py:268
  0.5 1.5 %collective-permute-start.1 = (bf16[1,2,4096]{2,1,0:T(2,128)(2,1)}, bf16[1,2,4096]{2,1,0:T(2,128)(2,1)S(1)}, u32[]{:S(2)}, u32[]{:S(2)}) collective-permute-start(bf16[1,2,4096]{2,1,0:T(2,128)(2,1)} %grad_hbm.1), channel_id=1, source_target_pairs={{0,1},{1,0},{2,3},{3,2},{4,5},{5,4},{6,7},{7,6},{8,9},{9,8},{10,11... | collective-permute-start | bytes 49160 | tf_op jit(solution)/shard_map/ppermute | solution.py:268
  2.0 8.4 %collective-permute-start.3 = (bf16[4,9216]{1,0:T(4,128)(2,1)S(1)}, bf16[4,9216]{1,0:T(4,128)(2,1)S(1)}, u32[]{:S(2)}, u32[]{:S(2)}) collective-permute-start(bf16[4,9216]{1,0:T(4,128)(2,1)S(1)} %join.1), channel_id=1, source_target_pairs={{0,10},{1,13},{2,8},{3,15},{4,14},{5,11},{6,12},{7,9},{8,2},{9,5},... | collective-permute-start | bytes 221192 | tf_op jit(solution)/shard_map/ppermute | solution.py:254
  6.0 4.5 %collective-permute-start.2 = (bf16[4,9216]{1,0:T(4,128)(2,1)S(1)}, bf16[4,9216]{1,0:T(4,128)(2,1)S(1)}, u32[]{:S(2)}, u32[]{:S(2)}) collective-permute-start(bf16[4,9216]{1,0:T(4,128)(2,1)S(1)} %join.1), channel_id=1, source_target_pairs={{0,8},{1,15},{2,10},{3,13},{4,12},{5,9},{6,14},{7,11},{8,0},{9,7},... | collective-permute-start | bytes 221192 | tf_op jit(solution)/shard_map/ppermute | solution.py:254
  10.5 2.3 %collective-permute-start.4 = (bf16[8,8192]{1,0:T(8,128)(2,1)S(1)}, bf16[8,8192]{1,0:T(8,128)(2,1)S(1)}, u32[]{:S(2)}, u32[]{:S(2)}) collective-permute-start(bf16[8,8192]{1,0:T(8,128)(2,1)S(1)} %get-tuple-element.30.near_ref.after), channel_id=1, source_target_pairs={{0,1},{1,0},{2,3},{3,2},{4,5},{5,4},{6,7},{7,6},{8,9},{9,8},{10,11... | collective-permute-start | bytes 393224 | tf_op jit(solution)/shard_map/ppermute | solution.py:268
  15.2 1.4 %collective-permute-start.6 = (f32[8,4096]{1,0:T(8,128)S(1)}, f32[8,4096]{1,0:T(8,128)S(1)}, u32[]{:S(2)}, u32[]{:S(2)}) collective-permute-start(f32[8,4096]{1,0:T(8,128)S(1)} %get-tuple-element.39), channel_id=1, source_target_pairs={{0,1},{1,0},{2,3},{3,2},{4,5},{5,4},{6,7},{7,6},{8,9},{9,8},{10,11... | collective-permute-start | bytes 393224 | tf_op jit(solution)/shard_map/ppermute | solution.py:268
  16.7 5.4 %collective-permute-start.7 = (bf16[4,4096]{1,0:T(4,128)(2,1)S(1)}, bf16[4,4096]{1,0:T(4,128)(2,1)S(1)}, u32[]{:S(2)}, u32[]{:S(2)}) collective-permute-start(bf16[4,4096]{1,0:T(4,128)(2,1)S(1)} %get-tuple-element.41), channel_id=1, source_target_pairs={{0,4},{1,3},{2,6},{3,5},{4,0},{5,7},{6,2},{7,1},{8,28},{9,27},{10,... | collective-permute-start | bytes 98312 | tf_op jit(solution)/shard_map/ppermute | solution.py:262
  18.5 3.9 %collective-permute-start.8 = (bf16[4,4096]{1,0:T(4,128)(2,1)S(1)}, bf16[4,4096]{1,0:T(4,128)(2,1)S(1)}, u32[]{:S(2)}, u32[]{:S(2)}) collective-permute-start(bf16[4,4096]{1,0:T(4,128)(2,1)S(1)} %get-tuple-element.40.local_ref), channel_id=1, source_target_pairs={{0,16},{1,7},{2,18},{3,1},{4,20},{5,3},{6,22},{7,5},{8,24},{9,31},... | collective-permute-start | bytes 98312 | tf_op jit(solution)/shard_map/ppermute | solution.py:262
  20.0 2.5 %collective-permute-start.5 = (bf16[2,10240]{1,0:T(2,128)(2,1)S(1)}, bf16[2,10240]{1,0:T(2,128)(2,1)S(1)}, u32[]{:S(2)}, u32[]{:S(2)}) collective-permute-start(bf16[2,10240]{1,0:T(2,128)(2,1)S(1)} %get-tuple-element.32.stayed_ref), channel_id=1, source_target_pairs={{0,1},{1,0},{2,3},{3,2},{4,5},{5,4},{6,7},{7,6},{8,24},{9,25},{10,... | collective-permute-start | bytes 122888 | tf_op jit(solution)/shard_map/ppermute | solution.py:265
  22.5 1.3 %collective-permute-start.9 = (f32[2,4096]{1,0:T(2,128)S(1)}, f32[2,4096]{1,0:T(2,128)S(1)}, u32[]{:S(2)}, u32[]{:S(2)}) collective-permute-start(f32[2,4096]{1,0:T(2,128)S(1)} %get-tuple-element.48), channel_id=1, source_target_pairs={{0,1},{1,0},{2,3},{3,2},{4,5},{5,4},{6,7},{7,6},{8,9},{9,8},{10,11... | collective-permute-start | bytes 98312 | tf_op jit(solution)/shard_map/ppermute | solution.py:268
